TPU v7x, 32 devices: a whole 2x2x4 slice. The times are simulated.
32 devices in a mesh: dp: 2 (over x), seq: 16 (over z, y, core).
Axes of the slice: x: 2, y: 2, z: 4, core: 2. Of those that a mesh axis runs over, the one named last changes fastest.
Arguments:
- queries: bfloat16 [4096, 2048], P(('dp', 'seq')), may hold values from -8 to 8
- keys: bfloat16 [4096, 1024], P(('dp', 'seq')), may hold values from -15 to 15
- values: bfloat16 [4096, 1024], P(('dp', 'seq')), may hold values from -6 to 6
- output_gradient: bfloat16 [4096, 2048], P(('dp', 'seq')), may hold values from -6 to 6
- doc_lengths: int32 [32], replicated, may hold values from 1 to 512, 4096 in all
Outputs:
- attended: bfloat16 [4096, 2048], P(('dp', 'seq'))
- q_grad: float32 [4096, 2048], P(('dp', 'seq'))
- k_grad: float32 [4096, 1024], P(('dp', 'seq'))
- v_grad: float32 [4096, 1024], P(('dp', 'seq'))
Inputs may be any that keep to these rules, and one draw needn't show every extreme that they name: `doc_lengths`: the documents fill all 4096 positions of the sequence in order, and the longest has exactly 512 tokens.
All inputs are finite; a program needn't handle non-finite values.
Results may differ from a plain program's by a relative error of at most 0.04.
Values may be sent and summed in bfloat16 or wider, within the bound.
No kernel may reach another device: no remote copies, remote signals or barrier semaphores. Data moves between devices by JAX's collectives and lax.ppermute only.
A program may use at most 64 MiB of HBM per device.

v0:
```python
import jax
import jax.numpy as jnp
from jax import lax
from jax.sharding import PartitionSpec as P

QUERY_HEADS = 16
KEY_VALUE_HEADS = 8
HEAD_SIZE = 128
LOCAL_WINDOW = 256


score_scale = 168.0 ** (-0.5)


def passed_along(value, axis, steps):
    count = lax.axis_size(axis)
    leading, last = (max(0, -steps), min(count, count - steps))
    return lax.ppermute(value, axis, [(source, source + steps) for source in range(leading, last)])


def doc_index(positions, doc_ends):
    doc_count = jnp.sum((doc_ends[None, :] <= positions[:, None]).astype(jnp.int32), axis=1)
    return jnp.where(positions < 0, -1, doc_count)


def live_pairs(query_pos, key_pos, doc_ends):
    spacing = query_pos[:, None] - key_pos[None, :]
    same_doc = doc_index(query_pos, doc_ends)[:, None] == doc_index(key_pos, doc_ends)[None, :]
    return same_doc & (spacing >= 0) & (spacing < LOCAL_WINDOW)


def pair_scores(heads_of_queries, heads_of_keys, live_mask):
    raw_scores = jnp.einsum(
        "qgrd,kgd->grqk", heads_of_queries, heads_of_keys, preferred_element_type=jnp.float32
    )
    return jnp.where(live_mask[None, None], raw_scores * score_scale, -jnp.inf)


def weighted_values(scores, log_total, heads_of_values):
    weights = jnp.exp(scores - log_total[..., None]).astype(jnp.bfloat16)
    return jnp.einsum(
        "grqk,kgd->qgrd", weights, heads_of_values, preferred_element_type=jnp.float32
    )


def pair_grads(
    scores, log_total, grad_dot, heads_of_queries, head_gradients, heads_of_keys, heads_of_values
):
    probs_full = jnp.exp(scores - log_total[..., None])
    weights = probs_full.astype(jnp.bfloat16)
    prob_grad = jnp.einsum(
        "qgrd,kgd->grqk", head_gradients, heads_of_values, preferred_element_type=jnp.float32
    )
    score_grad = (probs_full * (prob_grad - grad_dot[..., None]) * score_scale).astype(jnp.bfloat16)
    query_part = jnp.einsum(
        "grqk,kgd->qgrd", score_grad, heads_of_keys, preferred_element_type=jnp.float32
    )
    key_portion = jnp.einsum(
        "grqk,qgrd->kgd", score_grad, heads_of_queries, preferred_element_type=jnp.float32
    )
    value_portion = jnp.einsum(
        "grqk,qgrd->kgd", weights, head_gradients, preferred_element_type=jnp.float32
    )
    return (query_part, key_portion, value_portion)


def on_device(queries, keys, values, output_gradient, doc_lengths):
    count_of_rows = queries.shape[0]
    query_groups = QUERY_HEADS // KEY_VALUE_HEADS
    halo_depth = max(1, LOCAL_WINDOW // count_of_rows)
    device_rank = lax.axis_index(("dp", "seq"))
    doc_ends = jnp.cumsum(doc_lengths)
    offsets = jnp.arange(count_of_rows, dtype=jnp.int32)
    query_pos = device_rank * count_of_rows + offsets
    heads_of_queries = queries.reshape(count_of_rows, KEY_VALUE_HEADS, query_groups, HEAD_SIZE)
    head_gradients = output_gradient.reshape(
        count_of_rows, KEY_VALUE_HEADS, query_groups, HEAD_SIZE
    )
    piece_list = [(keys, values)]
    for distance in range(1, halo_depth + 1):
        piece_list.append(passed_along((keys, values), ("dp", "seq"), distance))
    key_blocks = []
    for source_rows in range(halo_depth + 1):
        heads_of_keys = piece_list[source_rows][0].reshape(
            count_of_rows, KEY_VALUE_HEADS, HEAD_SIZE
        )
        heads_of_values = piece_list[source_rows][1].reshape(
            count_of_rows, KEY_VALUE_HEADS, HEAD_SIZE
        )
        live_mask = live_pairs(
            query_pos, (device_rank - source_rows) * count_of_rows + offsets, doc_ends
        )
        scores = pair_scores(heads_of_queries, heads_of_keys, live_mask)
        key_blocks.append((heads_of_keys, heads_of_values, live_mask, scores))
    row_max = jnp.max(key_blocks[0][3], axis=-1)
    for entry in key_blocks[1:]:
        row_max = jnp.maximum(row_max, jnp.max(entry[3], axis=-1))
    row_total = jnp.zeros_like(row_max)
    for entry in key_blocks:
        row_total = row_total + jnp.sum(jnp.exp(entry[3] - row_max[..., None]), axis=-1)
    log_total = row_max + jnp.log(row_total)
    context_rows = jnp.zeros((count_of_rows, KEY_VALUE_HEADS, query_groups, HEAD_SIZE), jnp.float32)
    for heads_of_keys, heads_of_values, live_mask, scores in key_blocks:
        context_rows = context_rows + weighted_values(scores, log_total, heads_of_values)
    attended = context_rows.reshape(count_of_rows, QUERY_HEADS * HEAD_SIZE).astype(jnp.bfloat16)
    output_widened = attended.astype(jnp.float32).reshape(
        count_of_rows, KEY_VALUE_HEADS, query_groups, HEAD_SIZE
    )
    grad_dot = jnp.transpose(
        jnp.sum(head_gradients.astype(jnp.float32) * output_widened, axis=-1), (1, 2, 0)
    )
    query_gradient = jnp.zeros(
        (count_of_rows, KEY_VALUE_HEADS, query_groups, HEAD_SIZE), jnp.float32
    )
    key_gradient = jnp.zeros((count_of_rows, KEY_VALUE_HEADS, HEAD_SIZE), jnp.float32)
    value_gradient = jnp.zeros((count_of_rows, KEY_VALUE_HEADS, HEAD_SIZE), jnp.float32)
    for source_rows in range(halo_depth + 1):
        heads_of_keys, heads_of_values, live_mask, scores = key_blocks[source_rows]
        if source_rows == 0:
            parts = pair_grads(
                scores,
                log_total,
                grad_dot,
                heads_of_queries,
                head_gradients,
                heads_of_keys,
                heads_of_values,
            )
            key_gradient = parts[1]
            value_gradient = parts[2]
        else:
            parts = pair_grads(
                scores,
                log_total,
                grad_dot,
                heads_of_queries,
                head_gradients,
                heads_of_keys,
                heads_of_values,
            )
            returned = (
                passed_along(parts[1].astype(jnp.bfloat16), ("dp", "seq"), -source_rows).astype(
                    jnp.float32
                ),
                passed_along(parts[2].astype(jnp.bfloat16), ("dp", "seq"), -source_rows).astype(
                    jnp.float32
                ),
            )
            key_gradient = key_gradient + returned[0]
            value_gradient = value_gradient + returned[1]
        query_gradient = query_gradient + parts[0]
    return (
        attended,
        query_gradient.reshape(count_of_rows, QUERY_HEADS * HEAD_SIZE),
        key_gradient.reshape(count_of_rows, KEY_VALUE_HEADS * HEAD_SIZE),
        value_gradient.reshape(count_of_rows, KEY_VALUE_HEADS * HEAD_SIZE),
    )


def solution(mesh):
    placed = (
        P(("dp", "seq"), None),
        P(("dp", "seq"), None),
        P(("dp", "seq"), None),
        P(("dp", "seq"), None),
        P(),
    )
    return jax.shard_map(
        on_device,
        mesh=mesh,
        in_specs=placed,
        out_specs=(
            P(("dp", "seq"), None),
            P(("dp", "seq"), None),
            P(("dp", "seq"), None),
            P(("dp", "seq"), None),
        ),
        check_vma=False,
    )
```

profile of v0, /device:TPU:2, one launch (start us, length us, event | category | flops | bytes accessed | tf_op | source)
XLA Modules:
  0.0 68.0 jit_solution(15843586245133203571)
XLA Ops:
  0.6 1.8 %copy.92 = bf16[128,1024]{0,1:T(8,128)(2,1)} copy(bf16[128,1024]{1,0:T(8,128)(2,1)} %param.6) | data formatting | bytes 524288 | tf_op args[1]
  2.4 3.4 %collective-permute-start.1 = (bf16[128,1024]{0,1:T(8,128)(2,1)}, bf16[128,1024]{0,1:T(8,128)(2,1)S(1)}, u32[]{:S(2)}, u32[]{:S(2)}) collective-permute-start(bf16[128,1024]{0,1:T(8,128)(2,1)} %copy.92), channel_id=1, source_target_pairs={{0,2},{1,3},{2,4},{3,5},{4,6},{5,7},{6,8},{7,9},{8,10},{9,11},{10,... | collective-permute-start | bytes 786440 | tf_op jit(solution)/shard_map/ppermute | solution.py:18
  5.8 1.9 %collective-permute-start = (bf16[128,1024]{0,1:T(8,128)(2,1)}, bf16[128,1024]{0,1:T(8,128)(2,1)S(1)}, u32[]{:S(2)}, u32[]{:S(2)}) collective-permute-start(bf16[128,1024]{0,1:T(8,128)(2,1)} %copy.92), channel_id=1, source_target_pairs={{0,1},{1,2},{2,3},{3,4},{4,5},{5,6},{6,7},{7,8},{8,9},{9,10},{10,1... | collective-permute-start | bytes 786440 | tf_op jit(solution)/shard_map/ppermute | solution.py:18
  7.8 3.4 %collective-permute-start.3 = (bf16[128,1024]{1,0:T(8,128)(2,1)}, bf16[128,1024]{1,0:T(8,128)(2,1)}, u32[]{:S(2)}, u32[]{:S(2)}) collective-permute-start(bf16[128,1024]{1,0:T(8,128)(2,1)} %param.7), channel_id=1, source_target_pairs={{0,2},{1,3},{2,4},{3,5},{4,6},{5,7},{6,8},{7,9},{8,10},{9,11},{10,... | collective-permute-start | bytes 786440 | tf_op jit(solution)/shard_map/ppermute | solution.py:18
  11.2 3.3 %collective-permute-start.2 = (bf16[128,1024]{1,0:T(8,128)(2,1)}, bf16[128,1024]{1,0:T(8,128)(2,1)}, u32[]{:S(2)}, u32[]{:S(2)}) collective-permute-start(bf16[128,1024]{1,0:T(8,128)(2,1)} %param.7), channel_id=1, source_target_pairs={{0,1},{1,2},{2,3},{3,4},{4,5},{5,6},{6,7},{7,8},{8,9},{9,10},{10,1... | collective-permute-start | bytes 786440 | tf_op jit(solution)/shard_map/ppermute | solution.py:18
  15.6 1.7 %copy.181 = bf16[16,8,8,128]{3,2,1,0:T(8,128)(2,1)} copy(bf16[16,8,8,128]{3,1,2,0:T(8,128)(2,1)} %bitcast.69) | data formatting | bytes 524288
  22.0 1.3 %fusion.55 = (f32[8,2,128]{2,1,0:T(2,128)S(1)}, f32[8,2,128,128]{2,3,1,0:T(8,128)S(1)}) fusion(bf16[128,8,128,1]{0,2,3,1:T(8,128)(2,1)} %bitcast.192, bf16[128,8,2,128]{3,2,1,0:T(2,128)(2,1)S(1)} %reshape.318, pred[128,128]{0,1:T(8,128)(4,1)S(1)} %get-tuple-element.24), kind=kOutput, calls=%fused_computation.87 | convolution fusion | flops 67893248 | bytes 1859584 | tf_op jit(solution)/shard_map/qgrd,kgd->grqk/dot_general | solution.py:33
  24.3 1.3 %fusion.30 = f32[8,2,128,128]{2,3,1,0:T(8,128)} fusion(bf16[128,8,128,1]{2,1,0,3:T(8,128)(2,1)S(1)} %bitcast.181, f32[8,2,128,128]{2,3,1,0:T(8,128)S(1)} %get-tuple-element.28, f32[8,2,128]{2,1,0:T(2,128)S(1)} %bitcast.196), kind=kOutput, calls=%fused_computation.55 | convolution fusion | flops 67633152 | bytes 2367488 | tf_op jit(solution)/shard_map/grqk,kgd->qgrd/dot_general | solution.py:41
  27.5 1.8 %copy.100 = bf16[128,1024]{0,1:T(8,128)(2,1)} copy(bf16[128,1024]{1,0:T(8,128)(2,1)} %collective-permute-done.2) | data formatting | bytes 524288 | tf_op jit(solution)/shard_map/ppermute | solution.py:18
  29.3 2.6 %convolution_add_fusion.3 = f32[8,2,128,128]{2,3,1,0:T(8,128)} fusion(f32[8,2,128,128]{2,3,1,0:T(8,128)} %fusion.30, bf16[128,8,128,1]{0,2,3,1:T(8,128)(2,1)} %bitcast.183, f32[8,2,128,128]{2,3,1,0:T(8,128)S(1)} %get-tuple-element.30, f32[8,2,128]{2,1,0:T(2,128)S(1)} %bitcast.198), kind=kOutput, calls=%fused_computation.3 | convolution fusion | flops 67895296 | bytes 3416064 | tf_op jit(solution)/shard_map/grqk,kgd->qgrd/dot_general | solution.py:41
  32.9 1.8 %copy.102 = bf16[128,1024]{0,1:T(8,128)(2,1)} copy(bf16[128,1024]{1,0:T(8,128)(2,1)} %collective-permute-done.3) | data formatting | bytes 524288 | tf_op jit(solution)/shard_map/ppermute | solution.py:18
  34.7 2.5 %multiply_reduce_fusion = (f32[128,8,2]{0,2,1:T(2,128)S(1)}, bf16[8,2,128,128]{2,3,1,0:T(8,128)(2,1)}) fusion(bf16[128,2048]{0,1:T(8,128)(2,1)S(1)} %copy.104, f32[8,2,128,128]{2,3,1,0:T(8,128)} %convolution_add_fusion.3, bf16[128,8,128,1]{0,2,3,1:T(8,128)(2,1)} %bitcast.185, f32[8,2,128,128]{2,3,1,0:T(8,128)S(1)} %get-tuple-element.26, ...), kind=kOutput, calls=%fused_computation.43 | convolution fusion | flops 69203968 | bytes 3424256 | tf_op jit(solution)/shard_map/grqk,kgd->qgrd/dot_general | solution.py:41
  37.2 1.2 %fusion.16 = bf16[8,2,128,128]{2,3,1,0:T(8,128)(2,1)} fusion(bf16[128,8,128,1]{0,2,3,1:T(8,128)(2,1)S(1)} %bitcast.184, bf16[128,8,2,128]{0,3,2,1:T(8,128)(2,1)S(1)} %bitcast.176, f32[8,2,128,128]{2,3,1,0:T(8,128)S(1)} %get-tuple-element.30, f32[8,2,128]{2,1,0:T(2,128)S(1)} %bitcast.205, f32[8,2,128]{2,1,0:T(2,128)S(1)} %bitcast.201), kind=kOutput, calls=%fused_computation.26 | convolution fusion | flops 68419584 | bytes 2375680 | tf_op jit(solution)/shard_map/qgrd,kgd->grqk/dot_general | solution.py:51
  38.5 1.2 %fusion.17 = bf16[8,2,128,128]{2,3,1,0:T(8,128)(2,1)} fusion(bf16[128,8,128,1]{0,2,3,1:T(8,128)(2,1)S(1)} %bitcast.186, bf16[128,8,2,128]{0,3,2,1:T(8,128)(2,1)S(1)} %bitcast.177, f32[8,2,128,128]{2,3,1,0:T(8,128)S(1)} %get-tuple-element.26, f32[8,2,128]{2,1,0:T(2,128)S(1)} %bitcast.206, f32[8,2,128]{2,1,0:T(2,128)S(1)} %bitcast.202), kind=kOutput, calls=%fused_computation.27 | convolution fusion | flops 68419584 | bytes 2375680 | tf_op jit(solution)/shard_map/qgrd,kgd->grqk/dot_general | solution.py:51
  40.1 4.9 %collective-permute-start.7 = (bf16[128,8,128]{0,2,1:T(8,128)(2,1)}, bf16[128,8,128]{0,2,1:T(8,128)(2,1)}, u32[]{:S(2)}, u32[]{:S(2)}) collective-permute-start(bf16[128,8,128]{0,2,1:T(8,128)(2,1)} %fusion.23), channel_id=1, source_target_pairs={{2,0},{3,1},{4,2},{5,3},{6,4},{7,5},{8,6},{9,7},{10,8},{11,9},{12,... | collective-permute-start | bytes 786440 | tf_op jit(solution)/shard_map/ppermute | solution.py:18
  45.0 2.0 %collective-permute-start.6 = (bf16[128,8,128]{0,2,1:T(8,128)(2,1)}, bf16[128,8,128]{0,2,1:T(8,128)(2,1)}, u32[]{:S(2)}, u32[]{:S(2)}) collective-permute-start(bf16[128,8,128]{0,2,1:T(8,128)(2,1)} %fusion.24), channel_id=1, source_target_pairs={{1,0},{2,1},{3,2},{4,3},{5,4},{6,5},{7,6},{8,7},{9,8},{10,9},{11,1... | collective-permute-start | bytes 786440 | tf_op jit(solution)/shard_map/ppermute | solution.py:18
  47.1 2.1 %copy.126 = bf16[128,2048]{1,0:T(8,128)(2,1)} copy(bf16[128,2048]{0,1:T(8,128)(2,1)} %bitcast.188) | data formatting | bytes 1048576
  49.2 1.1 %fusion.25 = bf16[128,8,128]{0,2,1:T(8,128)(2,1)} fusion(bf16[8,2,128,128]{2,3,1,0:T(8,128)(2,1)S(1)} %copy-done.2, bf16[128,8,2,128]{3,2,1,0:T(2,128)(2,1)S(1)} %reshape.318), kind=kOutput, calls=%fused_computation.41 | convolution fusion | flops 67239936 | bytes 1310720 | tf_op jit(solution)/shard_map/grqk,qgrd->kgd/dot_general | solution.py:58
  51.3 2.5 %collective-permute-start.4 = (bf16[128,8,128]{0,2,1:T(8,128)(2,1)}, bf16[128,8,128]{0,2,1:T(8,128)(2,1)}, u32[]{:S(2)}, u32[]{:S(2)}) collective-permute-start(bf16[128,8,128]{0,2,1:T(8,128)(2,1)} %fusion.26), channel_id=1, source_target_pairs={{1,0},{2,1},{3,2},{4,3},{5,4},{6,5},{7,6},{8,7},{9,8},{10,9},{11,1... | collective-permute-start | bytes 786440 | tf_op jit(solution)/shard_map/ppermute | solution.py:18
  53.9 3.3 %collective-permute-start.5 = (bf16[128,8,128]{0,2,1:T(8,128)(2,1)}, bf16[128,8,128]{0,2,1:T(8,128)(2,1)}, u32[]{:S(2)}, u32[]{:S(2)}) collective-permute-start(bf16[128,8,128]{0,2,1:T(8,128)(2,1)} %fusion.25), channel_id=1, source_target_pairs={{2,0},{3,1},{4,2},{5,3},{6,4},{7,5},{8,6},{9,7},{10,8},{11,9},{12,... | collective-permute-start | bytes 786440 | tf_op jit(solution)/shard_map/ppermute | solution.py:18
  58.4 1.3 %convolution_add_fusion = f32[8,2,128,128]{2,3,1,0:T(8,128)} fusion(f32[8,2,128,128]{2,3,1,0:T(8,128)S(1)} %convolution_add_fusion.1, bf16[128,8,128,1]{0,2,3,1:T(8,128)(2,1)S(1)} %bitcast.193, bf16[8,2,128,128]{2,3,1,0:T(8,128)(2,1)S(1)} %copy-done.2), kind=kOutput, calls=%fused_computation | convolution fusion | flops 67371008 | bytes 2883584 | tf_op jit(solution)/shard_map/grqk,kgd->qgrd/dot_general | solution.py:55
  59.7 2.5 %copy.127 = f32[128,2048]{1,0:T(8,128)} copy(f32[128,2048]{0,1:T(8,128)} %bitcast.180) | data formatting | bytes 2097152
  62.2 1.3 %convert_add_fusion = f32[128,8,128]{0,2,1:T(8,128)S(1)} fusion(bf16[128,8,128]{0,2,1:T(8,128)(2,1)} %collective-permute-done.7, bf16[128,8,128]{0,2,1:T(8,128)(2,1)} %collective-permute-done.6, bf16[128,8,2,128]{0,3,2,1:T(8,128)(2,1)S(1)} %bitcast.179, f32[8,2,128,128]{2,3,1,0:T(8,128)S(1)} %copy-done.1, f32[8,2,128]{2,1,0:T(2,128)S(1)} %bitcast.204), kind=kOutput, calls=%fused_computation.53 | convolution fusion | flops 68157440 | bytes 2629632 | tf_op jit(solution)/shard_map/grqk,qgrd->kgd/dot_general | solution.py:61
  65.6 1.4 %convert_add_fusion.1 = f32[128,8,128]{0,2,1:T(8,128)S(1)} fusion(bf16[128,8,128]{0,2,1:T(8,128)(2,1)} %collective-permute-done.5, bf16[128,8,128]{0,2,1:T(8,128)(2,1)} %collective-permute-done.4, bf16[8,2,128,128]{2,3,1,0:T(8,128)(2,1)S(1)} %fusion.15, bf16[128,8,2,128]{3,2,1,0:T(2,128)(2,1)S(1)} %reshape.318), kind=kOutput, calls=%fused_computation.54 | convolution fusion | flops 67633152 | bytes 2097152 | tf_op jit(solution)/shard_map/grqk,qgrd->kgd/dot_general | solution.py:58
  (67 shorter events, 15.3 us)
Async XLA Ops:
  2.4 18.9 %collective-permute-start.1 = (bf16[128,1024]{0,1:T(8,128)(2,1)}, bf16[128,1024]{0,1:T(8,128)(2,1)S(1)}, u32[]{:S(2)}, u32[]{:S(2)}) collective-permute-start(bf16[128,1024]{0,1:T(8,128)(2,1)} %copy.92), channel_id=1, source_target_pairs={{0,2},{1,3},{2,4},{3,5},{4,6},{5,7},{6,8},{7,9},{8,10},{9,11},{10,... | collective-permute-start | bytes 786440 | tf_op jit(solution)/shard_map/ppermute | solution.py:18
  5.8 14.8 %collective-permute-start = (bf16[128,1024]{0,1:T(8,128)(2,1)}, bf16[128,1024]{0,1:T(8,128)(2,1)S(1)}, u32[]{:S(2)}, u32[]{:S(2)}) collective-permute-start(bf16[128,1024]{0,1:T(8,128)(2,1)} %copy.92), channel_id=1, source_target_pairs={{0,1},{1,2},{2,3},{3,4},{4,5},{5,6},{6,7},{7,8},{8,9},{9,10},{10,1... | collective-permute-start | bytes 786440 | tf_op jit(solution)/shard_map/ppermute | solution.py:18
  7.8 25.2 %collective-permute-start.3 = (bf16[128,1024]{1,0:T(8,128)(2,1)}, bf16[128,1024]{1,0:T(8,128)(2,1)}, u32[]{:S(2)}, u32[]{:S(2)}) collective-permute-start(bf16[128,1024]{1,0:T(8,128)(2,1)} %param.7), channel_id=1, source_target_pairs={{0,2},{1,3},{2,4},{3,5},{4,6},{5,7},{6,8},{7,9},{8,10},{9,11},{10,... | collective-permute-start | bytes 786440 | tf_op jit(solution)/shard_map/ppermute | solution.py:18
  11.2 16.3 %collective-permute-start.2 = (bf16[128,1024]{1,0:T(8,128)(2,1)}, bf16[128,1024]{1,0:T(8,128)(2,1)}, u32[]{:S(2)}, u32[]{:S(2)}) collective-permute-start(bf16[128,1024]{1,0:T(8,128)(2,1)} %param.7), channel_id=1, source_target_pairs={{0,1},{1,2},{2,3},{3,4},{4,5},{5,6},{6,7},{7,8},{8,9},{9,10},{10,1... | collective-permute-start | bytes 786440 | tf_op jit(solution)/shard_map/ppermute | solution.py:18
  14.5 0.7 copy-start.15
  15.5 1.8 %copy-start.8 = (bf16[128,1024]{1,0:T(8,128)(2,1)S(1)}, bf16[128,1024]{1,0:T(8,128)(2,1)}, u32[]{:S(2)}) copy-start(bf16[128,1024]{1,0:T(8,128)(2,1)} %param.6) | copy-start | bytes 786436
  17.3 1.0 %copy-start.13 = (bf16[128,2048]{1,0:T(8,128)(2,1)S(1)}, bf16[128,2048]{1,0:T(8,128)(2,1)}, u32[]{:S(2)}) copy-start(bf16[128,2048]{1,0:T(8,128)(2,1)} %param.5) | copy-start | bytes 1572868
  18.4 1.0 %copy-start.14 = (bf16[128,2048]{1,0:T(8,128)(2,1)S(1)}, bf16[128,2048]{1,0:T(8,128)(2,1)}, u32[]{:S(2)}) copy-start(bf16[128,2048]{1,0:T(8,128)(2,1)} %param.8) | copy-start | bytes 1572868
  20.2 3.8 %copy-start = (f32[8,2,128,128]{2,3,1,0:T(8,128)}, f32[8,2,128,128]{2,3,1,0:T(8,128)S(1)}, u32[]{:S(2)}) copy-start(f32[8,2,128,128]{2,3,1,0:T(8,128)S(1)} %get-tuple-element.28) | copy-start | bytes 3145732
  20.6 0.7 %copy-start.11 = (bf16[128,1024]{0,1:T(8,128)(2,1)}, bf16[128,1024]{0,1:T(8,128)(2,1)S(1)}, u32[]{:S(2)}) copy-start(bf16[128,1024]{0,1:T(8,128)(2,1)S(1)} %collective-permute-done) | copy-start | bytes 786436
  21.3 0.7 %copy-start.9 = (bf16[128,1024]{0,1:T(8,128)(2,1)}, bf16[128,1024]{0,1:T(8,128)(2,1)S(1)}, u32[]{:S(2)}) copy-start(bf16[128,1024]{0,1:T(8,128)(2,1)S(1)} %collective-permute-done.1) | copy-start | bytes 786436
  23.4 1.0 %copy-start.4 = (bf16[16,8,8,128]{3,2,1,0:T(8,128)(2,1)S(1)}, bf16[16,8,8,128]{3,2,1,0:T(8,128)(2,1)}, u32[]{:S(2)}) copy-start(bf16[16,8,8,128]{3,2,1,0:T(8,128)(2,1)} %copy.181) | copy-start | bytes 786436
  34.7 2.5 %copy-start.6 = (bf16[128,1024]{0,1:T(8,128)(2,1)S(1)}, bf16[128,1024]{0,1:T(8,128)(2,1)}, u32[]{:S(2)}) copy-start(bf16[128,1024]{0,1:T(8,128)(2,1)} %copy.100) | copy-start | bytes 786436
  37.2 1.2 %copy-start.7 = (bf16[128,1024]{0,1:T(8,128)(2,1)S(1)}, bf16[128,1024]{0,1:T(8,128)(2,1)}, u32[]{:S(2)}) copy-start(bf16[128,1024]{0,1:T(8,128)(2,1)} %copy.102) | copy-start | bytes 786436
  38.5 1.2 %copy-start.1 = (f32[8,2,128,128]{2,3,1,0:T(8,128)S(1)}, f32[8,2,128,128]{2,3,1,0:T(8,128)}, u32[]{:S(2)}) copy-start(f32[8,2,128,128]{2,3,1,0:T(8,128)} %copy-done) | copy-start | bytes 3145732
  38.5 1.3 %copy-start.5 = (bf16[16,8,8,128]{3,2,1,0:T(8,128)(2,1)S(1)}, bf16[16,8,8,128]{3,2,1,0:T(8,128)(2,1)}, u32[]{:S(2)}) copy-start(bf16[16,8,8,128]{3,2,1,0:T(8,128)(2,1)} %copy.181) | copy-start | bytes 786436
  40.1 22.1 %collective-permute-start.7 = (bf16[128,8,128]{0,2,1:T(8,128)(2,1)}, bf16[128,8,128]{0,2,1:T(8,128)(2,1)}, u32[]{:S(2)}, u32[]{:S(2)}) collective-permute-start(bf16[128,8,128]{0,2,1:T(8,128)(2,1)} %fusion.23), channel_id=1, source_target_pairs={{2,0},{3,1},{4,2},{5,3},{6,4},{7,5},{8,6},{9,7},{10,8},{11,9},{12,... | collective-permute-start | bytes 786440 | tf_op jit(solution)/shard_map/ppermute | solution.py:18
  45.0 17.2 %collective-permute-start.6 = (bf16[128,8,128]{0,2,1:T(8,128)(2,1)}, bf16[128,8,128]{0,2,1:T(8,128)(2,1)}, u32[]{:S(2)}, u32[]{:S(2)}) collective-permute-start(bf16[128,8,128]{0,2,1:T(8,128)(2,1)} %fusion.24), channel_id=1, source_target_pairs={{1,0},{2,1},{3,2},{4,3},{5,4},{6,5},{7,6},{8,7},{9,8},{10,9},{11,1... | collective-permute-start | bytes 786440 | tf_op jit(solution)/shard_map/ppermute | solution.py:18
  47.1 2.1 %copy-start.2 = (bf16[8,2,128,128]{2,3,1,0:T(8,128)(2,1)S(1)}, bf16[8,2,128,128]{2,3,1,0:T(8,128)(2,1)}, u32[]{:S(2)}) copy-start(bf16[8,2,128,128]{2,3,1,0:T(8,128)(2,1)} %fusion.17) | copy-start | bytes 1572868
  49.2 1.1 %copy-start.3 = (bf16[8,2,128,128]{2,3,1,0:T(8,128)(2,1)S(1)}, bf16[8,2,128,128]{2,3,1,0:T(8,128)(2,1)}, u32[]{:S(2)}) copy-start(bf16[8,2,128,128]{2,3,1,0:T(8,128)(2,1)} %fusion.16) | copy-start | bytes 1572868
  51.3 6.2 %copy-start.12 = (bf16[128,1024]{0,1:T(8,128)(2,1)S(1)}, bf16[128,1024]{0,1:T(8,128)(2,1)}, u32[]{:S(2)}) copy-start(bf16[128,1024]{0,1:T(8,128)(2,1)} %copy-done.11) | copy-start | bytes 786436
  51.3 13.3 %collective-permute-start.4 = (bf16[128,8,128]{0,2,1:T(8,128)(2,1)}, bf16[128,8,128]{0,2,1:T(8,128)(2,1)}, u32[]{:S(2)}, u32[]{:S(2)}) collective-permute-start(bf16[128,8,128]{0,2,1:T(8,128)(2,1)} %fusion.26), channel_id=1, source_target_pairs={{1,0},{2,1},{3,2},{4,3},{5,4},{6,5},{7,6},{8,7},{9,8},{10,9},{11,1... | collective-permute-start | bytes 786440 | tf_op jit(solution)/shard_map/ppermute | solution.py:18
  53.9 11.8 %collective-permute-start.5 = (bf16[128,8,128]{0,2,1:T(8,128)(2,1)}, bf16[128,8,128]{0,2,1:T(8,128)(2,1)}, u32[]{:S(2)}, u32[]{:S(2)}) collective-permute-start(bf16[128,8,128]{0,2,1:T(8,128)(2,1)} %fusion.25), channel_id=1, source_target_pairs={{2,0},{3,1},{4,2},{5,3},{6,4},{7,5},{8,6},{9,7},{10,8},{11,9},{12,... | collective-permute-start | bytes 786440 | tf_op jit(solution)/shard_map/ppermute | solution.py:18
  57.5 1.0 %copy-start.10 = (bf16[128,1024]{0,1:T(8,128)(2,1)S(1)}, bf16[128,1024]{0,1:T(8,128)(2,1)}, u32[]{:S(2)}) copy-start(bf16[128,1024]{0,1:T(8,128)(2,1)} %copy-done.9) | copy-start | bytes 786436
where the time goes:
time: 68.8 us; the launch traced here: 68 us
  starting transfers between devices  24.8 us (36%)
  matrix products  20 us (29%)
  local copies, waits for them, and re-layouts  18.9 us (27%)
  waiting for transfers between devices  2.26 us (3%)
  other arithmetic  1.14 us (2%)
  between operations  0.92 us (1%)
    ppermute x8, starting transfers between devices, passed_along(): lax.ppermute(value, axis, [(source, source + steps) for source in range(l...  24.8 us
    unnamed x40, local copies, waits for them, and re-layouts  14.6 us
    dot_general x3, matrix products, weighted_values(): jnp.einsum('grqk,kgd->qgrd', weights, heads_of_values, preferred_element_...  6.42 us
    ppermute x2, local copies, waits for them, and re-layouts, passed_along(): lax.ppermute(value, axis, [(source, source + steps) for source in range(l...  3.58 us
    dot_general x3, matrix products, pair_grads(): jnp.einsum('grqk,qgrd->kgd', score_grad, heads_of_queries, preferred_elem...  3.51 us
    dot_general x3, matrix products, pair_grads(): jnp.einsum('grqk,qgrd->kgd', weights, head_gradients, preferred_element_t...  3.41 us
    dot_general x3, matrix products, pair_grads(): jnp.einsum('qgrd,kgd->grqk', head_gradients, heads_of_values, preferred_e...  2.78 us
    ppermute x8, waiting for transfers between devices, passed_along(): lax.ppermute(value, axis, [(source, source + steps) for source in range(l...  2.26 us
  transfers between devices with their start and end apart: 8, of which 3 were waited for; matrix products, arithmetic and copies ran while one was open for 36% of the time, Pallas kernels for 0%

commit v1 on v0

v1 whole, which is shorter than its diff:
```python
import functools

import jax
import jax.numpy as jnp
from jax import lax
from jax.experimental import pallas as pl
from jax.experimental.pallas import tpu as pltpu
from jax.sharding import PartitionSpec as P

QUERY_HEADS = 16
KEY_VALUE_HEADS = 8
HEAD_SIZE = 128
LOCAL_WINDOW = 256
GROUP = QUERY_HEADS // KEY_VALUE_HEADS
AXES = ("dp", "seq")

score_scale = 168.0 ** (-0.5)
LOG2E = 1.4426950408889634
NEGATIVE = -1e30
STEP_HEADS = 2

CONTRACT_LAST = (((1,), (1,)), ((), ()))
CONTRACT_FIRST = (((0,), (0,)), ((), ()))


def dot(a, b):
    return jnp.dot(a, b, preferred_element_type=jnp.float32)


def dot_last(a, b):
    return lax.dot_general(a, b, CONTRACT_LAST, preferred_element_type=jnp.float32)


def dot_first(a, b):
    return lax.dot_general(a, b, CONTRACT_FIRST, preferred_element_type=jnp.float32)


def stacked(ref, head):
    wide = GROUP * HEAD_SIZE
    return jnp.concatenate(
        [ref[:, head * wide + j * HEAD_SIZE : head * wide + (j + 1) * HEAD_SIZE] for j in range(GROUP)],
        axis=0,
    )


def columns(ref, head):
    return ref[:, head * HEAD_SIZE : (head + 1) * HEAD_SIZE]


def fill_bias(rank_ref, lens_ref, bias_ref, rows):
    docs = lens_ref.shape[1]
    first = rank_ref[0] * rows
    later = lax.broadcasted_iota(jnp.int32, (docs, docs), 0)
    earlier = lax.broadcasted_iota(jnp.int32, (docs, docs), 1)
    lens = jnp.broadcast_to(lens_ref[...].astype(jnp.float32), (docs, docs))
    ends = jnp.sum(jnp.where(earlier <= later, lens, 0.0), axis=1, keepdims=True)
    wide = GROUP * rows
    query = first + lax.broadcasted_iota(jnp.int32, (1, wide), 1) % rows
    ended = jnp.where(ends <= query.astype(jnp.float32), ends, 0.0)
    start = jnp.max(ended, axis=0, keepdims=True).astype(jnp.int32)
    lowest = jnp.maximum(start, query - (LOCAL_WINDOW - 1))
    key = first - 2 * rows + lax.broadcasted_iota(jnp.int32, (3 * rows, wide), 0)
    bias_ref[...] = jnp.where((key >= lowest) & (key <= query), 0.0, NEGATIVE)


def value_kernel(
    rank_ref, lens_ref, q_ref, g_ref, k2_ref, ka_ref, kb_ref, k0_ref,
    prob_ref, dv2_ref, dv1_ref, dv0_ref, bias_ref,
):
    rows = q_ref.shape[0]

    @pl.when(pl.program_id(0) == 0)
    def _():
        fill_bias(rank_ref, lens_ref, bias_ref, rows)

    for head in range(STEP_HEADS):
        queries = stacked(q_ref, head)
        keys = jnp.concatenate(
            [columns(k2_ref, head), columns(ka_ref, head) + columns(kb_ref, head), columns(k0_ref, head)],
            axis=0,
        )
        scores = dot_last(keys, queries) * (score_scale * LOG2E) + bias_ref[...]
        top = jnp.max(scores, axis=0, keepdims=True)
        raised = jnp.exp2(scores - top)
        total = jnp.sum(raised, axis=0, keepdims=True)
        prob = (raised * (1.0 / total)).astype(jnp.bfloat16)
        prob_ref[head] = prob
        grads = dot(prob, stacked(g_ref, head))
        here = slice(head * HEAD_SIZE, (head + 1) * HEAD_SIZE)
        dv2_ref[:, here] = grads[:rows].astype(jnp.bfloat16)
        dv1_ref[:, here] = grads[rows : 2 * rows].astype(jnp.bfloat16)
        dv0_ref[:, here] = grads[2 * rows :]


def key_kernel(
    prob_ref, q_ref, g_ref, v2_ref, va_ref, vb_ref, v0_ref,
    dscore_ref, dk2_ref, dk1_ref, dk0_ref,
):
    rows = q_ref.shape[0]
    for head in range(STEP_HEADS):
        values = jnp.concatenate(
            [columns(v2_ref, head), columns(va_ref, head) + columns(vb_ref, head), columns(v0_ref, head)],
            axis=0,
        )
        dprob = dot_last(values, stacked(g_ref, head))
        prob = prob_ref[head].astype(jnp.float32)
        delta = jnp.sum(prob * dprob, axis=0, keepdims=True)
        dscore = (prob * (dprob - delta) * score_scale).astype(jnp.bfloat16)
        dscore_ref[head] = dscore
        grads = dot(dscore, stacked(q_ref, head))
        here = slice(head * HEAD_SIZE, (head + 1) * HEAD_SIZE)
        dk2_ref[:, here] = grads[:rows].astype(jnp.bfloat16)
        dk1_ref[:, here] = grads[rows : 2 * rows].astype(jnp.bfloat16)
        dk0_ref[:, here] = grads[2 * rows :]


def query_kernel(
    prob_ref, dscore_ref, k2_ref, ka_ref, kb_ref, k0_ref, v2_ref, va_ref, vb_ref, v0_ref,
    out_ref, dq_ref,
):
    rows = out_ref.shape[0]
    for head in range(STEP_HEADS):
        values = jnp.concatenate(
            [columns(v2_ref, head), columns(va_ref, head) + columns(vb_ref, head), columns(v0_ref, head)],
            axis=0,
        )
        keys = jnp.concatenate(
            [columns(k2_ref, head), columns(ka_ref, head) + columns(kb_ref, head), columns(k0_ref, head)],
            axis=0,
        )
        out = dot_first(prob_ref[head], values)
        grads = dot_first(dscore_ref[head], keys)
        for j in range(GROUP):
            at = (head * GROUP + j) * HEAD_SIZE
            out_ref[:, at : at + HEAD_SIZE] = out[j * rows : (j + 1) * rows].astype(jnp.bfloat16)
            dq_ref[:, at : at + HEAD_SIZE] = grads[j * rows : (j + 1) * rows]


def shape(dims, dtype):
    return jax.ShapeDtypeStruct(dims, dtype)


def on_device(queries, keys, values, output_gradient, doc_lengths):
    rows = queries.shape[0]
    devices = lax.axis_size(AXES)
    rank = lax.axis_index(AXES)
    odd = rank % 2 == 1
    docs = doc_lengths.shape[0]

    ahead = [(r, r + 2) for r in range(devices - 2)]
    behind = [(r + 2, r) for r in range(devices - 2)]
    to_odd = [(r, r + 1) for r in range(0, devices, 2)]
    to_even = [(r + 1, r) for r in range(0, devices, 2)]
    swap = to_odd + to_even

    narrow = STEP_HEADS * HEAD_SIZE
    steps = KEY_VALUE_HEADS // STEP_HEADS
    wide_block = pl.BlockSpec((rows, GROUP * narrow), lambda i: (0, i))
    block = pl.BlockSpec((rows, narrow), lambda i: (0, i))
    pair_block = pl.BlockSpec((STEP_HEADS, 3 * rows, GROUP * rows), lambda i: (i, 0, 0))
    kv_width = keys.shape[1]
    pairs = shape((KEY_VALUE_HEADS, 3 * rows, GROUP * rows), jnp.bfloat16)
    half = shape((rows, kv_width), jnp.bfloat16)
    full = shape((rows, kv_width), jnp.float32)

    k2 = lax.ppermute(keys, AXES, ahead)
    v2 = lax.ppermute(values, AXES, ahead)
    ka = lax.ppermute(keys, AXES, to_odd)
    va = lax.ppermute(values, AXES, to_odd)
    kb = lax.ppermute(k2, AXES, to_even)
    vb = lax.ppermute(v2, AXES, to_even)

    prob, dv2, dv1, dv0 = pl.pallas_call(
        value_kernel,
        grid=(steps,),
        in_specs=[
            pl.BlockSpec(memory_space=pltpu.SMEM),
            pl.BlockSpec((1, docs), lambda i: (0, 0)),
            wide_block, wide_block, block, block, block, block,
        ],
        out_specs=[pair_block, block, block, block],
        out_shape=[pairs, half, half, full],
        scratch_shapes=[pltpu.VMEM((3 * rows, GROUP * rows), jnp.float32)],
        name="value_grads",
    )(rank.reshape(1), doc_lengths.reshape(1, docs), queries, output_gradient, k2, ka, kb, keys)
    dv1 = lax.ppermute(dv1, AXES, swap).astype(jnp.float32)
    dv_send = (dv2.astype(jnp.float32) + jnp.where(odd, dv1, 0.0)).astype(jnp.bfloat16)
    dv_back = lax.ppermute(dv_send, AXES, behind)

    dscore, dk2, dk1, dk0 = pl.pallas_call(
        key_kernel,
        grid=(steps,),
        in_specs=[pair_block, wide_block, wide_block, block, block, block, block],
        out_specs=[pair_block, block, block, block],
        out_shape=[pairs, half, half, full],
        name="key_grads",
    )(prob, queries, output_gradient, v2, va, vb, values)
    dk1 = lax.ppermute(dk1, AXES, swap).astype(jnp.float32)
    dk_send = (dk2.astype(jnp.float32) + jnp.where(odd, dk1, 0.0)).astype(jnp.bfloat16)
    dk_back = lax.ppermute(dk_send, AXES, behind)

    attended, dq = pl.pallas_call(
        query_kernel,
        grid=(steps,),
        in_specs=[pair_block, pair_block] + [block] * 8,
        out_specs=[wide_block, wide_block],
        out_shape=[shape(queries.shape, jnp.bfloat16), shape(queries.shape, jnp.float32)],
        name="query_grads",
    )(prob, dscore, k2, ka, kb, keys, v2, va, vb, values)

    dv = dv0 + jnp.where(odd, 0.0, dv1) + dv_back.astype(jnp.float32)
    dk = dk0 + jnp.where(odd, 0.0, dk1) + dk_back.astype(jnp.float32)
    return attended, dq, dk, dv


def solution(mesh):
    split = P(AXES, None)
    return jax.shard_map(
        on_device,
        mesh=mesh,
        in_specs=(split, split, split, split, P()),
        out_specs=(split, split, split, split),
        check_vma=False,
    )
```

time: 68.8 us -> 55.1 us (0.80)
  the two profiles are of different devices: /device:TPU:2 before, /device:TPU:6 now
where the time goes in v1:
time: 55.1 us; the launch traced here: 54.6 us
  starting transfers between devices  24 us (44%)
  Pallas kernels  15.6 us (28%)
  waiting for transfers between devices  10.7 us (19%)
  other arithmetic  1.97 us (4%)
  local copies, waits for them, and re-layouts  1.57 us (3%)
  between operations  0.84 us (2%)
    ppermute x1, waiting for transfers between devices, on_device(): dk_back = lax.ppermute(dk_send, AXES, behind)  7.43 us
    ppermute x1, starting transfers between devices, on_device(): dv_back = lax.ppermute(dv_send, AXES, behind)  6.01 us
    pallas_call x1, Pallas kernels, on_device(): pl.pallas_call(value_kernel, grid=(steps,), in_specs=[pl.BlockSpec(memory...  5.34 us
    pallas_call x1, Pallas kernels, on_device(): pl.pallas_call(key_kernel, grid=(steps,), in_specs=[pair_block, wide_bloc...  5.31 us
    pallas_call x1, Pallas kernels, on_device(): pl.pallas_call(query_kernel, grid=(steps,), in_specs=[pair_block, pair_bl...  4.92 us
    ppermute x1, starting transfers between devices, on_device(): k2 = lax.ppermute(keys, AXES, ahead)  3.43 us
    ppermute x1, starting transfers between devices, on_device(): v2 = lax.ppermute(values, AXES, ahead)  3.43 us
    ppermute x1, waiting for transfers between devices, on_device(): k2 = lax.ppermute(keys, AXES, ahead)  3.11 us
  transfers between devices with their start and end apart: 10, of which 3 were waited for; matrix products, arithmetic and copies ran while one was open for 2% of the time, Pallas kernels for 29%

profile of v1, /device:TPU:6, one launch (start us, length us, event | category | flops | bytes accessed | tf_op | source)
XLA Modules:
  0.0 54.6 jit_solution(999026482276441360)
XLA Ops:
  0.6 3.4 %collective-permute-start = (bf16[128,1024]{1,0:T(8,128)(2,1)}, bf16[128,1024]{1,0:T(8,128)(2,1)S(1)}, u32[]{:S(2)}, u32[]{:S(2)}) collective-permute-start(bf16[128,1024]{1,0:T(8,128)(2,1)} %k0_ref.3), channel_id=1, source_target_pairs={{0,2},{1,3},{2,4},{3,5},{4,6},{5,7},{6,8},{7,9},{8,10},{9,11},{10,... | collective-permute-start | bytes 786440 | tf_op jit(solution)/shard_map/ppermute | solution.py:166
  4.1 3.4 %collective-permute-start.3 = (bf16[128,1024]{1,0:T(8,128)(2,1)}, bf16[128,1024]{1,0:T(8,128)(2,1)S(1)}, u32[]{:S(2)}, u32[]{:S(2)}) collective-permute-start(bf16[128,1024]{1,0:T(8,128)(2,1)} %v0_ref.3), channel_id=1, source_target_pairs={{0,2},{1,3},{2,4},{3,5},{4,6},{5,7},{6,8},{7,9},{8,10},{9,11},{10,... | collective-permute-start | bytes 786440 | tf_op jit(solution)/shard_map/ppermute | solution.py:167
  7.5 1.3 %collective-permute-start.1 = (bf16[128,1024]{1,0:T(8,128)(2,1)}, bf16[128,1024]{1,0:T(8,128)(2,1)S(1)}, u32[]{:S(2)}, u32[]{:S(2)}) collective-permute-start(bf16[128,1024]{1,0:T(8,128)(2,1)} %k0_ref.3), channel_id=1, source_target_pairs={{0,1},{2,3},{4,5},{6,7},{8,9},{10,11},{12,13},{14,15},{16,17},{18,... | collective-permute-start | bytes 786440 | tf_op jit(solution)/shard_map/ppermute | solution.py:168
  8.8 3.1 %collective-permute-done.k2_ref = bf16[128,1024]{1,0:T(8,128)(2,1)S(1)} collective-permute-done((bf16[128,1024]{1,0:T(8,128)(2,1)}, bf16[128,1024]{1,0:T(8,128)(2,1)S(1)}, u32[]{:S(2)}, u32[]{:S(2)}) %collective-permute-start) | collective-permute-done | bytes 262176 | tf_op jit(solution)/shard_map/ppermute | solution.py:166
  11.9 1.3 %collective-permute-start.2 = (bf16[128,1024]{1,0:T(8,128)(2,1)S(1)}, bf16[128,1024]{1,0:T(8,128)(2,1)S(1)}, u32[]{:S(2)}, u32[]{:S(2)}) collective-permute-start(bf16[128,1024]{1,0:T(8,128)(2,1)S(1)} %collective-permute-done.k2_ref), channel_id=1, source_target_pairs={{1,0},{3,2},{5,4},{7,6},{9,8},{11,10},{13,12},{15,14},{17,16},{19,... | collective-permute-start | bytes 786440 | tf_op jit(solution)/shard_map/ppermute | solution.py:170
  13.2 3.1 %collective-permute-start.4 = (bf16[128,1024]{1,0:T(8,128)(2,1)}, bf16[128,1024]{1,0:T(8,128)(2,1)S(1)}, u32[]{:S(2)}, u32[]{:S(2)}) collective-permute-start(bf16[128,1024]{1,0:T(8,128)(2,1)} %v0_ref.3), channel_id=1, source_target_pairs={{0,1},{2,3},{4,5},{6,7},{8,9},{10,11},{12,13},{14,15},{16,17},{18,... | collective-permute-start | bytes 786440 | tf_op jit(solution)/shard_map/ppermute | solution.py:169
  16.3 0.1 collective-permute-done.3.v2_ref
  16.4 1.3 %collective-permute-start.5 = (bf16[128,1024]{1,0:T(8,128)(2,1)S(1)}, bf16[128,1024]{1,0:T(8,128)(2,1)S(1)}, u32[]{:S(2)}, u32[]{:S(2)}) collective-permute-start(bf16[128,1024]{1,0:T(8,128)(2,1)S(1)} %collective-permute-done.3.v2_ref), channel_id=1, source_target_pairs={{1,0},{3,2},{5,4},{7,6},{9,8},{11,10},{13,12},{15,14},{17,16},{19,... | collective-permute-start | bytes 786440 | tf_op jit(solution)/shard_map/ppermute | solution.py:171
  17.7 0.7 %copy-done.4 = bf16[128,1024]{1,0:T(8,128)(2,1)} copy-done((bf16[128,1024]{1,0:T(8,128)(2,1)}, bf16[128,1024]{1,0:T(8,128)(2,1)S(1)}, u32[]{:S(2)}) %copy-start.4) | copy-done | bytes 262168
  18.4 0.1 copy-done.5
  18.5 5.3 %value_grads.1 = (bf16[8,384,256]{2,1,0:T(8,128)(2,1)}, bf16[128,1024]{1,0:T(8,128)(2,1)}, bf16[128,1024]{1,0:T(8,128)(2,1)}, f32[128,1024]{1,0:T(8,128)}) custom-call(s32[1]{0:T(128)} %bitcast.rank_ref, s32[1,32]{1,0:T(1,128)} %bitcast.2, bf16[128,2048]{1,0:T(8,128)(2,1)} %q_ref.3, bf16[128,2048]{1,0:T(8,128)(2,1)} %g_ref.3, bf16[128,1024]{1,0:T(8,128)(2,1)} %copy-done.3, ...), custom_call_target="tpu_custom_call" | custom-call | tf_op jit(solution)/shard_map/value_grads/pallas_call | solution.py:173
  23.8 1.2 %collective-permute-start.8 = (bf16[128,1024]{1,0:T(8,128)(2,1)}, bf16[128,1024]{1,0:T(8,128)(2,1)S(1)}, u32[]{:S(2)}, u32[]{:S(2)}) collective-permute-start(bf16[128,1024]{1,0:T(8,128)(2,1)} %get-tuple-element.22), channel_id=1, source_target_pairs={{0,1},{2,3},{4,5},{6,7},{8,9},{10,11},{12,13},{14,15},{16,17},{18,... | collective-permute-start | bytes 786440 | tf_op jit(solution)/shard_map/ppermute | solution.py:186
  25.1 0.7 %copy-done.1 = bf16[128,1024]{1,0:T(8,128)(2,1)} copy-done((bf16[128,1024]{1,0:T(8,128)(2,1)}, bf16[128,1024]{1,0:T(8,128)(2,1)S(1)}, u32[]{:S(2)}) %copy-start.1) | copy-done | bytes 262168
  25.8 0.1 copy-done.2
  25.8 5.3 %key_grads.1 = (bf16[8,384,256]{2,1,0:T(8,128)(2,1)}, bf16[128,1024]{1,0:T(8,128)(2,1)}, bf16[128,1024]{1,0:T(8,128)(2,1)}, f32[128,1024]{1,0:T(8,128)}) custom-call(bf16[8,384,256]{2,1,0:T(8,128)(2,1)} %get-tuple-element.14.prob_ref, bf16[128,2048]{1,0:T(8,128)(2,1)} %q_ref.3, bf16[128,2048]{1,0:T(8,128)(2,1)} %g_ref.3, bf16[128,1024]{1,0:T(8,128)(2,1)} %copy-done, ...), custom_call_target="tpu_custom_call" | custom-call | tf_op jit(solution)/shard_map/key_grads/pallas_call | solution.py:190
  31.2 0.1 collective-permute-start.6
  31.2 0.1 fusion.7
  31.3 6.0 %collective-permute-start.9 = (bf16[128,1024]{1,0:T(8,128)(2,1)S(1)}, bf16[128,1024]{1,0:T(8,128)(2,1)S(1)}, u32[]{:S(2)}, u32[]{:S(2)}) collective-permute-start(bf16[128,1024]{1,0:T(8,128)(2,1)S(1)} %fusion.7), channel_id=1, source_target_pairs={{2,0},{3,1},{4,2},{5,3},{6,4},{7,5},{8,6},{9,7},{10,8},{11,9},{12,... | collective-permute-start | bytes 786440 | tf_op jit(solution)/shard_map/ppermute | solution.py:188
  37.3 4.9 %query_grads.1 = (bf16[128,2048]{1,0:T(8,128)(2,1)}, f32[128,2048]{1,0:T(8,128)}) custom-call(bf16[8,384,256]{2,1,0:T(8,128)(2,1)} %get-tuple-element.14.prob_ref, bf16[8,384,256]{2,1,0:T(8,128)(2,1)} %get-tuple-element.15.dscore_ref, bf16[128,1024]{1,0:T(8,128)(2,1)} %copy-done.3, bf16[128,1024]{1,0:T(8,128)(2,1)} %copy-done.4, ...), custom_call_target="tpu_custom_call" | custom-call | tf_op jit(solution)/shard_map/query_grads/pallas_call | solution.py:202
  42.3 0.1 fusion.3
  42.4 3.0 %collective-permute-start.7 = (bf16[128,1024]{1,0:T(8,128)(2,1)S(1)}, bf16[128,1024]{1,0:T(8,128)(2,1)S(1)}, u32[]{:S(2)}, u32[]{:S(2)}) collective-permute-start(bf16[128,1024]{1,0:T(8,128)(2,1)S(1)} %fusion.3), channel_id=1, source_target_pairs={{2,0},{3,1},{4,2},{5,3},{6,4},{7,5},{8,6},{9,7},{10,8},{11,9},{12,... | collective-permute-start | bytes 786440 | tf_op jit(solution)/shard_map/ppermute | solution.py:200
  45.4 0.9 %fusion.5 = f32[128,1024]{1,0:T(8,128)} fusion(f32[128,1024]{1,0:T(8,128)S(1)} %copy-done.6, bf16[128,1024]{1,0:T(8,128)(2,1)S(1)} %collective-permute-done.8, bf16[128,1024]{1,0:T(8,128)(2,1)S(1)} %collective-permute-done.9, pred[]{:T(512)S(6)} %eq.5), kind=kLoop, calls=%fused_computation.9 | loop fusion | flops 655360 | bytes 1572865 | tf_op jit(solution)/shard_map/add | solution.py:211
  46.3 7.4 %collective-permute-done.7 = bf16[128,1024]{1,0:T(8,128)(2,1)S(1)} collective-permute-done((bf16[128,1024]{1,0:T(8,128)(2,1)S(1)}, bf16[128,1024]{1,0:T(8,128)(2,1)S(1)}, u32[]{:S(2)}, u32[]{:S(2)}) %collective-permute-start.7) | collective-permute-done | bytes 262176 | tf_op jit(solution)/shard_map/ppermute | solution.py:200
  53.7 0.9 %fusion.1 = f32[128,1024]{1,0:T(8,128)} fusion(f32[128,1024]{1,0:T(8,128)S(1)} %copy-done.7, bf16[128,1024]{1,0:T(8,128)(2,1)S(1)} %collective-permute-done.6, bf16[128,1024]{1,0:T(8,128)(2,1)S(1)} %collective-permute-done.7, pred[]{:T(512)S(6)} %eq.5), kind=kLoop, calls=%fused_computation.5 | loop fusion | flops 655360 | bytes 1572865 | tf_op jit(solution)/shard_map/add | solution.py:212
  (23 shorter events, 0.1 us)
Async XLA Ops:
  0.6 11.3 %collective-permute-start = (bf16[128,1024]{1,0:T(8,128)(2,1)}, bf16[128,1024]{1,0:T(8,128)(2,1)S(1)}, u32[]{:S(2)}, u32[]{:S(2)}) collective-permute-start(bf16[128,1024]{1,0:T(8,128)(2,1)} %k0_ref.3), channel_id=1, source_target_pairs={{0,2},{1,3},{2,4},{3,5},{4,6},{5,7},{6,8},{7,9},{8,10},{9,11},{10,... | collective-permute-start | bytes 786440 | tf_op jit(solution)/shard_map/ppermute | solution.py:166
  4.1 12.3 %collective-permute-start.3 = (bf16[128,1024]{1,0:T(8,128)(2,1)}, bf16[128,1024]{1,0:T(8,128)(2,1)S(1)}, u32[]{:S(2)}, u32[]{:S(2)}) collective-permute-start(bf16[128,1024]{1,0:T(8,128)(2,1)} %v0_ref.3), channel_id=1, source_target_pairs={{0,2},{1,3},{2,4},{3,5},{4,6},{5,7},{6,8},{7,9},{8,10},{9,11},{10,... | collective-permute-start | bytes 786440 | tf_op jit(solution)/shard_map/ppermute | solution.py:167
  7.5 10.2 %collective-permute-start.1 = (bf16[128,1024]{1,0:T(8,128)(2,1)}, bf16[128,1024]{1,0:T(8,128)(2,1)S(1)}, u32[]{:S(2)}, u32[]{:S(2)}) collective-permute-start(bf16[128,1024]{1,0:T(8,128)(2,1)} %k0_ref.3), channel_id=1, source_target_pairs={{0,1},{2,3},{4,5},{6,7},{8,9},{10,11},{12,13},{14,15},{16,17},{18,... | collective-permute-start | bytes 786440 | tf_op jit(solution)/shard_map/ppermute | solution.py:168
  11.9 5.8 %copy-start.3 = (bf16[128,1024]{1,0:T(8,128)(2,1)}, bf16[128,1024]{1,0:T(8,128)(2,1)S(1)}, u32[]{:S(2)}) copy-start(bf16[128,1024]{1,0:T(8,128)(2,1)S(1)} %collective-permute-done.k2_ref) | copy-start | bytes 786436
  11.9 5.8 %collective-permute-start.2 = (bf16[128,1024]{1,0:T(8,128)(2,1)S(1)}, bf16[128,1024]{1,0:T(8,128)(2,1)S(1)}, u32[]{:S(2)}, u32[]{:S(2)}) collective-permute-start(bf16[128,1024]{1,0:T(8,128)(2,1)S(1)} %collective-permute-done.k2_ref), channel_id=1, source_target_pairs={{1,0},{3,2},{5,4},{7,6},{9,8},{11,10},{13,12},{15,14},{17,16},{19,... | collective-permute-start | bytes 786440 | tf_op jit(solution)/shard_map/ppermute | solution.py:170
  13.2 11.8 %collective-permute-start.4 = (bf16[128,1024]{1,0:T(8,128)(2,1)}, bf16[128,1024]{1,0:T(8,128)(2,1)S(1)}, u32[]{:S(2)}, u32[]{:S(2)}) collective-permute-start(bf16[128,1024]{1,0:T(8,128)(2,1)} %v0_ref.3), channel_id=1, source_target_pairs={{0,1},{2,3},{4,5},{6,7},{8,9},{10,11},{12,13},{14,15},{16,17},{18,... | collective-permute-start | bytes 786440 | tf_op jit(solution)/shard_map/ppermute | solution.py:169
  16.4 8.7 %copy-start = (bf16[128,1024]{1,0:T(8,128)(2,1)}, bf16[128,1024]{1,0:T(8,128)(2,1)S(1)}, u32[]{:S(2)}) copy-start(bf16[128,1024]{1,0:T(8,128)(2,1)S(1)} %collective-permute-done.3.v2_ref) | copy-start | bytes 786436
  16.4 8.6 %collective-permute-start.5 = (bf16[128,1024]{1,0:T(8,128)(2,1)S(1)}, bf16[128,1024]{1,0:T(8,128)(2,1)S(1)}, u32[]{:S(2)}, u32[]{:S(2)}) collective-permute-start(bf16[128,1024]{1,0:T(8,128)(2,1)S(1)} %collective-permute-done.3.v2_ref), channel_id=1, source_target_pairs={{1,0},{3,2},{5,4},{7,6},{9,8},{11,10},{13,12},{15,14},{17,16},{19,... | collective-permute-start | bytes 786440 | tf_op jit(solution)/shard_map/ppermute | solution.py:171
  17.7 0.7 %copy-start.4 = (bf16[128,1024]{1,0:T(8,128)(2,1)}, bf16[128,1024]{1,0:T(8,128)(2,1)S(1)}, u32[]{:S(2)}) copy-start(bf16[128,1024]{1,0:T(8,128)(2,1)S(1)} %collective-permute-done.1.ka_ref) | copy-start | bytes 786436
  17.7 0.8 %copy-start.5 = (bf16[128,1024]{1,0:T(8,128)(2,1)}, bf16[128,1024]{1,0:T(8,128)(2,1)S(1)}, u32[]{:S(2)}) copy-start(bf16[128,1024]{1,0:T(8,128)(2,1)S(1)} %collective-permute-done.2.kb_ref) | copy-start | bytes 786436
  23.8 7.4 %collective-permute-start.8 = (bf16[128,1024]{1,0:T(8,128)(2,1)}, bf16[128,1024]{1,0:T(8,128)(2,1)S(1)}, u32[]{:S(2)}, u32[]{:S(2)}) collective-permute-start(bf16[128,1024]{1,0:T(8,128)(2,1)} %get-tuple-element.22), channel_id=1, source_target_pairs={{0,1},{2,3},{4,5},{6,7},{8,9},{10,11},{12,13},{14,15},{16,17},{18,... | collective-permute-start | bytes 786440 | tf_op jit(solution)/shard_map/ppermute | solution.py:186
  25.0 0.7 %copy-start.1 = (bf16[128,1024]{1,0:T(8,128)(2,1)}, bf16[128,1024]{1,0:T(8,128)(2,1)S(1)}, u32[]{:S(2)}) copy-start(bf16[128,1024]{1,0:T(8,128)(2,1)S(1)} %collective-permute-done.4.va_ref) | copy-start | bytes 786436
  25.0 0.8 %copy-start.2 = (bf16[128,1024]{1,0:T(8,128)(2,1)}, bf16[128,1024]{1,0:T(8,128)(2,1)S(1)}, u32[]{:S(2)}) copy-start(bf16[128,1024]{1,0:T(8,128)(2,1)S(1)} %collective-permute-done.5.vb_ref) | copy-start | bytes 786436
  25.8 5.4 %copy-start.8 = (bf16[128,1024]{1,0:T(8,128)(2,1)S(1)}, bf16[128,1024]{1,0:T(8,128)(2,1)}, u32[]{:S(2)}) copy-start(bf16[128,1024]{1,0:T(8,128)(2,1)} %get-tuple-element.23) | copy-start | bytes 786436
  31.2 11.1 %collective-permute-start.6 = (bf16[128,1024]{1,0:T(8,128)(2,1)}, bf16[128,1024]{1,0:T(8,128)(2,1)S(1)}, u32[]{:S(2)}, u32[]{:S(2)}) collective-permute-start(bf16[128,1024]{1,0:T(8,128)(2,1)} %get-tuple-element.19), channel_id=1, source_target_pairs={{0,1},{2,3},{4,5},{6,7},{8,9},{10,11},{12,13},{14,15},{16,17},{18,... | collective-permute-start | bytes 786440 | tf_op jit(solution)/shard_map/ppermute | solution.py:198
  31.3 14.1 %collective-permute-start.9 = (bf16[128,1024]{1,0:T(8,128)(2,1)S(1)}, bf16[128,1024]{1,0:T(8,128)(2,1)S(1)}, u32[]{:S(2)}, u32[]{:S(2)}) collective-permute-start(bf16[128,1024]{1,0:T(8,128)(2,1)S(1)} %fusion.7), channel_id=1, source_target_pairs={{2,0},{3,1},{4,2},{5,3},{6,4},{7,5},{8,6},{9,7},{10,8},{11,9},{12,... | collective-permute-start | bytes 786440 | tf_op jit(solution)/shard_map/ppermute | solution.py:188
  37.3 5.0 %copy-start.9 = (bf16[128,1024]{1,0:T(8,128)(2,1)S(1)}, bf16[128,1024]{1,0:T(8,128)(2,1)}, u32[]{:S(2)}) copy-start(bf16[128,1024]{1,0:T(8,128)(2,1)} %get-tuple-element.20) | copy-start | bytes 786436
  37.3 8.0 %copy-start.6 = (f32[128,1024]{1,0:T(8,128)S(1)}, f32[128,1024]{1,0:T(8,128)}, u32[]{:S(2)}) copy-start(f32[128,1024]{1,0:T(8,128)} %get-tuple-element.21) | copy-start | bytes 1572868
  42.3 11.5 %copy-start.7 = (f32[128,1024]{1,0:T(8,128)S(1)}, f32[128,1024]{1,0:T(8,128)}, u32[]{:S(2)}) copy-start(f32[128,1024]{1,0:T(8,128)} %get-tuple-element.18) | copy-start | bytes 1572868
  42.4 11.3 %collective-permute-start.7 = (bf16[128,1024]{1,0:T(8,128)(2,1)S(1)}, bf16[128,1024]{1,0:T(8,128)(2,1)S(1)}, u32[]{:S(2)}, u32[]{:S(2)}) collective-permute-start(bf16[128,1024]{1,0:T(8,128)(2,1)S(1)} %fusion.3), channel_id=1, source_target_pairs={{2,0},{3,1},{4,2},{5,3},{6,4},{7,5},{8,6},{9,7},{10,8},{11,9},{12,... | collective-permute-start | bytes 786440 | tf_op jit(solution)/shard_map/ppermute | solution.py:200

commit v2 on v1

v2 whole, which is shorter than its diff:
```python
import jax
import jax.numpy as jnp
from jax import lax
from jax.experimental import pallas as pl
from jax.experimental.pallas import tpu as pltpu
from jax.sharding import PartitionSpec as P

QUERY_HEADS = 16
KEY_VALUE_HEADS = 8
HEAD_SIZE = 128
LOCAL_WINDOW = 256
GROUP = QUERY_HEADS // KEY_VALUE_HEADS
CORES = 2
CORE_HEADS = KEY_VALUE_HEADS // CORES
AXES = ("dp", "seq")

score_scale = 168.0 ** (-0.5)
LOG2E = 1.4426950408889634
NEGATIVE = -1e30

CONTRACT_LAST = (((1,), (1,)), ((), ()))
CONTRACT_FIRST = (((0,), (0,)), ((), ()))


def dot(a, b):
    return jnp.dot(a, b, preferred_element_type=jnp.float32)


def dot_last(a, b):
    return lax.dot_general(a, b, CONTRACT_LAST, preferred_element_type=jnp.float32)


def dot_first(a, b):
    return lax.dot_general(a, b, CONTRACT_FIRST, preferred_element_type=jnp.float32)


def span(head):
    return slice(head * HEAD_SIZE, (head + 1) * HEAD_SIZE)


def both(odd, mine, other, head):
    a, b = mine[:, span(head)], other[:, span(head)]
    return jnp.where(odd, b, a), jnp.where(odd, a, b)


def stacked(odd, mine, other, head):
    pieces = [both(odd, mine, other, head * GROUP + j) for j in range(GROUP)]
    return [jnp.concatenate([piece[block] for piece in pieces], axis=0) for block in range(CORES)]


def put(odd, mine, other, head, first, second):
    mine[:, span(head)] = jnp.where(odd, second, first).astype(mine.dtype)
    other[:, span(head)] = jnp.where(odd, first, second).astype(other.dtype)


def split_kernel(rank_ref, *refs):
    count = len(refs) // 3
    odd = rank_ref[0] % 2
    for i in range(count):
        source, mine, other = refs[i], refs[count + 2 * i], refs[count + 2 * i + 1]
        width = source.shape[1] // 2

        @pl.when(odd == 0)
        def _():
            mine[...] = source[:, :width]
            other[...] = source[:, width:]

        @pl.when(odd == 1)
        def _():
            mine[...] = source[:, width:]
            other[...] = source[:, :width]


def bias_kernel(rank_ref, lens_ref, bias_ref):
    _, span_rows, rows = bias_ref.shape
    docs = lens_ref.shape[1]
    later = lax.broadcasted_iota(jnp.int32, (docs, docs), 0)
    earlier = lax.broadcasted_iota(jnp.int32, (docs, docs), 1)
    lens = jnp.broadcast_to(lens_ref[...].astype(jnp.float32), (docs, docs))
    ends = jnp.sum(jnp.where(earlier <= later, lens, 0.0), axis=1, keepdims=True)
    for block in range(CORES):
        first = (rank_ref[0] // CORES * CORES + block) * rows
        query = first + lax.broadcasted_iota(jnp.int32, (1, rows), 1)
        ended = jnp.where(ends <= query.astype(jnp.float32), ends, 0.0)
        start = jnp.max(ended, axis=0, keepdims=True).astype(jnp.int32)
        lowest = jnp.maximum(start, query - (LOCAL_WINDOW - 1))
        key = first - 2 * rows + lax.broadcasted_iota(jnp.int32, (span_rows, rows), 0)
        bias_ref[block] = jnp.where((key >= lowest) & (key <= query), 0.0, NEGATIVE)


def value_kernel(
    rank_ref, bias_ref, qm, qo, gm, go, km, ko, k2m, k2o,
    prob_ref, dvm, dvo,
):
    rows = qm.shape[0]
    odd = rank_ref[0] % 2 == 1
    for head in range(CORE_HEADS):
        blocks = both(odd, k2m, k2o, head) + both(odd, km, ko, head)
        queries = stacked(odd, qm, qo, head)
        gradients = stacked(odd, gm, go, head)
        grads = []
        for block in range(CORES):
            keys = jnp.concatenate(blocks[block : block + 3], axis=0)
            bias = jnp.concatenate([bias_ref[block]] * GROUP, axis=1)
            scores = dot_last(keys, queries[block]) * (score_scale * LOG2E) + bias
            top = jnp.max(scores, axis=0, keepdims=True)
            raised = jnp.exp2(scores - top)
            total = jnp.sum(raised, axis=0, keepdims=True)
            prob = (raised * (1.0 / total)).astype(jnp.bfloat16)
            prob_ref[head * CORES + block] = prob
            grads.append(dot(prob[: (2 - block) * rows], gradients[block]))
        put(odd, dvm, dvo, head, grads[0][:rows], grads[0][rows:] + grads[1])


def key_kernel(
    rank_ref, prob_ref, qm, qo, gm, go, vm, vo, v2m, v2o,
    dscore_ref, dkm, dko,
):
    rows = qm.shape[0]
    odd = rank_ref[0] % 2 == 1
    for head in range(CORE_HEADS):
        blocks = both(odd, v2m, v2o, head) + both(odd, vm, vo, head)
        queries = stacked(odd, qm, qo, head)
        gradients = stacked(odd, gm, go, head)
        grads = []
        for block in range(CORES):
            values = jnp.concatenate(blocks[block : block + 3], axis=0)
            dprob = dot_last(values, gradients[block])
            prob = prob_ref[head * CORES + block].astype(jnp.float32)
            delta = jnp.sum(prob * dprob, axis=0, keepdims=True)
            dscore = (prob * ((dprob - delta) * score_scale)).astype(jnp.bfloat16)
            dscore_ref[head * CORES + block] = dscore
            grads.append(dot(dscore[: (2 - block) * rows], queries[block]))
        put(odd, dkm, dko, head, grads[0][:rows], grads[0][rows:] + grads[1])


def rest_kernel(
    rank_ref, prob_ref, dscore_ref, qm, qo, gm, go, km, ko, k2m, k2o, vm, vo, v2m, v2o,
    outm, outo, dqm, dqo, dkm, dko, dvm, dvo,
):
    rows = qm.shape[0]
    odd = rank_ref[0] % 2 == 1
    for head in range(CORE_HEADS):
        keys = both(odd, k2m, k2o, head) + both(odd, km, ko, head)
        values = both(odd, v2m, v2o, head) + both(odd, vm, vo, head)
        queries = stacked(odd, qm, qo, head)
        gradients = stacked(odd, gm, go, head)
        outs, dqs, dks, dvs = [], [], [], []
        for block in range(CORES):
            prob = prob_ref[head * CORES + block]
            dscore = dscore_ref[head * CORES + block]
            outs.append(dot_first(prob, jnp.concatenate(values[block : block + 3], axis=0)))
            dqs.append(dot_first(dscore, jnp.concatenate(keys[block : block + 3], axis=0)))
            dks.append(dot(dscore[(2 - block) * rows :], queries[block]))
            dvs.append(dot(prob[(2 - block) * rows :], gradients[block]))
        for j in range(GROUP):
            at = slice(j * rows, (j + 1) * rows)
            put(odd, outm, outo, head * GROUP + j, outs[0][at], outs[1][at])
            put(odd, dqm, dqo, head * GROUP + j, dqs[0][at], dqs[1][at])
        put(odd, dkm, dko, head, dks[0] + dks[1][:rows], dks[1][rows:])
        put(odd, dvm, dvo, head, dvs[0] + dvs[1][:rows], dvs[1][rows:])


def join_kernel(rank_ref, *refs):
    count = len(refs) // 3
    odd = rank_ref[0] % 2
    for i in range(count):
        mine, other, target = refs[2 * i], refs[2 * i + 1], refs[2 * count + i]
        width = target.shape[1] // 2

        @pl.when(odd == 0)
        def _():
            target[:, :width] = mine[...]
            target[:, width:] = other[...]

        @pl.when(odd == 1)
        def _():
            target[:, width:] = mine[...]
            target[:, :width] = other[...]


def add_kernel(rank_ref, mine, other, backm, backo, target):
    odd = rank_ref[0] % 2
    width = target.shape[1] // 2

    @pl.when(odd == 0)
    def _():
        target[:, :width] = mine[...] + backm[...].astype(jnp.float32)
        target[:, width:] = other[...] + backo[...].astype(jnp.float32)

    @pl.when(odd == 1)
    def _():
        target[:, width:] = mine[...] + backm[...].astype(jnp.float32)
        target[:, :width] = other[...] + backo[...].astype(jnp.float32)


def shape(dims, dtype):
    return jax.ShapeDtypeStruct(dims, dtype)


def run(kernel, name, outputs, index, *operands):
    small = pl.BlockSpec(memory_space=pltpu.SMEM)
    whole = pl.BlockSpec(memory_space=pltpu.VMEM)
    return pl.pallas_call(
        kernel,
        in_specs=[small] + [whole] * len(operands),
        out_specs=[whole] * len(outputs),
        out_shape=outputs,
        compiler_params=pltpu.CompilerParams(vmem_limit_bytes=40 * 2**20),
        cost_estimate=pl.CostEstimate(flops=5000000000, bytes_accessed=1, transcendentals=0),
        name=name,
    )(index, *operands)


def on_device(queries, keys, values, output_gradient, doc_lengths):
    rows = queries.shape[0]
    devices = lax.axis_size(AXES)
    index = lax.axis_index(AXES).reshape(1)
    docs = doc_lengths.shape[0]

    ahead = [(r, (r + 2) % devices) for r in range(devices)]
    across = [(r, ((r + 2) % devices) ^ 1) for r in range(devices)]
    behind = [(there, here) for here, there in ahead]
    recross = [(there, here) for here, there in across]
    swap = [(r, r ^ 1) for r in range(devices)]

    def moved(value, pairs):
        return lax.ppermute(value, AXES, pairs)

    narrow = shape((rows, keys.shape[1] // CORES), jnp.bfloat16)
    wide = shape((rows, queries.shape[1] // CORES), jnp.bfloat16)
    narrow_sum = shape(narrow.shape, jnp.float32)
    wide_sum = shape(wide.shape, jnp.float32)
    pairs = shape((KEY_VALUE_HEADS, 3 * rows, GROUP * rows), jnp.bfloat16)

    km, kx = run(split_kernel, "split_keys", [narrow] * 2, index, keys)
    k2m, k2o = moved(km, ahead), moved(kx, across)
    vm, vx = run(split_kernel, "split_values", [narrow] * 2, index, values)
    v2m, v2o = moved(vm, ahead), moved(vx, across)
    qm, qx, gm, gx = run(split_kernel, "split_rows", [wide] * 4, index, queries, output_gradient)
    ko, vo, qo, go = (moved(x, swap) for x in (kx, vx, qx, gx))
    (bias,) = run(
        bias_kernel, "bias", [shape((CORES, 3 * rows, rows), jnp.float32)],
        index, doc_lengths.reshape(1, docs),
    )

    prob, dvm, dvo = run(
        value_kernel, "value_grads", [pairs, narrow, narrow],
        index, bias, qm, qo, gm, go, km, ko, k2m, k2o,
    )
    dv_back = moved(dvm, behind), moved(dvo, recross)
    dscore, dkm, dko = run(
        key_kernel, "key_grads", [pairs, narrow, narrow],
        index, prob, qm, qo, gm, go, vm, vo, v2m, v2o,
    )
    dk_back = moved(dkm, behind), moved(dko, recross)
    outm, outo, dqm, dqo, dkm, dko, dvm, dvo = run(
        rest_kernel, "other_grads",
        [wide, wide, wide_sum, wide_sum, narrow_sum, narrow_sum, narrow_sum, narrow_sum],
        index, prob, dscore, qm, qo, gm, go, km, ko, k2m, k2o, vm, vo, v2m, v2o,
    )
    outo, dqo, dko, dvo = (moved(x, swap) for x in (outo, dqo, dko, dvo))
    attended, dq = run(
        join_kernel, "join_rows",
        [shape(queries.shape, jnp.bfloat16), shape(queries.shape, jnp.float32)],
        index, outm, outo, dqm, dqo,
    )
    full = shape(keys.shape, jnp.float32)
    (dv,) = run(add_kernel, "join_values", [full], index, dvm, dvo, *dv_back)
    (dk,) = run(add_kernel, "join_keys", [full], index, dkm, dko, *dk_back)
    return attended, dq, dk, dv


def solution(mesh):
    split = P(AXES, None)
    return jax.shard_map(
        on_device,
        mesh=mesh,
        in_specs=(split, split, split, split, P()),
        out_specs=(split, split, split, split),
        check_vma=False,
    )
```

time: 55.1 us -> 43.9 us (0.80)
  the two profiles are of different devices: /device:TPU:6 before, /device:TPU:0 now
where the time goes in v2:
time: 43.9 us; the launch traced here: 43.8 us
  waiting for transfers between devices  21.5 us (49%)
  starting transfers between devices  10.5 us (24%)
  Pallas kernels  9.91 us (23%)
  local copies, waits for them, and re-layouts  1.09 us (2%)
  between operations  0.74 us (2%)
    ppermute x16, waiting for transfers between devices, moved(): return lax.ppermute(value, AXES, pairs)  21.5 us
    ppermute x16, starting transfers between devices, moved(): return lax.ppermute(value, AXES, pairs)  10.5 us
    pallas_call x10, Pallas kernels, run(): pl.pallas_call(kernel, in_specs=[small] + [whole] * len(operands), out_sp...  9.91 us
    unnamed x10, local copies, waits for them, and re-layouts  1.09 us
  transfers between devices with their start and end apart: 16, of which 8 were waited for; matrix products, arithmetic and copies ran while one was open for 0% of the time, Pallas kernels for 11%

profile of v2, /device:TPU:0, one launch (start us, length us, event | category | flops | bytes accessed | tf_op | source)
XLA Modules:
  0.0 43.8 jit_solution(10596916060991583248)
XLA Ops:
  0.6 0.9 %copy-done.2 = bf16[128,1024]{1,0:T(8,128)(2,1)S(1)} copy-done((bf16[128,1024]{1,0:T(8,128)(2,1)S(1)}, bf16[128,1024]{1,0:T(8,128)(2,1)}, u32[]{:S(2)}) %copy-start.2) | copy-done | bytes 262168
  1.6 2.5 %collective-permute-start.4 = (bf16[128,512]{1,0:T(8,128)(2,1)S(1)}, bf16[128,512]{1,0:T(8,128)(2,1)S(1)}, u32[]{:S(2)}, u32[]{:S(2)}) collective-permute-start(bf16[128,512]{1,0:T(8,128)(2,1)S(1)} %get-tuple-element.33), channel_id=1, source_target_pairs={{0,3},{1,2},{2,5},{3,4},{4,7},{5,6},{6,9},{7,8},{8,11},{9,10},{10,... | collective-permute-start | bytes 393224 | tf_op jit(solution)/shard_map/ppermute | solution.py:228
  4.1 0.7 %collective-permute-start.2 = (bf16[128,512]{1,0:T(8,128)(2,1)S(1)}, bf16[128,512]{1,0:T(8,128)(2,1)S(1)}, u32[]{:S(2)}, u32[]{:S(2)}) collective-permute-start(bf16[128,512]{1,0:T(8,128)(2,1)S(1)} %get-tuple-element.33), channel_id=1, source_target_pairs={{0,1},{1,0},{2,3},{3,2},{4,5},{5,4},{6,7},{7,6},{8,9},{9,8},{10,11... | collective-permute-start | bytes 393224 | tf_op jit(solution)/shard_map/ppermute | solution.py:228
  4.8 1.5 %collective-permute-start.3 = (bf16[128,512]{1,0:T(8,128)(2,1)S(1)}, bf16[128,512]{1,0:T(8,128)(2,1)S(1)}, u32[]{:S(2)}, u32[]{:S(2)}) collective-permute-start(bf16[128,512]{1,0:T(8,128)(2,1)S(1)} %get-tuple-element.32.km), channel_id=1, source_target_pairs={{0,2},{1,3},{2,4},{3,5},{4,6},{5,7},{6,8},{7,9},{8,10},{9,11},{10,... | collective-permute-start | bytes 393224 | tf_op jit(solution)/shard_map/ppermute | solution.py:228
  6.5 0.5 %collective-permute-start.1 = (bf16[128,1024]{1,0:T(8,128)(2,1)S(1)}, bf16[128,1024]{1,0:T(8,128)(2,1)S(1)}, u32[]{:S(2)}, u32[]{:S(2)}) collective-permute-start(bf16[128,1024]{1,0:T(8,128)(2,1)S(1)} %get-tuple-element.31), channel_id=1, source_target_pairs={{0,1},{1,0},{2,3},{3,2},{4,5},{5,4},{6,7},{7,6},{8,9},{9,8},{10,11... | collective-permute-start | bytes 786440 | tf_op jit(solution)/shard_map/ppermute | solution.py:228
  7.2 4.0 %collective-permute-done.4.k2o = bf16[128,512]{1,0:T(8,128)(2,1)S(1)} collective-permute-done((bf16[128,512]{1,0:T(8,128)(2,1)S(1)}, bf16[128,512]{1,0:T(8,128)(2,1)S(1)}, u32[]{:S(2)}, u32[]{:S(2)}) %collective-permute-start.4) | collective-permute-done | bytes 131104 | tf_op jit(solution)/shard_map/ppermute | solution.py:228
  11.3 1.5 %collective-permute-start.5 = (bf16[128,512]{1,0:T(8,128)(2,1)S(1)}, bf16[128,512]{1,0:T(8,128)(2,1)S(1)}, u32[]{:S(2)}, u32[]{:S(2)}) collective-permute-start(bf16[128,512]{1,0:T(8,128)(2,1)S(1)} %get-tuple-element.36), channel_id=1, source_target_pairs={{0,1},{1,0},{2,3},{3,2},{4,5},{5,4},{6,7},{7,6},{8,9},{9,8},{10,11... | collective-permute-start | bytes 393224 | tf_op jit(solution)/shard_map/ppermute | solution.py:228
  12.8 2.1 %collective-permute-done.3.k2m = bf16[128,512]{1,0:T(8,128)(2,1)S(1)} collective-permute-done((bf16[128,512]{1,0:T(8,128)(2,1)S(1)}, bf16[128,512]{1,0:T(8,128)(2,1)S(1)}, u32[]{:S(2)}, u32[]{:S(2)}) %collective-permute-start.3) | collective-permute-done | bytes 131104 | tf_op jit(solution)/shard_map/ppermute | solution.py:228
  14.9 2.8 %value_grads.1 = (bf16[8,384,256]{2,1,0:T(8,128)(2,1)S(1)}, bf16[128,512]{1,0:T(8,128)(2,1)S(1)}, bf16[128,512]{1,0:T(8,128)(2,1)S(1)}) custom-call(s32[1]{0:T(128)} %bitcast.rank_ref, f32[2,384,128]{2,1,0:T(8,128)S(1)} %bias.1.bias_ref, bf16[128,1024]{1,0:T(8,128)(2,1)S(1)} %get-tuple-element.28.qm, bf16[128,1024]{1,0:T(8,128)(2,1)S(1)} %collective-permute-done.qo, ...), custom_call_target="tpu_custom_call" | custom-call | flops 5000000000 | bytes 1 | tf_op jit(solution)/shard_map/value_grads/pallas_call | solution.py:204
  17.7 1.6 %collective-permute-done.7.v2o = bf16[128,512]{1,0:T(8,128)(2,1)S(1)} collective-permute-done((bf16[128,512]{1,0:T(8,128)(2,1)S(1)}, bf16[128,512]{1,0:T(8,128)(2,1)S(1)}, u32[]{:S(2)}, u32[]{:S(2)}) %collective-permute-start.7) | collective-permute-done | bytes 131104 | tf_op jit(solution)/shard_map/ppermute | solution.py:228
  19.2 4.5 %collective-permute-done.6.v2m = bf16[128,512]{1,0:T(8,128)(2,1)S(1)} collective-permute-done((bf16[128,512]{1,0:T(8,128)(2,1)S(1)}, bf16[128,512]{1,0:T(8,128)(2,1)S(1)}, u32[]{:S(2)}, u32[]{:S(2)}) %collective-permute-start.6) | collective-permute-done | bytes 131104 | tf_op jit(solution)/shard_map/ppermute | solution.py:228
  23.7 2.4 %key_grads.1 = (bf16[8,384,256]{2,1,0:T(8,128)(2,1)S(1)}, bf16[128,512]{1,0:T(8,128)(2,1)S(1)}, bf16[128,512]{1,0:T(8,128)(2,1)S(1)}) custom-call(s32[1]{0:T(128)} %bitcast.rank_ref, bf16[8,384,256]{2,1,0:T(8,128)(2,1)S(1)} %get-tuple-element.34.prob_ref, bf16[128,1024]{1,0:T(8,128)(2,1)S(1)} %get-tuple-element.28.qm, ...), custom_call_target="tpu_custom_call" | custom-call | flops 5000000000 | bytes 1 | tf_op jit(solution)/shard_map/key_grads/pallas_call | solution.py:204
  26.1 1.6 %other_grads.1 = (bf16[128,1024]{1,0:T(8,128)(2,1)S(1)}, bf16[128,1024]{1,0:T(8,128)(2,1)S(1)}, f32[128,1024]{1,0:T(8,128)S(1)}, f32[128,1024]{1,0:T(8,128)S(1)}...) custom-call(s32[1]{0:T(128)} %bitcast.rank_ref, ...), custom_call_target="tpu_custom_call" | custom-call | flops 5000000000 | bytes 1 | tf_op jit(solution)/shard_map/other_grads/pallas_call | solution.py:204
  28.0 1.2 %collective-permute-start.12 = (bf16[128,512]{1,0:T(8,128)(2,1)S(1)}, bf16[128,512]{1,0:T(8,128)(2,1)S(1)}, u32[]{:S(2)}, u32[]{:S(2)}) collective-permute-start(bf16[128,512]{1,0:T(8,128)(2,1)S(1)} %get-tuple-element.47), channel_id=1, source_target_pairs={{3,0},{2,1},{5,2},{4,3},{7,4},{6,5},{9,6},{8,7},{11,8},{10,9},{13,... | collective-permute-start | bytes 393224 | tf_op jit(solution)/shard_map/ppermute | solution.py:228
  29.2 0.3 collective-permute-start.14
  29.5 1.3 %collective-permute-start.15 = (bf16[128,512]{1,0:T(8,128)(2,1)S(1)}, bf16[128,512]{1,0:T(8,128)(2,1)S(1)}, u32[]{:S(2)}, u32[]{:S(2)}) collective-permute-start(bf16[128,512]{1,0:T(8,128)(2,1)S(1)} %get-tuple-element.51), channel_id=1, source_target_pairs={{3,0},{2,1},{5,2},{4,3},{7,4},{6,5},{9,6},{8,7},{11,8},{10,9},{13,... | collective-permute-start | bytes 393224 | tf_op jit(solution)/shard_map/ppermute | solution.py:228
  30.8 3.4 %collective-permute-done.11.backm = bf16[128,512]{1,0:T(8,128)(2,1)S(1)} collective-permute-done((bf16[128,512]{1,0:T(8,128)(2,1)S(1)}, bf16[128,512]{1,0:T(8,128)(2,1)S(1)}, u32[]{:S(2)}, u32[]{:S(2)}) %collective-permute-start.11) | collective-permute-done | bytes 131104 | tf_op jit(solution)/shard_map/ppermute | solution.py:228
  34.1 1.9 %collective-permute-done.12.backo = bf16[128,512]{1,0:T(8,128)(2,1)S(1)} collective-permute-done((bf16[128,512]{1,0:T(8,128)(2,1)S(1)}, bf16[128,512]{1,0:T(8,128)(2,1)S(1)}, u32[]{:S(2)}, u32[]{:S(2)}) %collective-permute-start.12) | collective-permute-done | bytes 131104 | tf_op jit(solution)/shard_map/ppermute | solution.py:228
  36.0 0.7 %collective-permute-start.13 = (f32[128,512]{1,0:T(8,128)S(1)}, f32[128,512]{1,0:T(8,128)S(1)}, u32[]{:S(2)}, u32[]{:S(2)}) collective-permute-start(f32[128,512]{1,0:T(8,128)S(1)} %get-tuple-element.49), channel_id=1, source_target_pairs={{0,1},{1,0},{2,3},{3,2},{4,5},{5,4},{6,7},{7,6},{8,9},{9,8},{10,11... | collective-permute-start | bytes 786440 | tf_op jit(solution)/shard_map/ppermute | solution.py:228
  36.8 0.8 %join_keys.1 = f32[128,1024]{1,0:T(8,128)} custom-call(s32[1]{0:T(128)} %bitcast.rank_ref, f32[128,512]{1,0:T(8,128)S(1)} %get-tuple-element.44.mine, f32[128,512]{1,0:T(8,128)S(1)} %collective-permute-done.10.other, bf16[128,512]{1,0:T(8,128)(2,1)S(1)} %collective-permute-done.11.backm, bf16[128,512]{1,0:T(8,128)(2,1)S(1)} %collective-permute-done.12.backo), custom_call_target="tpu_custom_call" | custom-call | flops 5000000000 | bytes 1 | tf_op jit(solution)/shard_map/join_keys/pallas_call | solution.py:204
  37.6 2.1 %collective-permute-done.14.backm = bf16[128,512]{1,0:T(8,128)(2,1)S(1)} collective-permute-done((bf16[128,512]{1,0:T(8,128)(2,1)S(1)}, bf16[128,512]{1,0:T(8,128)(2,1)S(1)}, u32[]{:S(2)}, u32[]{:S(2)}) %collective-permute-start.14) | collective-permute-done | bytes 131104 | tf_op jit(solution)/shard_map/ppermute | solution.py:228
  39.8 1.9 %collective-permute-done.15.backo = bf16[128,512]{1,0:T(8,128)(2,1)S(1)} collective-permute-done((bf16[128,512]{1,0:T(8,128)(2,1)S(1)}, bf16[128,512]{1,0:T(8,128)(2,1)S(1)}, u32[]{:S(2)}, u32[]{:S(2)}) %collective-permute-start.15) | collective-permute-done | bytes 131104 | tf_op jit(solution)/shard_map/ppermute | solution.py:228
  41.7 0.8 %join_values.1 = f32[128,1024]{1,0:T(8,128)} custom-call(s32[1]{0:T(128)} %bitcast.rank_ref, f32[128,512]{1,0:T(8,128)S(1)} %get-tuple-element.48.mine, f32[128,512]{1,0:T(8,128)S(1)} %collective-permute-done.13.other, bf16[128,512]{1,0:T(8,128)(2,1)S(1)} %collective-permute-done.14.backm, bf16[128,512]{1,0:T(8,128)(2,1)S(1)} %collective-permute-done.15.backo), custom_call_target="tpu_custom_call" | custom-call | flops 5000000000 | bytes 1 | tf_op jit(solution)/shard_map/join_values/pallas_call | solution.py:204
  42.5 1.3 %join_rows.1 = (bf16[128,2048]{1,0:T(8,128)(2,1)}, f32[128,2048]{1,0:T(8,128)}) custom-call(s32[1]{0:T(128)} %bitcast.rank_ref, bf16[128,1024]{1,0:T(8,128)(2,1)S(1)} %get-tuple-element.38.refs_0_, bf16[128,1024]{1,0:T(8,128)(2,1)S(1)} %collective-permute-done.8.refs_1_, f32[128,1024]{1,0:T(8,128)S(1)} %get-tuple-element.40.refs_2_, ...), custom_call_target="tpu_custom_call" | custom-call | flops 5000000000 | bytes 1 | tf_op jit(solution)/shard_map/join_rows/pallas_call | solution.py:204
  (28 shorter events, 0.8 us)
Async XLA Ops:
  0.6 1.0 %copy-start.2 = (bf16[128,1024]{1,0:T(8,128)(2,1)S(1)}, bf16[128,1024]{1,0:T(8,128)(2,1)}, u32[]{:S(2)}) copy-start(bf16[128,1024]{1,0:T(8,128)(2,1)} %refs_0_.4) | copy-start | bytes 786436
  1.6 4.7 %copy-start = (bf16[128,2048]{1,0:T(8,128)(2,1)S(1)}, bf16[128,2048]{1,0:T(8,128)(2,1)}, u32[]{:S(2)}) copy-start(bf16[128,2048]{1,0:T(8,128)(2,1)} %refs_0_.3) | copy-start | bytes 1572868
  1.6 4.7 %copy-start.1 = (bf16[128,2048]{1,0:T(8,128)(2,1)S(1)}, bf16[128,2048]{1,0:T(8,128)(2,1)}, u32[]{:S(2)}) copy-start(bf16[128,2048]{1,0:T(8,128)(2,1)} %refs_1_.1) | copy-start | bytes 1572868
  1.6 9.6 %collective-permute-start.4 = (bf16[128,512]{1,0:T(8,128)(2,1)S(1)}, bf16[128,512]{1,0:T(8,128)(2,1)S(1)}, u32[]{:S(2)}, u32[]{:S(2)}) collective-permute-start(bf16[128,512]{1,0:T(8,128)(2,1)S(1)} %get-tuple-element.33), channel_id=1, source_target_pairs={{0,3},{1,2},{2,5},{3,4},{4,7},{5,6},{6,9},{7,8},{8,11},{9,10},{10,... | collective-permute-start | bytes 393224 | tf_op jit(solution)/shard_map/ppermute | solution.py:228
  4.1 7.2 %collective-permute-start.2 = (bf16[128,512]{1,0:T(8,128)(2,1)S(1)}, bf16[128,512]{1,0:T(8,128)(2,1)S(1)}, u32[]{:S(2)}, u32[]{:S(2)}) collective-permute-start(bf16[128,512]{1,0:T(8,128)(2,1)S(1)} %get-tuple-element.33), channel_id=1, source_target_pairs={{0,1},{1,0},{2,3},{3,2},{4,5},{5,4},{6,7},{7,6},{8,9},{9,8},{10,11... | collective-permute-start | bytes 393224 | tf_op jit(solution)/shard_map/ppermute | solution.py:228
  4.8 2.2 %copy-start.3 = (bf16[128,1024]{1,0:T(8,128)(2,1)S(1)}, bf16[128,1024]{1,0:T(8,128)(2,1)}, u32[]{:S(2)}) copy-start(bf16[128,1024]{1,0:T(8,128)(2,1)} %refs_0_.5) | copy-start | bytes 786436
  4.8 10.1 %collective-permute-start.3 = (bf16[128,512]{1,0:T(8,128)(2,1)S(1)}, bf16[128,512]{1,0:T(8,128)(2,1)S(1)}, u32[]{:S(2)}, u32[]{:S(2)}) collective-permute-start(bf16[128,512]{1,0:T(8,128)(2,1)S(1)} %get-tuple-element.32.km), channel_id=1, source_target_pairs={{0,2},{1,3},{2,4},{3,5},{4,6},{5,7},{6,8},{7,9},{8,10},{9,11},{10,... | collective-permute-start | bytes 393224 | tf_op jit(solution)/shard_map/ppermute | solution.py:228
  6.4 8.5 %collective-permute-start = (bf16[128,1024]{1,0:T(8,128)(2,1)S(1)}, bf16[128,1024]{1,0:T(8,128)(2,1)S(1)}, u32[]{:S(2)}, u32[]{:S(2)}) collective-permute-start(bf16[128,1024]{1,0:T(8,128)(2,1)S(1)} %get-tuple-element.29), channel_id=1, source_target_pairs={{0,1},{1,0},{2,3},{3,2},{4,5},{5,4},{6,7},{7,6},{8,9},{9,8},{10,11... | collective-permute-start | bytes 786440 | tf_op jit(solution)/shard_map/ppermute | solution.py:228
  6.4 0.7 %copy-start.4 = (s32[32]{0:T(128)S(1)}, s32[32]{0:T(128)}, u32[]{:S(2)}) copy-start(s32[32]{0:T(128)} %param.9) | copy-start | bytes 388
  6.5 8.5 %collective-permute-start.1 = (bf16[128,1024]{1,0:T(8,128)(2,1)S(1)}, bf16[128,1024]{1,0:T(8,128)(2,1)S(1)}, u32[]{:S(2)}, u32[]{:S(2)}) collective-permute-start(bf16[128,1024]{1,0:T(8,128)(2,1)S(1)} %get-tuple-element.31), channel_id=1, source_target_pairs={{0,1},{1,0},{2,3},{3,2},{4,5},{5,4},{6,7},{7,6},{8,9},{9,8},{10,11... | collective-permute-start | bytes 786440 | tf_op jit(solution)/shard_map/ppermute | solution.py:228
  11.3 8.0 %collective-permute-start.7 = (bf16[128,512]{1,0:T(8,128)(2,1)S(1)}, bf16[128,512]{1,0:T(8,128)(2,1)S(1)}, u32[]{:S(2)}, u32[]{:S(2)}) collective-permute-start(bf16[128,512]{1,0:T(8,128)(2,1)S(1)} %get-tuple-element.36), channel_id=1, source_target_pairs={{0,3},{1,2},{2,5},{3,4},{4,7},{5,6},{6,9},{7,8},{8,11},{9,10},{10,... | collective-permute-start | bytes 393224 | tf_op jit(solution)/shard_map/ppermute | solution.py:228
  11.3 8.0 %collective-permute-start.5 = (bf16[128,512]{1,0:T(8,128)(2,1)S(1)}, bf16[128,512]{1,0:T(8,128)(2,1)S(1)}, u32[]{:S(2)}, u32[]{:S(2)}) collective-permute-start(bf16[128,512]{1,0:T(8,128)(2,1)S(1)} %get-tuple-element.36), channel_id=1, source_target_pairs={{0,1},{1,0},{2,3},{3,2},{4,5},{5,4},{6,7},{7,6},{8,9},{9,8},{10,11... | collective-permute-start | bytes 393224 | tf_op jit(solution)/shard_map/ppermute | solution.py:228
  14.9 8.8 %collective-permute-start.6 = (bf16[128,512]{1,0:T(8,128)(2,1)S(1)}, bf16[128,512]{1,0:T(8,128)(2,1)S(1)}, u32[]{:S(2)}, u32[]{:S(2)}) collective-permute-start(bf16[128,512]{1,0:T(8,128)(2,1)S(1)} %get-tuple-element.35.vm), channel_id=1, source_target_pairs={{0,2},{1,3},{2,4},{3,5},{4,6},{5,7},{6,8},{7,9},{8,10},{9,11},{10,... | collective-permute-start | bytes 393224 | tf_op jit(solution)/shard_map/ppermute | solution.py:228
  27.7 9.1 %collective-permute-start.10 = (f32[128,512]{1,0:T(8,128)S(1)}, f32[128,512]{1,0:T(8,128)S(1)}, u32[]{:S(2)}, u32[]{:S(2)}) collective-permute-start(f32[128,512]{1,0:T(8,128)S(1)} %get-tuple-element.45), channel_id=1, source_target_pairs={{0,1},{1,0},{2,3},{3,2},{4,5},{5,4},{6,7},{7,6},{8,9},{9,8},{10,11... | collective-permute-start | bytes 786440 | tf_op jit(solution)/shard_map/ppermute | solution.py:228
  27.8 6.3 %collective-permute-start.11 = (bf16[128,512]{1,0:T(8,128)(2,1)S(1)}, bf16[128,512]{1,0:T(8,128)(2,1)S(1)}, u32[]{:S(2)}, u32[]{:S(2)}) collective-permute-start(bf16[128,512]{1,0:T(8,128)(2,1)S(1)} %get-tuple-element.46), channel_id=1, source_target_pairs={{2,0},{3,1},{4,2},{5,3},{6,4},{7,5},{8,6},{9,7},{10,8},{11,9},{12,... | collective-permute-start | bytes 393224 | tf_op jit(solution)/shard_map/ppermute | solution.py:228
  28.0 8.0 %collective-permute-start.12 = (bf16[128,512]{1,0:T(8,128)(2,1)S(1)}, bf16[128,512]{1,0:T(8,128)(2,1)S(1)}, u32[]{:S(2)}, u32[]{:S(2)}) collective-permute-start(bf16[128,512]{1,0:T(8,128)(2,1)S(1)} %get-tuple-element.47), channel_id=1, source_target_pairs={{3,0},{2,1},{5,2},{4,3},{7,4},{6,5},{9,6},{8,7},{11,8},{10,9},{13,... | collective-permute-start | bytes 393224 | tf_op jit(solution)/shard_map/ppermute | solution.py:228
  29.2 10.6 %collective-permute-start.14 = (bf16[128,512]{1,0:T(8,128)(2,1)S(1)}, bf16[128,512]{1,0:T(8,128)(2,1)S(1)}, u32[]{:S(2)}, u32[]{:S(2)}) collective-permute-start(bf16[128,512]{1,0:T(8,128)(2,1)S(1)} %get-tuple-element.50), channel_id=1, source_target_pairs={{2,0},{3,1},{4,2},{5,3},{6,4},{7,5},{8,6},{9,7},{10,8},{11,9},{12,... | collective-permute-start | bytes 393224 | tf_op jit(solution)/shard_map/ppermute | solution.py:228
  29.5 12.2 %collective-permute-start.15 = (bf16[128,512]{1,0:T(8,128)(2,1)S(1)}, bf16[128,512]{1,0:T(8,128)(2,1)S(1)}, u32[]{:S(2)}, u32[]{:S(2)}) collective-permute-start(bf16[128,512]{1,0:T(8,128)(2,1)S(1)} %get-tuple-element.51), channel_id=1, source_target_pairs={{3,0},{2,1},{5,2},{4,3},{7,4},{6,5},{9,6},{8,7},{11,8},{10,9},{13,... | collective-permute-start | bytes 393224 | tf_op jit(solution)/shard_map/ppermute | solution.py:228
  34.1 8.4 %collective-permute-start.8 = (bf16[128,1024]{1,0:T(8,128)(2,1)S(1)}, bf16[128,1024]{1,0:T(8,128)(2,1)S(1)}, u32[]{:S(2)}, u32[]{:S(2)}) collective-permute-start(bf16[128,1024]{1,0:T(8,128)(2,1)S(1)} %get-tuple-element.39), channel_id=1, source_target_pairs={{0,1},{1,0},{2,3},{3,2},{4,5},{5,4},{6,7},{7,6},{8,9},{9,8},{10,11... | collective-permute-start | bytes 786440 | tf_op jit(solution)/shard_map/ppermute | solution.py:228
  36.0 5.6 %collective-permute-start.13 = (f32[128,512]{1,0:T(8,128)S(1)}, f32[128,512]{1,0:T(8,128)S(1)}, u32[]{:S(2)}, u32[]{:S(2)}) collective-permute-start(f32[128,512]{1,0:T(8,128)S(1)} %get-tuple-element.49), channel_id=1, source_target_pairs={{0,1},{1,0},{2,3},{3,2},{4,5},{5,4},{6,7},{7,6},{8,9},{9,8},{10,11... | collective-permute-start | bytes 786440 | tf_op jit(solution)/shard_map/ppermute | solution.py:228
  36.8 5.7 %collective-permute-start.9 = (f32[128,1024]{1,0:T(8,128)S(1)}, f32[128,1024]{1,0:T(8,128)S(1)}, u32[]{:S(2)}, u32[]{:S(2)}) collective-permute-start(f32[128,1024]{1,0:T(8,128)S(1)} %get-tuple-element.41), channel_id=1, source_target_pairs={{0,1},{1,0},{2,3},{3,2},{4,5},{5,4},{6,7},{7,6},{8,9},{9,8},{10,11... | collective-permute-start | bytes 1572872 | tf_op jit(solution)/shard_map/ppermute | solution.py:228

commit v3 on v2

v3 whole, which is shorter than its diff:
```python
import functools

import jax
import jax.numpy as jnp
from jax import lax
from jax.experimental import pallas as pl
from jax.experimental.pallas import tpu as pltpu
from jax.sharding import PartitionSpec as P

QUERY_HEADS = 16
KEY_VALUE_HEADS = 8
HEAD_SIZE = 128
LOCAL_WINDOW = 256
GROUP = QUERY_HEADS // KEY_VALUE_HEADS
CORES = 2
CORE_HEADS = KEY_VALUE_HEADS // CORES
CORE_QUERIES = QUERY_HEADS // CORES
AT_GRADIENTS = CORE_QUERIES
AT_KEYS = 2 * CORE_QUERIES
AT_VALUES = AT_KEYS + CORE_HEADS
ALL_SENT = AT_VALUES + CORE_HEADS
AXES = ("dp", "seq")

score_scale = 168.0 ** (-0.5)
LOG2E = 1.4426950408889634
NEGATIVE = -1e30

CONTRACT_LAST = (((1,), (1,)), ((), ()))
CONTRACT_FIRST = (((0,), (0,)), ((), ()))


COST = {"far_keys": 20000, "own_values": 20000}


def dot(a, b):
    return jnp.dot(a, b, preferred_element_type=jnp.float32)


def dot_last(a, b):
    return lax.dot_general(a, b, CONTRACT_LAST, preferred_element_type=jnp.float32)


def dot_first(a, b):
    return lax.dot_general(a, b, CONTRACT_FIRST, preferred_element_type=jnp.float32)


def span(head):
    return slice(head * HEAD_SIZE, (head + 1) * HEAD_SIZE)


def both(odd, mine, other, head, offset=0):
    a, b = mine[:, span(head)], other[:, span(offset + head)]
    return jnp.where(odd, b, a), jnp.where(odd, a, b)


def stacked(odd, mine, other, head, offset):
    pieces = [both(odd, mine, other, head * GROUP + j, offset) for j in range(GROUP)]
    return [jnp.concatenate([piece[block] for piece in pieces], axis=0) for block in range(CORES)]


def put(odd, mine, other, head, first, second, offset=0):
    mine[:, span(head)] = jnp.where(odd, second, first).astype(mine.dtype)
    other[:, span(offset + head)] = jnp.where(odd, first, second).astype(other.dtype)


def split_kernel(rank_ref, source, mine, other):
    odd = rank_ref[0] % 2
    width = source.shape[1] // CORES
    for core in range(CORES):

        @pl.when(odd == core)
        def _():
            mine[...] = source[:, core * width : (core + 1) * width]
            other[...] = source[:, (1 - core) * width : (2 - core) * width]


def rows_kernel(rank_ref, q_ref, g_ref, v_ref, kx, qm, gm, vm, vx, sent):
    odd = rank_ref[0] % 2
    wide, narrow = qm.shape[1], vm.shape[1]
    at_keys, at_values = AT_KEYS * HEAD_SIZE, AT_VALUES * HEAD_SIZE
    for core in range(CORES):
        here = slice(core * wide, (core + 1) * wide)
        there = slice((1 - core) * wide, (2 - core) * wide)

        @pl.when(odd == core)
        def _():
            qm[...] = q_ref[:, here]
            gm[...] = g_ref[:, here]
            sent[:, :wide] = q_ref[:, there]
            sent[:, wide : 2 * wide] = g_ref[:, there]
            vm[...] = v_ref[:, core * narrow : (core + 1) * narrow]
            vx[...] = v_ref[:, (1 - core) * narrow : (2 - core) * narrow]
            sent[:, at_values:] = v_ref[:, (1 - core) * narrow : (2 - core) * narrow]

    sent[:, at_keys:at_values] = kx[...]


def bias_kernel(rank_ref, lens_ref, bias_ref):
    _, span_rows, rows = bias_ref.shape
    docs = lens_ref.shape[1]
    later = lax.broadcasted_iota(jnp.int32, (docs, docs), 0)
    earlier = lax.broadcasted_iota(jnp.int32, (docs, docs), 1)
    lens = jnp.broadcast_to(lens_ref[...].astype(jnp.float32), (docs, docs))
    ends = jnp.sum(jnp.where(earlier <= later, lens, 0.0), axis=1, keepdims=True)
    for block in range(CORES):
        first = (rank_ref[0] // CORES * CORES + block) * rows
        query = first + lax.broadcasted_iota(jnp.int32, (1, rows), 1)
        ended = jnp.where(ends <= query.astype(jnp.float32), ends, 0.0)
        start = jnp.max(ended, axis=0, keepdims=True).astype(jnp.int32)
        lowest = jnp.maximum(start, query - (LOCAL_WINDOW - 1))
        key = first - 2 * rows + lax.broadcasted_iota(jnp.int32, (span_rows, rows), 0)
        bias_ref[block] = jnp.where((key >= lowest) & (key <= query), 0.0, NEGATIVE)


def order_kernel(rank_ref, mine, other, first, second):
    odd = rank_ref[0] % 2
    for core in range(CORES):

        @pl.when(odd == core)
        def _():
            (second if core else first)[...] = mine[...]
            (first if core else second)[...] = other[...]


def value_kernel(
    rank_ref, bias_ref, qm, gm, km, near, ka, kb,
    prob_ref, dvm, dvo,
):
    rows = qm.shape[0]
    odd = rank_ref[0] % 2 == 1
    for head in range(CORE_HEADS):
        blocks = (ka[:, span(head)], kb[:, span(head)]) + both(odd, km, near, head, AT_KEYS)
        queries = stacked(odd, qm, near, head, 0)
        gradients = stacked(odd, gm, near, head, AT_GRADIENTS)
        grads = []
        for block in range(CORES):
            keys = jnp.concatenate(blocks[block : block + 3], axis=0)
            bias = jnp.concatenate([bias_ref[block]] * GROUP, axis=1)
            scores = dot_last(keys, queries[block]) * (score_scale * LOG2E) + bias
            top = jnp.max(scores, axis=0, keepdims=True)
            raised = jnp.exp2(scores - top)
            total = jnp.sum(raised, axis=0, keepdims=True)
            prob = (raised * (1.0 / total)).astype(jnp.bfloat16)
            prob_ref[head * CORES + block] = prob
            grads.append(dot(prob[: (2 - block) * rows], gradients[block]))
        put(odd, dvm, dvo, head, grads[0][:rows], grads[0][rows:] + grads[1])


def local_sum(core, pairs_ref, sources, head, rows):
    at = head * CORES + core
    total = dot(pairs_ref[at, 2 * rows :], sources[core])
    if core == 0:
        total += dot(pairs_ref[at + 1, rows : 2 * rows], sources[1])
    return total


def local_grads(core, prob_ref, dscore_ref, keys, values, queries, head, rows):
    at = head * CORES + core
    out = dot_first(prob_ref[at], jnp.concatenate(values[core : core + 3], axis=0))
    dq = dot_first(dscore_ref[at], jnp.concatenate(keys[core : core + 3], axis=0))
    dk = local_sum(core, dscore_ref, queries, head, rows)
    return out, dq, dk


def key_kernel(
    rank_ref, prob_ref, qm, gm, km, vm, near, ka, kb, v2m, v2o,
    dscore_ref, dkm, dko, sent,
):
    rows = qm.shape[0]
    odd = rank_ref[0] % 2 == 1
    for head in range(CORE_HEADS):
        values = both(odd, v2m, v2o, head) + both(odd, vm, near, head, AT_VALUES)
        queries = stacked(odd, qm, near, head, 0)
        gradients = stacked(odd, gm, near, head, AT_GRADIENTS)
        grads = []
        for block in range(CORES):
            dprob = dot_last(jnp.concatenate(values[block : block + 3], axis=0), gradients[block])
            prob = prob_ref[head * CORES + block].astype(jnp.float32)
            delta = jnp.sum(prob * dprob, axis=0, keepdims=True)
            dscore = (prob * ((dprob - delta) * score_scale)).astype(jnp.bfloat16)
            dscore_ref[head * CORES + block] = dscore
            grads.append(dot(dscore[: (2 - block) * rows], queries[block]))
        put(odd, dkm, dko, head, grads[0][:rows], grads[0][rows:] + grads[1])
    for core in range(CORES):

        @pl.when(rank_ref[0] % 2 != core)
        def _():
            for head in range(CORE_HEADS):
                keys = (ka[:, span(head)], kb[:, span(head)]) + both(odd, km, near, head, AT_KEYS)
                values = both(odd, v2m, v2o, head) + both(odd, vm, near, head, AT_VALUES)
                queries = stacked(odd, qm, near, head, 0)
                gradients = stacked(odd, gm, near, head, AT_GRADIENTS)
                out, dq, dk = local_grads(core, prob_ref, dscore_ref, keys, values, queries, head, rows)
                for j in range(GROUP):
                    at = slice(j * rows, (j + 1) * rows)
                    sent[:, span(head * GROUP + j)] = out[at].astype(jnp.bfloat16)
                    sent[:, span(AT_GRADIENTS + head * GROUP + j)] = dq[at].astype(jnp.bfloat16)
                sent[:, span(AT_KEYS + head)] = dk.astype(jnp.bfloat16)
                dv = local_sum(core, prob_ref, gradients, head, rows)
                sent[:, span(AT_VALUES + head)] = dv.astype(jnp.bfloat16)


def own_values_kernel(rank_ref, prob_ref, gm, near, backm, dvm):
    rows = gm.shape[0]
    odd = rank_ref[0] % 2 == 1
    for core in range(CORES):

        @pl.when(rank_ref[0] % 2 == core)
        def _():
            for head in range(CORE_HEADS):
                gradients = stacked(odd, gm, near, head, AT_GRADIENTS)
                dv = local_sum(core, prob_ref, gradients, head, rows)
                dvm[:, span(head)] = dv + backm[:, span(head)].astype(jnp.float32)


def rows_grads_kernel(
    rank_ref, prob_ref, dscore_ref, qm, gm, km, vm, near, ka, kb, v2m, v2o, got, dvm, backo,
    out_ref, dq_ref, dkm, dv_ref,
):
    rows = qm.shape[0]
    odd = rank_ref[0] % 2 == 1
    wide, narrow = qm.shape[1], km.shape[1]
    for core in range(CORES):

        @pl.when(rank_ref[0] % 2 == core)
        def _():
            there = slice((1 - core) * wide, (2 - core) * wide)
            out_ref[:, there] = got[:, :wide]
            dq_ref[:, there] = got[:, wide : 2 * wide].astype(jnp.float32)
            dv_ref[:, core * narrow : (core + 1) * narrow] = dvm[...]
            dv_ref[:, (1 - core) * narrow : (2 - core) * narrow] = backo[...].astype(jnp.float32) + got[
                :, AT_VALUES * HEAD_SIZE :
            ].astype(jnp.float32)
            for head in range(CORE_HEADS):
                keys = (ka[:, span(head)], kb[:, span(head)]) + both(odd, km, near, head, AT_KEYS)
                values = both(odd, v2m, v2o, head) + both(odd, vm, near, head, AT_VALUES)
                queries = stacked(odd, qm, near, head, 0)
                out, dq, dk = local_grads(core, prob_ref, dscore_ref, keys, values, queries, head, rows)
                for j in range(GROUP):
                    at = slice(j * rows, (j + 1) * rows)
                    here = span(core * CORE_QUERIES + head * GROUP + j)
                    out_ref[:, here] = out[at].astype(jnp.bfloat16)
                    dq_ref[:, here] = dq[at]
                dkm[:, span(head)] = dk


def add_kernel(offset, rank_ref, mine, near, backm, backo, target):
    odd = rank_ref[0] % 2
    width = mine.shape[1]
    offset = offset * HEAD_SIZE
    for core in range(CORES):
        here = slice(core * width, (core + 1) * width)
        there = slice((1 - core) * width, (2 - core) * width)

        @pl.when(odd == core)
        def _():
            target[:, here] = mine[...] + backm[...].astype(jnp.float32)
            target[:, there] = near[:, offset : offset + width].astype(jnp.float32) + backo[...].astype(jnp.float32)


def shape(dims, dtype):
    return jax.ShapeDtypeStruct(dims, dtype)


def run(kernel, name, outputs, index, *operands):
    small = pl.BlockSpec(memory_space=pltpu.SMEM)
    whole = pl.BlockSpec(memory_space=pltpu.VMEM)
    return pl.pallas_call(
        kernel,
        in_specs=[small] + [whole] * len(operands),
        out_specs=[whole] * len(outputs),
        out_shape=outputs,
        compiler_params=pltpu.CompilerParams(vmem_limit_bytes=40 * 2**20),
        cost_estimate=pl.CostEstimate(flops=COST.get(name, 0) * 1000000, bytes_accessed=1000, transcendentals=0),
        name=name,
    )(index, *operands)


def on_device(queries, keys, values, output_gradient, doc_lengths):
    rows = queries.shape[0]
    devices = lax.axis_size(AXES)
    index = lax.axis_index(AXES).reshape(1)
    docs = doc_lengths.shape[0]

    ahead = [(r, (r + 2) % devices) for r in range(devices)]
    across = [(r, ((r + 2) % devices) ^ 1) for r in range(devices)]
    behind = [(there, here) for here, there in ahead]
    recross = [(there, here) for here, there in across]
    swap = [(r, r ^ 1) for r in range(devices)]

    def moved(value, pairs):
        return lax.ppermute(value, AXES, pairs)

    narrow = shape((rows, keys.shape[1] // CORES), jnp.bfloat16)
    wide = shape((rows, queries.shape[1] // CORES), jnp.bfloat16)
    narrow_sum = shape(narrow.shape, jnp.float32)
    wide_sum = shape(wide.shape, jnp.float32)
    pairs = shape((KEY_VALUE_HEADS, 3 * rows, GROUP * rows), jnp.bfloat16)

    full = shape(keys.shape, jnp.float32)
    all_sent = shape((rows, ALL_SENT * HEAD_SIZE), jnp.bfloat16)
    km, kx = run(split_kernel, "split_keys", [narrow] * 2, index, keys)
    k2m, k2o = moved(km, ahead), moved(kx, across)
    qm, gm, vm, vx, sent = run(
        rows_kernel, "split_rows", [wide, wide, narrow, narrow, all_sent],
        index, queries, output_gradient, values, kx,
    )
    v2m, v2o = moved(vm, ahead), moved(vx, across)
    near = moved(sent, swap)
    (bias,) = run(
        bias_kernel, "bias", [shape((CORES, 3 * rows, rows), jnp.float32)],
        index, doc_lengths.reshape(1, docs),
    )
    ka, kb = run(order_kernel, "far_keys", [narrow] * 2, index, k2m, k2o)
    prob, dvm, dvo = run(
        value_kernel, "value_grads", [pairs, narrow, narrow],
        index, bias, qm, gm, km, near, ka, kb,
    )
    dv_back = moved(dvm, behind), moved(dvo, recross)
    dscore, dkm, dko, sent = run(
        key_kernel, "key_grads", [pairs, narrow, narrow, all_sent],
        index, prob, qm, gm, km, vm, near, ka, kb, v2m, v2o,
    )
    dk_back = moved(dkm, behind), moved(dko, recross)
    got = moved(sent, swap)
    (dvm,) = run(
        own_values_kernel, "own_values", [narrow_sum], index, prob, gm, near, dv_back[0]
    )
    got, dvm = lax.optimization_barrier((got, dvm))
    attended, dq, dkm, dv = run(
        rows_grads_kernel, "other_grads",
        [shape(queries.shape, jnp.bfloat16), shape(queries.shape, jnp.float32), narrow_sum, full],
        index, prob, dscore, qm, gm, km, vm, near, ka, kb, v2m, v2o, got, dvm, dv_back[1],
    )
    (dk,) = run(functools.partial(add_kernel, AT_KEYS), "join_keys", [full], index, dkm, got, *dk_back)
    return attended, dq, dk, dv


def solution(mesh):
    split = P(AXES, None)
    return jax.shard_map(
        on_device,
        mesh=mesh,
        in_specs=(split, split, split, split, P()),
        out_specs=(split, split, split, split),
        check_vma=False,
    )
```

time: 43.9 us -> 34 us (0.77)
  waiting for transfers between devices: 21.5 us -> 5.93 us
  starting transfers between devices: 10.5 us -> 13.7 us
  local copies, waits for them, and re-layouts: 1.09 us -> 3.98 us
  Pallas kernels: 9.91 us -> 9.46 us
    ppermute x16 -> x10, waiting for transfers between devices: 21.5 us -> 5.93 us  [moved(): return lax.ppermute(value, AXES, pairs)]
    ppermute x16 -> x10, starting transfers between devices: 10.5 us -> 13.7 us  [moved(): return lax.ppermute(value, AXES, pairs)]
    unnamed x10, local copies, waits for them, and re-layouts: 1.09 us -> 3.98 us
    pallas_call x10 -> x9, Pallas kernels: 9.91 us -> 9.46 us  [run(): pl.pallas_call(kernel, in_specs=[small] + [whole] * len(operands), out_sp...]
  transfers between devices with their start and end apart: 16 -> 10, of which waited for: 8 -> 4; matrix products, arithmetic and copies ran while one was open for 0% -> 0% of each run, Pallas kernels for 11% -> 25%
where the time goes in v3:
time: 34 us; the launch traced here: 33.8 us
  starting transfers between devices  13.7 us (40%)
  Pallas kernels  9.46 us (28%)
  waiting for transfers between devices  5.93 us (17%)
  local copies, waits for them, and re-layouts  3.98 us (12%)
  between operations  0.73 us (2%)
    ppermute x10, starting transfers between devices, moved(): return lax.ppermute(value, AXES, pairs)  13.7 us
    pallas_call x9, Pallas kernels, run(): pl.pallas_call(kernel, in_specs=[small] + [whole] * len(operands), out_sp...  9.46 us
    ppermute x10, waiting for transfers between devices, moved(): return lax.ppermute(value, AXES, pairs)  5.93 us
    unnamed x10, local copies, waits for them, and re-layouts  3.98 us
  transfers between devices with their start and end apart: 10, of which 4 were waited for; matrix products, arithmetic and copies ran while one was open for 0% of the time, Pallas kernels for 25%

profile of v3, /device:TPU:0, one launch (start us, length us, event | category | flops | bytes accessed | tf_op | source)
XLA Modules:
  0.0 33.8 jit_solution(13694786094948628935)
XLA Ops:
  0.7 0.9 %copy-done.2 = bf16[128,1024]{1,0:T(8,128)(2,1)S(1)} copy-done((bf16[128,1024]{1,0:T(8,128)(2,1)S(1)}, bf16[128,1024]{1,0:T(8,128)(2,1)}, u32[]{:S(2)}) %copy-start.2) | copy-done | bytes 262168
  1.6 2.5 %collective-permute-start.2 = (bf16[128,512]{1,0:T(8,128)(2,1)S(1)}, bf16[128,512]{1,0:T(8,128)(2,1)S(1)}, u32[]{:S(2)}, u32[]{:S(2)}) collective-permute-start(bf16[128,512]{1,0:T(8,128)(2,1)S(1)} %get-tuple-element.26.kx), channel_id=1, source_target_pairs={{0,3},{1,2},{2,5},{3,4},{4,7},{5,6},{6,9},{7,8},{8,11},{9,10},{10,... | collective-permute-start | bytes 393224 | tf_op jit(solution)/shard_map/ppermute | solution.py:292
  4.1 1.5 %collective-permute-start.1 = (bf16[128,512]{1,0:T(8,128)(2,1)S(1)}, bf16[128,512]{1,0:T(8,128)(2,1)S(1)}, u32[]{:S(2)}, u32[]{:S(2)}) collective-permute-start(bf16[128,512]{1,0:T(8,128)(2,1)S(1)} %get-tuple-element.29.km), channel_id=1, source_target_pairs={{0,2},{1,3},{2,4},{3,5},{4,6},{5,7},{6,8},{7,9},{8,10},{9,11},{10,... | collective-permute-start | bytes 393224 | tf_op jit(solution)/shard_map/ppermute | solution.py:292
  5.6 1.0 %copy-done = bf16[128,2048]{1,0:T(8,128)(2,1)S(1)} copy-done((bf16[128,2048]{1,0:T(8,128)(2,1)S(1)}, bf16[128,2048]{1,0:T(8,128)(2,1)}, u32[]{:S(2)}) %copy-start) | copy-done | bytes 524312
  6.6 1.0 %copy-done.1 = bf16[128,2048]{1,0:T(8,128)(2,1)S(1)} copy-done((bf16[128,2048]{1,0:T(8,128)(2,1)S(1)}, bf16[128,2048]{1,0:T(8,128)(2,1)}, u32[]{:S(2)}) %copy-start.1) | copy-done | bytes 524312
  7.7 0.9 %copy-done.3 = bf16[128,1024]{1,0:T(8,128)(2,1)S(1)} copy-done((bf16[128,1024]{1,0:T(8,128)(2,1)S(1)}, bf16[128,1024]{1,0:T(8,128)(2,1)}, u32[]{:S(2)}) %copy-start.3) | copy-done | bytes 262168
  8.6 0.1 split_rows.1
  8.7 1.6 %collective-permute-start.4 = (bf16[128,512]{1,0:T(8,128)(2,1)S(1)}, bf16[128,512]{1,0:T(8,128)(2,1)S(1)}, u32[]{:S(2)}, u32[]{:S(2)}) collective-permute-start(bf16[128,512]{1,0:T(8,128)(2,1)S(1)} %get-tuple-element.35), channel_id=1, source_target_pairs={{0,3},{1,2},{2,5},{3,4},{4,7},{5,6},{6,9},{7,8},{8,11},{9,10},{10,... | collective-permute-start | bytes 393224 | tf_op jit(solution)/shard_map/ppermute | solution.py:292
  10.3 1.5 %collective-permute-start.3 = (bf16[128,512]{1,0:T(8,128)(2,1)S(1)}, bf16[128,512]{1,0:T(8,128)(2,1)S(1)}, u32[]{:S(2)}, u32[]{:S(2)}) collective-permute-start(bf16[128,512]{1,0:T(8,128)(2,1)S(1)} %get-tuple-element.34.vm), channel_id=1, source_target_pairs={{0,2},{1,3},{2,4},{3,5},{4,6},{5,7},{6,8},{7,9},{8,10},{9,11},{10,... | collective-permute-start | bytes 393224 | tf_op jit(solution)/shard_map/ppermute | solution.py:292
  11.8 0.0 collective-permute-start
  11.8 0.1 bias.1.bias_ref
  12.0 2.9 %collective-permute-done.1.mine = bf16[128,512]{1,0:T(8,128)(2,1)S(1)} collective-permute-done((bf16[128,512]{1,0:T(8,128)(2,1)S(1)}, bf16[128,512]{1,0:T(8,128)(2,1)S(1)}, u32[]{:S(2)}, u32[]{:S(2)}) %collective-permute-start.1) | collective-permute-done | bytes 131104 | tf_op jit(solution)/shard_map/ppermute | solution.py:292
  14.9 2.7 %value_grads.1 = (bf16[8,384,256]{2,1,0:T(8,128)(2,1)S(1)}, bf16[128,512]{1,0:T(8,128)(2,1)S(1)}, bf16[128,512]{1,0:T(8,128)(2,1)S(1)}) custom-call(s32[1]{0:T(128)} %bitcast.rank_ref, f32[2,384,128]{2,1,0:T(8,128)S(1)} %bias.1.bias_ref, bf16[128,1024]{1,0:T(8,128)(2,1)S(1)} %get-tuple-element.27.qm, bf16[128,1024]{1,0:T(8,128)(2,1)S(1)} %get-tuple-element.28.gm, ...), custom_call_target="tpu_custom_call" | custom-call | bytes 1000 | tf_op jit(solution)/shard_map/value_grads/pallas_call | solution.py:268
  17.7 3.3 %collective-permute-start.6 = (bf16[128,512]{1,0:T(8,128)(2,1)S(1)}, bf16[128,512]{1,0:T(8,128)(2,1)S(1)}, u32[]{:S(2)}, u32[]{:S(2)}) collective-permute-start(bf16[128,512]{1,0:T(8,128)(2,1)S(1)} %get-tuple-element.38), channel_id=1, source_target_pairs={{2,0},{3,1},{4,2},{5,3},{6,4},{7,5},{8,6},{9,7},{10,8},{11,9},{12,... | collective-permute-start | bytes 393224 | tf_op jit(solution)/shard_map/ppermute | solution.py:292
  21.0 0.1 collective-permute-done.3.v2m
  21.1 3.1 %key_grads.1 = (bf16[8,384,256]{2,1,0:T(8,128)(2,1)S(1)}, bf16[128,512]{1,0:T(8,128)(2,1)S(1)}, bf16[128,512]{1,0:T(8,128)(2,1)S(1)}, bf16[128,3072]{1,0:T(8,128)(2,1)S(1)}) custom-call(s32[1]{0:T(128)} %bitcast.rank_ref, bf16[8,384,256]{2,1,0:T(8,128)(2,1)S(1)} %get-tuple-element.33.prob_ref, bf16[128,1024]{1,0:T(8,128)(2,1)S(1)} %get-tuple-element.27.qm, ...), custom_call_target="tpu_custom_call" | custom-call | bytes 1000 | tf_op jit(solution)/shard_map/key_grads/pallas_call | solution.py:268
  24.3 1.8 %collective-permute-start.8 = (bf16[128,512]{1,0:T(8,128)(2,1)S(1)}, bf16[128,512]{1,0:T(8,128)(2,1)S(1)}, u32[]{:S(2)}, u32[]{:S(2)}) collective-permute-start(bf16[128,512]{1,0:T(8,128)(2,1)S(1)} %get-tuple-element.45), channel_id=1, source_target_pairs={{2,0},{3,1},{4,2},{5,3},{6,4},{7,5},{8,6},{9,7},{10,8},{11,9},{12,... | collective-permute-start | bytes 393224 | tf_op jit(solution)/shard_map/ppermute | solution.py:292
  26.1 1.0 %collective-permute-start.9 = (bf16[128,512]{1,0:T(8,128)(2,1)S(1)}, bf16[128,512]{1,0:T(8,128)(2,1)S(1)}, u32[]{:S(2)}, u32[]{:S(2)}) collective-permute-start(bf16[128,512]{1,0:T(8,128)(2,1)S(1)} %get-tuple-element.46), channel_id=1, source_target_pairs={{3,0},{2,1},{5,2},{4,3},{7,4},{6,5},{9,6},{8,7},{11,8},{10,9},{13,... | collective-permute-start | bytes 393224 | tf_op jit(solution)/shard_map/ppermute | solution.py:292
  27.0 0.5 %collective-permute-start.5 = (bf16[128,3072]{1,0:T(8,128)(2,1)S(1)}, bf16[128,3072]{1,0:T(8,128)(2,1)S(1)}, u32[]{:S(2)}, u32[]{:S(2)}) collective-permute-start(bf16[128,3072]{1,0:T(8,128)(2,1)S(1)} %get-tuple-element.37), channel_id=1, source_target_pairs={{0,1},{1,0},{2,3},{3,2},{4,5},{5,4},{6,7},{7,6},{8,9},{9,8},{10,11... | collective-permute-start | bytes 2359304 | tf_op jit(solution)/shard_map/ppermute | solution.py:292
  27.6 0.3 own_values.1.dvm
  27.9 1.6 %collective-permute-done.5.got.near = bf16[128,3072]{1,0:T(8,128)(2,1)S(1)} collective-permute-done((bf16[128,3072]{1,0:T(8,128)(2,1)S(1)}, bf16[128,3072]{1,0:T(8,128)(2,1)S(1)}, u32[]{:S(2)}, u32[]{:S(2)}) %collective-permute-start.5) | collective-permute-done | bytes 786464 | tf_op jit(solution)/shard_map/ppermute | solution.py:292
  29.5 2.1 %other_grads.1 = (bf16[128,2048]{1,0:T(8,128)(2,1)}, f32[128,2048]{1,0:T(8,128)}, f32[128,512]{1,0:T(8,128)S(1)}, f32[128,1024]{1,0:T(8,128)}) custom-call(s32[1]{0:T(128)} %bitcast.rank_ref, bf16[8,384,256]{2,1,0:T(8,128)(2,1)S(1)} %get-tuple-element.33.prob_ref, bf16[8,384,256]{2,1,0:T(8,128)(2,1)S(1)} %get-tuple-element.36.dscore_ref, ...), custom_call_target="tpu_custom_call" | custom-call | bytes 1000 | tf_op jit(solution)/shard_map/other_grads/pallas_call | solution.py:268
  31.6 1.3 %collective-permute-done.9.backo = bf16[128,512]{1,0:T(8,128)(2,1)S(1)} collective-permute-done((bf16[128,512]{1,0:T(8,128)(2,1)S(1)}, bf16[128,512]{1,0:T(8,128)(2,1)S(1)}, u32[]{:S(2)}, u32[]{:S(2)}) %collective-permute-start.9) | collective-permute-done | bytes 131104 | tf_op jit(solution)/shard_map/ppermute | solution.py:292
  32.9 0.8 %join_keys.1 = f32[128,1024]{1,0:T(8,128)} custom-call(s32[1]{0:T(128)} %bitcast.rank_ref, f32[128,512]{1,0:T(8,128)S(1)} %get-tuple-element.44.mine, bf16[128,3072]{1,0:T(8,128)(2,1)S(1)} %collective-permute-done.5.got.near, bf16[128,512]{1,0:T(8,128)(2,1)S(1)} %collective-permute-done.8.backm, bf16[128,512]{1,0:T(8,128)(2,1)S(1)} %collective-permute-done.9.backo), custom_call_target="tpu_custom_call" | custom-call | bytes 1000 | tf_op jit(solution)/shard_map/join_keys/pallas_call | solution.py:268
  (15 shorter events, 0.1 us)
Async XLA Ops:
  0.6 11.2 %copy-start.4 = (s32[32]{0:T(128)S(1)}, s32[32]{0:T(128)}, u32[]{:S(2)}) copy-start(s32[32]{0:T(128)} %param.9) | copy-start | bytes 388
  0.6 1.0 %copy-start.2 = (bf16[128,1024]{1,0:T(8,128)(2,1)S(1)}, bf16[128,1024]{1,0:T(8,128)(2,1)}, u32[]{:S(2)}) copy-start(bf16[128,1024]{1,0:T(8,128)(2,1)} %source.1) | copy-start | bytes 786436
  1.6 10.4 %collective-permute-start.2 = (bf16[128,512]{1,0:T(8,128)(2,1)S(1)}, bf16[128,512]{1,0:T(8,128)(2,1)S(1)}, u32[]{:S(2)}, u32[]{:S(2)}) collective-permute-start(bf16[128,512]{1,0:T(8,128)(2,1)S(1)} %get-tuple-element.26.kx), channel_id=1, source_target_pairs={{0,3},{1,2},{2,5},{3,4},{4,7},{5,6},{6,9},{7,8},{8,11},{9,10},{10,... | collective-permute-start | bytes 393224 | tf_op jit(solution)/shard_map/ppermute | solution.py:292
  4.1 10.8 %collective-permute-start.1 = (bf16[128,512]{1,0:T(8,128)(2,1)S(1)}, bf16[128,512]{1,0:T(8,128)(2,1)S(1)}, u32[]{:S(2)}, u32[]{:S(2)}) collective-permute-start(bf16[128,512]{1,0:T(8,128)(2,1)S(1)} %get-tuple-element.29.km), channel_id=1, source_target_pairs={{0,2},{1,3},{2,4},{3,5},{4,6},{5,7},{6,8},{7,9},{8,10},{9,11},{10,... | collective-permute-start | bytes 393224 | tf_op jit(solution)/shard_map/ppermute | solution.py:292
  5.6 1.0 %copy-start = (bf16[128,2048]{1,0:T(8,128)(2,1)S(1)}, bf16[128,2048]{1,0:T(8,128)(2,1)}, u32[]{:S(2)}) copy-start(bf16[128,2048]{1,0:T(8,128)(2,1)} %q_ref.1) | copy-start | bytes 1572868
  6.6 1.0 %copy-start.1 = (bf16[128,2048]{1,0:T(8,128)(2,1)S(1)}, bf16[128,2048]{1,0:T(8,128)(2,1)}, u32[]{:S(2)}) copy-start(bf16[128,2048]{1,0:T(8,128)(2,1)} %g_ref.1) | copy-start | bytes 1572868
  7.7 0.9 %copy-start.3 = (bf16[128,1024]{1,0:T(8,128)(2,1)S(1)}, bf16[128,1024]{1,0:T(8,128)(2,1)}, u32[]{:S(2)}) copy-start(bf16[128,1024]{1,0:T(8,128)(2,1)} %v_ref.1) | copy-start | bytes 786436
  8.7 12.3 %collective-permute-start.4 = (bf16[128,512]{1,0:T(8,128)(2,1)S(1)}, bf16[128,512]{1,0:T(8,128)(2,1)S(1)}, u32[]{:S(2)}, u32[]{:S(2)}) collective-permute-start(bf16[128,512]{1,0:T(8,128)(2,1)S(1)} %get-tuple-element.35), channel_id=1, source_target_pairs={{0,3},{1,2},{2,5},{3,4},{4,7},{5,6},{6,9},{7,8},{8,11},{9,10},{10,... | collective-permute-start | bytes 393224 | tf_op jit(solution)/shard_map/ppermute | solution.py:292
  10.3 10.8 %collective-permute-start.3 = (bf16[128,512]{1,0:T(8,128)(2,1)S(1)}, bf16[128,512]{1,0:T(8,128)(2,1)S(1)}, u32[]{:S(2)}, u32[]{:S(2)}) collective-permute-start(bf16[128,512]{1,0:T(8,128)(2,1)S(1)} %get-tuple-element.34.vm), channel_id=1, source_target_pairs={{0,2},{1,3},{2,4},{3,5},{4,6},{5,7},{6,8},{7,9},{8,10},{9,11},{10,... | collective-permute-start | bytes 393224 | tf_op jit(solution)/shard_map/ppermute | solution.py:292
  11.8 3.1 %collective-permute-start = (bf16[128,3072]{1,0:T(8,128)(2,1)S(1)}, bf16[128,3072]{1,0:T(8,128)(2,1)S(1)}, u32[]{:S(2)}, u32[]{:S(2)}) collective-permute-start(bf16[128,3072]{1,0:T(8,128)(2,1)S(1)} %get-tuple-element.30), channel_id=1, source_target_pairs={{0,1},{1,0},{2,3},{3,2},{4,5},{5,4},{6,7},{7,6},{8,9},{9,8},{10,11... | collective-permute-start | bytes 2359304 | tf_op jit(solution)/shard_map/ppermute | solution.py:292
  17.7 9.9 %collective-permute-start.6 = (bf16[128,512]{1,0:T(8,128)(2,1)S(1)}, bf16[128,512]{1,0:T(8,128)(2,1)S(1)}, u32[]{:S(2)}, u32[]{:S(2)}) collective-permute-start(bf16[128,512]{1,0:T(8,128)(2,1)S(1)} %get-tuple-element.38), channel_id=1, source_target_pairs={{2,0},{3,1},{4,2},{5,3},{6,4},{7,5},{8,6},{9,7},{10,8},{11,9},{12,... | collective-permute-start | bytes 393224 | tf_op jit(solution)/shard_map/ppermute | solution.py:292
  21.0 8.4 %collective-permute-start.7 = (bf16[128,512]{1,0:T(8,128)(2,1)S(1)}, bf16[128,512]{1,0:T(8,128)(2,1)S(1)}, u32[]{:S(2)}, u32[]{:S(2)}) collective-permute-start(bf16[128,512]{1,0:T(8,128)(2,1)S(1)} %get-tuple-element.41), channel_id=1, source_target_pairs={{3,0},{2,1},{5,2},{4,3},{7,4},{6,5},{9,6},{8,7},{11,8},{10,9},{13,... | collective-permute-start | bytes 393224 | tf_op jit(solution)/shard_map/ppermute | solution.py:292
  24.3 7.3 %collective-permute-start.8 = (bf16[128,512]{1,0:T(8,128)(2,1)S(1)}, bf16[128,512]{1,0:T(8,128)(2,1)S(1)}, u32[]{:S(2)}, u32[]{:S(2)}) collective-permute-start(bf16[128,512]{1,0:T(8,128)(2,1)S(1)} %get-tuple-element.45), channel_id=1, source_target_pairs={{2,0},{3,1},{4,2},{5,3},{6,4},{7,5},{8,6},{9,7},{10,8},{11,9},{12,... | collective-permute-start | bytes 393224 | tf_op jit(solution)/shard_map/ppermute | solution.py:292
  26.1 6.9 %collective-permute-start.9 = (bf16[128,512]{1,0:T(8,128)(2,1)S(1)}, bf16[128,512]{1,0:T(8,128)(2,1)S(1)}, u32[]{:S(2)}, u32[]{:S(2)}) collective-permute-start(bf16[128,512]{1,0:T(8,128)(2,1)S(1)} %get-tuple-element.46), channel_id=1, source_target_pairs={{3,0},{2,1},{5,2},{4,3},{7,4},{6,5},{9,6},{8,7},{11,8},{10,9},{13,... | collective-permute-start | bytes 393224 | tf_op jit(solution)/shard_map/ppermute | solution.py:292
  27.0 2.4 %collective-permute-start.5 = (bf16[128,3072]{1,0:T(8,128)(2,1)S(1)}, bf16[128,3072]{1,0:T(8,128)(2,1)S(1)}, u32[]{:S(2)}, u32[]{:S(2)}) collective-permute-start(bf16[128,3072]{1,0:T(8,128)(2,1)S(1)} %get-tuple-element.37), channel_id=1, source_target_pairs={{0,1},{1,0},{2,3},{3,2},{4,5},{5,4},{6,7},{7,6},{8,9},{9,8},{10,11... | collective-permute-start | bytes 2359304 | tf_op jit(solution)/shard_map/ppermute | solution.py:292

commit v4 on v3

--- a/solution.py
+++ b/solution.py
@@ -29,7 +29,7 @@
 CONTRACT_FIRST = (((0,), (0,)), ((), ()))
 
 
-COST = {"far_keys": 20000, "own_values": 20000}
+COST = {"split_keys": 20000, "far_keys": 20000, "own_values": 20000}
 
 
 def dot(a, b):
@@ -63,39 +63,27 @@
     other[:, span(offset + head)] = jnp.where(odd, first, second).astype(other.dtype)
 
 
-def split_kernel(rank_ref, source, mine, other):
-    odd = rank_ref[0] % 2
-    width = source.shape[1] // CORES
-    for core in range(CORES):
-
-        @pl.when(odd == core)
-        def _():
-            mine[...] = source[:, core * width : (core + 1) * width]
-            other[...] = source[:, (1 - core) * width : (2 - core) * width]
-
-
-def rows_kernel(rank_ref, q_ref, g_ref, v_ref, kx, qm, gm, vm, vx, sent):
-    odd = rank_ref[0] % 2
-    wide, narrow = qm.shape[1], vm.shape[1]
-    at_keys, at_values = AT_KEYS * HEAD_SIZE, AT_VALUES * HEAD_SIZE
-    for core in range(CORES):
-        here = slice(core * wide, (core + 1) * wide)
-        there = slice((1 - core) * wide, (2 - core) * wide)
-
-        @pl.when(odd == core)
-        def _():
-            qm[...] = q_ref[:, here]
-            gm[...] = g_ref[:, here]
-            sent[:, :wide] = q_ref[:, there]
-            sent[:, wide : 2 * wide] = g_ref[:, there]
-            vm[...] = v_ref[:, core * narrow : (core + 1) * narrow]
-            vx[...] = v_ref[:, (1 - core) * narrow : (2 - core) * narrow]
-            sent[:, at_values:] = v_ref[:, (1 - core) * narrow : (2 - core) * narrow]
-
-    sent[:, at_keys:at_values] = kx[...]
-
-
-def bias_kernel(rank_ref, lens_ref, bias_ref):
+def halves(odd, width):
+    return (
+        pl.ds(pl.multiple_of(odd * width, width), width),
+        pl.ds(pl.multiple_of((1 - odd) * width, width), width),
+    )
+
+
+def copied(pairs, sem):
+    copies = [pltpu.make_async_copy(source, target, sem.at[i]) for i, (source, target) in enumerate(pairs)]
+    for copy in copies:
+        copy.start()
+    return copies
+
+
+def split_kernel(rank_ref, source, mine, other, sem):
+    here, there = halves(rank_ref[0] % CORES, mine.shape[1])
+    for copy in copied([(source.at[:, here], mine), (source.at[:, there], other)], sem):
+        copy.wait()
+
+
+def fill_bias(rank, lens_ref, bias_ref):
     _, span_rows, rows = bias_ref.shape
     docs = lens_ref.shape[1]
     later = lax.broadcasted_iota(jnp.int32, (docs, docs), 0)
@@ -103,7 +91,7 @@
     lens = jnp.broadcast_to(lens_ref[...].astype(jnp.float32), (docs, docs))
     ends = jnp.sum(jnp.where(earlier <= later, lens, 0.0), axis=1, keepdims=True)
     for block in range(CORES):
-        first = (rank_ref[0] // CORES * CORES + block) * rows
+        first = (rank // CORES * CORES + block) * rows
         query = first + lax.broadcasted_iota(jnp.int32, (1, rows), 1)
         ended = jnp.where(ends <= query.astype(jnp.float32), ends, 0.0)
         start = jnp.max(ended, axis=0, keepdims=True).astype(jnp.int32)
@@ -112,6 +100,32 @@
         bias_ref[block] = jnp.where((key >= lowest) & (key <= query), 0.0, NEGATIVE)
 
 
+def rows_kernel(
+    rank_ref, lens_ref, q_ref, g_ref, k_ref, v_ref, qm, gm, vm, vx, sent, bias_ref, sem
+):
+    odd = rank_ref[0] % CORES
+    wide, narrow = qm.shape[1], vm.shape[1]
+    here, there = halves(odd, wide)
+    here_kv, there_kv = halves(odd, narrow)
+    at_keys, at_values = AT_KEYS * HEAD_SIZE, AT_VALUES * HEAD_SIZE
+    copies = copied(
+        [
+            (v_ref.at[:, here_kv], vm),
+            (v_ref.at[:, there_kv], vx),
+            (q_ref.at[:, there], sent.at[:, :wide]),
+            (g_ref.at[:, there], sent.at[:, wide : 2 * wide]),
+            (k_ref.at[:, there_kv], sent.at[:, at_keys:at_values]),
+            (v_ref.at[:, there_kv], sent.at[:, at_values:]),
+            (q_ref.at[:, here], qm),
+            (g_ref.at[:, here], gm),
+        ],
+        sem,
+    )
+    fill_bias(rank_ref[0], lens_ref, bias_ref)
+    for copy in copies:
+        copy.wait()
+
+
 def order_kernel(rank_ref, mine, other, first, second):
     odd = rank_ref[0] % 2
     for core in range(CORES):
@@ -120,6 +134,18 @@
         def _():
             (second if core else first)[...] = mine[...]
             (first if core else second)[...] = other[...]
+
+
+def staged(units, *stages):
+    held = {}
+    for step in range(len(units) + len(stages) - 1):
+        for depth, stage in enumerate(stages):
+            at = step - depth
+            if 0 <= at < len(units):
+                held[at] = stage(*units[at], *held.get(at, ()))
+
+
+UNITS = [(head, block) for head in range(CORE_HEADS) for block in range(CORES)]
 
 
 def value_kernel(
@@ -128,22 +154,30 @@
 ):
     rows = qm.shape[0]
     odd = rank_ref[0] % 2 == 1
-    for head in range(CORE_HEADS):
+    grads = {}
+
+    def score(head, block):
         blocks = (ka[:, span(head)], kb[:, span(head)]) + both(odd, km, near, head, AT_KEYS)
-        queries = stacked(odd, qm, near, head, 0)
-        gradients = stacked(odd, gm, near, head, AT_GRADIENTS)
-        grads = []
-        for block in range(CORES):
-            keys = jnp.concatenate(blocks[block : block + 3], axis=0)
-            bias = jnp.concatenate([bias_ref[block]] * GROUP, axis=1)
-            scores = dot_last(keys, queries[block]) * (score_scale * LOG2E) + bias
-            top = jnp.max(scores, axis=0, keepdims=True)
-            raised = jnp.exp2(scores - top)
-            total = jnp.sum(raised, axis=0, keepdims=True)
-            prob = (raised * (1.0 / total)).astype(jnp.bfloat16)
-            prob_ref[head * CORES + block] = prob
-            grads.append(dot(prob[: (2 - block) * rows], gradients[block]))
-        put(odd, dvm, dvo, head, grads[0][:rows], grads[0][rows:] + grads[1])
+        queries = stacked(odd, qm, near, head, 0)[block]
+        return (dot_last(jnp.concatenate(blocks[block : block + 3], axis=0), queries),)
+
+    def normalise(head, block, scores):
+        bias = jnp.concatenate([bias_ref[block]] * GROUP, axis=1)
+        scores = scores * (score_scale * LOG2E) + bias
+        top = jnp.max(scores, axis=0, keepdims=True)
+        raised = jnp.exp2(scores - top)
+        total = jnp.sum(raised, axis=0, keepdims=True)
+        prob = (raised * (1.0 / total)).astype(jnp.bfloat16)
+        prob_ref[head * CORES + block] = prob
+        return (prob[: (2 - block) * rows],)
+
+    def far_grads(head, block, prob):
+        grads[block] = dot(prob, stacked(odd, gm, near, head, AT_GRADIENTS)[block])
+        if block == 1:
+            put(odd, dvm, dvo, head, grads[0][:rows], grads[0][rows:] + grads[1])
+        return ()
+
+    staged(UNITS, score, lambda head, block, scores: (scores,), normalise, far_grads)
 
 
 def local_sum(core, pairs_ref, sources, head, rows):
@@ -162,42 +196,63 @@
     return out, dq, dk
 
 
+def chosen(odd, pieces):
+    return jnp.concatenate([jnp.where(odd, pieces[i], pieces[i + 1]) for i in range(3)], axis=0)
+
+
+def other_sum(odd, pairs_ref, sources, head, rows):
+    here = head * CORES
+    mine = jnp.where(odd, sources[0], sources[1])
+    total = dot(pairs_ref[here + jnp.where(odd, 0, 1), 2 * rows :], mine)
+    return total + jnp.where(odd, dot(pairs_ref[here + 1, rows : 2 * rows], sources[1]), 0.0)
+
+
 def key_kernel(
     rank_ref, prob_ref, qm, gm, km, vm, near, ka, kb, v2m, v2o,
     dscore_ref, dkm, dko, sent,
 ):
     rows = qm.shape[0]
     odd = rank_ref[0] % 2 == 1
-    for head in range(CORE_HEADS):
-        values = both(odd, v2m, v2o, head) + both(odd, vm, near, head, AT_VALUES)
-        queries = stacked(odd, qm, near, head, 0)
-        gradients = stacked(odd, gm, near, head, AT_GRADIENTS)
-        grads = []
-        for block in range(CORES):
-            dprob = dot_last(jnp.concatenate(values[block : block + 3], axis=0), gradients[block])
-            prob = prob_ref[head * CORES + block].astype(jnp.float32)
-            delta = jnp.sum(prob * dprob, axis=0, keepdims=True)
-            dscore = (prob * ((dprob - delta) * score_scale)).astype(jnp.bfloat16)
-            dscore_ref[head * CORES + block] = dscore
-            grads.append(dot(dscore[: (2 - block) * rows], queries[block]))
-        put(odd, dkm, dko, head, grads[0][:rows], grads[0][rows:] + grads[1])
-    for core in range(CORES):
-
-        @pl.when(rank_ref[0] % 2 != core)
-        def _():
-            for head in range(CORE_HEADS):
-                keys = (ka[:, span(head)], kb[:, span(head)]) + both(odd, km, near, head, AT_KEYS)
-                values = both(odd, v2m, v2o, head) + both(odd, vm, near, head, AT_VALUES)
-                queries = stacked(odd, qm, near, head, 0)
-                gradients = stacked(odd, gm, near, head, AT_GRADIENTS)
-                out, dq, dk = local_grads(core, prob_ref, dscore_ref, keys, values, queries, head, rows)
-                for j in range(GROUP):
-                    at = slice(j * rows, (j + 1) * rows)
-                    sent[:, span(head * GROUP + j)] = out[at].astype(jnp.bfloat16)
-                    sent[:, span(AT_GRADIENTS + head * GROUP + j)] = dq[at].astype(jnp.bfloat16)
-                sent[:, span(AT_KEYS + head)] = dk.astype(jnp.bfloat16)
-                dv = local_sum(core, prob_ref, gradients, head, rows)
-                sent[:, span(AT_VALUES + head)] = dv.astype(jnp.bfloat16)
+    grads = {}
+
+    def value_blocks(head):
+        return both(odd, v2m, v2o, head) + both(odd, vm, near, head, AT_VALUES)
+
+    def product(head, block):
+        gradients = stacked(odd, gm, near, head, AT_GRADIENTS)[block]
+        values = jnp.concatenate(value_blocks(head)[block : block + 3], axis=0)
+        return (dot_last(values, gradients),)
+
+    def scale(head, block, dprob):
+        at = head * CORES + block
+        prob = prob_ref[at].astype(jnp.float32)
+        delta = jnp.sum(prob * dprob, axis=0, keepdims=True)
+        dscore = (prob * ((dprob - delta) * score_scale)).astype(jnp.bfloat16)
+        dscore_ref[at] = dscore
+        return (dscore[: (2 - block) * rows],)
+
+    def far_grads(head, block, dscore):
+        grads[block] = dot(dscore, stacked(odd, qm, near, head, 0)[block])
+        if block == 1:
+            put(odd, dkm, dko, head, grads[0][:rows], grads[0][rows:] + grads[1])
+            send(head)
+        return ()
+
+    def send(head):
+        keys = (ka[:, span(head)], kb[:, span(head)]) + both(odd, km, near, head, AT_KEYS)
+        at = head * CORES + jnp.where(odd, 0, 1)
+        out = dot_first(prob_ref[at], chosen(odd, value_blocks(head)))
+        dq = dot_first(dscore_ref[at], chosen(odd, keys))
+        for j in range(GROUP):
+            piece = slice(j * rows, (j + 1) * rows)
+            sent[:, span(head * GROUP + j)] = out[piece].astype(jnp.bfloat16)
+            sent[:, span(AT_GRADIENTS + head * GROUP + j)] = dq[piece].astype(jnp.bfloat16)
+        dk = other_sum(odd, dscore_ref, stacked(odd, qm, near, head, 0), head, rows)
+        dv = other_sum(odd, prob_ref, stacked(odd, gm, near, head, AT_GRADIENTS), head, rows)
+        sent[:, span(AT_KEYS + head)] = dk.astype(jnp.bfloat16)
+        sent[:, span(AT_VALUES + head)] = dv.astype(jnp.bfloat16)
+
+    staged(UNITS, product, lambda head, block, dprob: (dprob,), scale, far_grads)
 
 
 def own_values_kernel(rank_ref, prob_ref, gm, near, backm, dvm):
@@ -262,14 +317,16 @@
     return jax.ShapeDtypeStruct(dims, dtype)
 
 
-def run(kernel, name, outputs, index, *operands):
+def run(kernel, name, outputs, index, *operands, far=(), scratch=()):
     small = pl.BlockSpec(memory_space=pltpu.SMEM)
     whole = pl.BlockSpec(memory_space=pltpu.VMEM)
+    there = pl.BlockSpec(memory_space=pltpu.HBM)
     return pl.pallas_call(
         kernel,
-        in_specs=[small] + [whole] * len(operands),
+        in_specs=[small] + [there if i in far else whole for i in range(len(operands))],
         out_specs=[whole] * len(outputs),
         out_shape=outputs,
+        scratch_shapes=scratch,
         compiler_params=pltpu.CompilerParams(vmem_limit_bytes=40 * 2**20),
         cost_estimate=pl.CostEstimate(flops=COST.get(name, 0) * 1000000, bytes_accessed=1000, transcendentals=0),
         name=name,
@@ -299,23 +356,26 @@
 
     full = shape(keys.shape, jnp.float32)
     all_sent = shape((rows, ALL_SENT * HEAD_SIZE), jnp.bfloat16)
-    km, kx = run(split_kernel, "split_keys", [narrow] * 2, index, keys)
+    def copies(count):
+        return [pltpu.SemaphoreType.DMA((count,))]
+
+    km, kx = run(split_kernel, "split_keys", [narrow] * 2, index, keys, far=(0,), scratch=copies(2))
     k2m, k2o = moved(km, ahead), moved(kx, across)
-    qm, gm, vm, vx, sent = run(
-        rows_kernel, "split_rows", [wide, wide, narrow, narrow, all_sent],
-        index, queries, output_gradient, values, kx,
+    queries, kx = lax.optimization_barrier((queries, kx))
+    qm, gm, vm, vx, sent, bias = run(
+        rows_kernel, "split_rows",
+        [wide, wide, narrow, narrow, all_sent, shape((CORES, 3 * rows, rows), jnp.float32)],
+        index, doc_lengths.reshape(1, docs), queries, output_gradient, keys, values,
+        far=(1, 2, 3, 4), scratch=copies(8),
     )
     v2m, v2o = moved(vm, ahead), moved(vx, across)
     near = moved(sent, swap)
-    (bias,) = run(
-        bias_kernel, "bias", [shape((CORES, 3 * rows, rows), jnp.float32)],
-        index, doc_lengths.reshape(1, docs),
-    )
     ka, kb = run(order_kernel, "far_keys", [narrow] * 2, index, k2m, k2o)
     prob, dvm, dvo = run(
         value_kernel, "value_grads", [pairs, narrow, narrow],
         index, bias, qm, gm, km, near, ka, kb,
     )
+    dvm, v2o = lax.optimization_barrier((dvm, v2o))
     dv_back = moved(dvm, behind), moved(dvo, recross)
     dscore, dkm, dko, sent = run(
         key_kernel, "key_grads", [pairs, narrow, narrow, all_sent],

time: 34 us -> 33.2 us (0.976)
  waiting for transfers between devices: 5.93 us -> 9.22 us
  local copies, waits for them, and re-layouts: 3.98 us -> 0.96 us
  Pallas kernels: 9.46 us -> 8.05 us
    ppermute x10, waiting for transfers between devices: 5.93 us -> 9.22 us  [moved(): return lax.ppermute(value, AXES, pairs)]
    unnamed x10 -> x12, local copies, waits for them, and re-layouts: 3.98 us -> 0.96 us
    pallas_call x9 -> x8, Pallas kernels: 9.46 us -> 8.05 us  [run(): pl.pallas_call(kernel, in_specs=[small] + [there if i in far else whole f...]
    ppermute x10, starting transfers between devices: 13.7 us -> 14 us  [moved(): return lax.ppermute(value, AXES, pairs)]
  transfers between devices with their start and end apart: 10 -> 10, of which waited for: 4 -> 4; matrix products, arithmetic and copies ran while one was open for 0% -> 0% of each run, Pallas kernels for 25% -> 22%
where the time goes in v4:
time: 33.2 us; the launch traced here: 33 us
  starting transfers between devices  14 us (42%)
  waiting for transfers between devices  9.22 us (28%)
  Pallas kernels  8.05 us (24%)
  local copies, waits for them, and re-layouts  0.96 us (3%)
  between operations  0.74 us (2%)
    ppermute x10, starting transfers between devices, moved(): return lax.ppermute(value, AXES, pairs)  14 us
    ppermute x10, waiting for transfers between devices, moved(): return lax.ppermute(value, AXES, pairs)  9.22 us
    pallas_call x8, Pallas kernels, run(): pl.pallas_call(kernel, in_specs=[small] + [there if i in far else whole f...  8.05 us
    unnamed x12, local copies, waits for them, and re-layouts  0.96 us
  transfers between devices with their start and end apart: 10, of which 4 were waited for; matrix products, arithmetic and copies ran while one was open for 0% of the time, Pallas kernels for 22%

profile of v4, /device:TPU:0, one launch (start us, length us, event | category | flops | bytes accessed | tf_op | source)
XLA Modules:
  0.0 33.0 jit_solution(11414315057397520763)
XLA Ops:
  0.6 0.9 %copy-done.2 = bf16[128,1024]{1,0:T(8,128)(2,1)S(1)} copy-done((bf16[128,1024]{1,0:T(8,128)(2,1)S(1)}, bf16[128,1024]{1,0:T(8,128)(2,1)}, u32[]{:S(2)}) %copy-start.2) | copy-done | bytes 262168
  1.6 0.1 split_keys.1
  1.7 2.5 %collective-permute-start.2 = (bf16[128,512]{1,0:T(8,128)(2,1)S(1)}, bf16[128,512]{1,0:T(8,128)(2,1)S(1)}, u32[]{:S(2)}, u32[]{:S(2)}) collective-permute-start(bf16[128,512]{1,0:T(8,128)(2,1)S(1)} %get-tuple-element.30), channel_id=1, source_target_pairs={{0,3},{1,2},{2,5},{3,4},{4,7},{5,6},{6,9},{7,8},{8,11},{9,10},{10,... | collective-permute-start | bytes 393224 | tf_op jit(solution)/shard_map/ppermute | solution.py:349
  4.1 1.5 %collective-permute-start.1 = (bf16[128,512]{1,0:T(8,128)(2,1)S(1)}, bf16[128,512]{1,0:T(8,128)(2,1)S(1)}, u32[]{:S(2)}, u32[]{:S(2)}) collective-permute-start(bf16[128,512]{1,0:T(8,128)(2,1)S(1)} %get-tuple-element.35.km), channel_id=1, source_target_pairs={{0,2},{1,3},{2,4},{3,5},{4,6},{5,7},{6,8},{7,9},{8,10},{9,11},{10,... | collective-permute-start | bytes 393224 | tf_op jit(solution)/shard_map/ppermute | solution.py:349
  5.7 0.4 %split_rows.1 = (bf16[128,1024]{1,0:T(8,128)(2,1)S(1)}, bf16[128,1024]{1,0:T(8,128)(2,1)S(1)}, bf16[128,512]{1,0:T(8,128)(2,1)S(1)}, bf16[128,512]{1,0:T(8,128)(...) custom-call(s32[1]{0:T(128)} %bitcast.rank_ref, s32[1,32]{1,0:T(1,128)S(1)} %bitcast.2, ...), custom_call_target="tpu_custom_call" | custom-call | bytes 1000 | tf_op jit(solution)/shard_map/split_rows/pallas_call | solution.py:324
  6.1 1.6 %collective-permute-start.4 = (bf16[128,512]{1,0:T(8,128)(2,1)S(1)}, bf16[128,512]{1,0:T(8,128)(2,1)S(1)}, u32[]{:S(2)}, u32[]{:S(2)}) collective-permute-start(bf16[128,512]{1,0:T(8,128)(2,1)S(1)} %get-tuple-element.42), channel_id=1, source_target_pairs={{0,3},{1,2},{2,5},{3,4},{4,7},{5,6},{6,9},{7,8},{8,11},{9,10},{10,... | collective-permute-start | bytes 393224 | tf_op jit(solution)/shard_map/ppermute | solution.py:349
  7.7 1.5 %collective-permute-start.3 = (bf16[128,512]{1,0:T(8,128)(2,1)S(1)}, bf16[128,512]{1,0:T(8,128)(2,1)S(1)}, u32[]{:S(2)}, u32[]{:S(2)}) collective-permute-start(bf16[128,512]{1,0:T(8,128)(2,1)S(1)} %get-tuple-element.40.vm), channel_id=1, source_target_pairs={{0,2},{1,3},{2,4},{3,5},{4,6},{5,7},{6,8},{7,9},{8,10},{9,11},{10,... | collective-permute-start | bytes 393224 | tf_op jit(solution)/shard_map/ppermute | solution.py:349
  9.2 0.0 collective-permute-start
  9.2 2.1 %collective-permute-done.2.other = bf16[128,512]{1,0:T(8,128)(2,1)S(1)} collective-permute-done((bf16[128,512]{1,0:T(8,128)(2,1)S(1)}, bf16[128,512]{1,0:T(8,128)(2,1)S(1)}, u32[]{:S(2)}, u32[]{:S(2)}) %collective-permute-start.2) | collective-permute-done | bytes 131104 | tf_op jit(solution)/shard_map/ppermute | solution.py:349
  11.3 4.5 %collective-permute-done.1.mine = bf16[128,512]{1,0:T(8,128)(2,1)S(1)} collective-permute-done((bf16[128,512]{1,0:T(8,128)(2,1)S(1)}, bf16[128,512]{1,0:T(8,128)(2,1)S(1)}, u32[]{:S(2)}, u32[]{:S(2)}) %collective-permute-start.1) | collective-permute-done | bytes 131104 | tf_op jit(solution)/shard_map/ppermute | solution.py:349
  15.8 0.0 collective-permute-done.near
  15.8 1.7 %value_grads.1 = (bf16[8,384,256]{2,1,0:T(8,128)(2,1)S(1)}, bf16[128,512]{1,0:T(8,128)(2,1)S(1)}, bf16[128,512]{1,0:T(8,128)(2,1)S(1)}) custom-call(s32[1]{0:T(128)} %bitcast.rank_ref, f32[2,384,128]{2,1,0:T(8,128)S(1)} %get-tuple-element.32.bias_ref, bf16[128,1024]{1,0:T(8,128)(2,1)S(1)} %get-tuple-element.33.qm, ...), custom_call_target="tpu_custom_call" | custom-call | bytes 1000 | tf_op jit(solution)/shard_map/value_grads/pallas_call | solution.py:324
  17.5 0.0 collective-permute-done.4.v2o
  17.6 2.5 %collective-permute-start.6 = (bf16[128,512]{1,0:T(8,128)(2,1)S(1)}, bf16[128,512]{1,0:T(8,128)(2,1)S(1)}, u32[]{:S(2)}, u32[]{:S(2)}) collective-permute-start(bf16[128,512]{1,0:T(8,128)(2,1)S(1)} %get-tuple-element.46), channel_id=1, source_target_pairs={{2,0},{3,1},{4,2},{5,3},{6,4},{7,5},{8,6},{9,7},{10,8},{11,9},{12,... | collective-permute-start | bytes 393224 | tf_op jit(solution)/shard_map/ppermute | solution.py:349
  20.1 0.8 %collective-permute-start.7 = (bf16[128,512]{1,0:T(8,128)(2,1)S(1)}, bf16[128,512]{1,0:T(8,128)(2,1)S(1)}, u32[]{:S(2)}, u32[]{:S(2)}) collective-permute-start(bf16[128,512]{1,0:T(8,128)(2,1)S(1)} %get-tuple-element.49), channel_id=1, source_target_pairs={{3,0},{2,1},{5,2},{4,3},{7,4},{6,5},{9,6},{8,7},{11,8},{10,9},{13,... | collective-permute-start | bytes 393224 | tf_op jit(solution)/shard_map/ppermute | solution.py:349
  20.9 2.6 %key_grads.1 = (bf16[8,384,256]{2,1,0:T(8,128)(2,1)S(1)}, bf16[128,512]{1,0:T(8,128)(2,1)S(1)}, bf16[128,512]{1,0:T(8,128)(2,1)S(1)}, bf16[128,3072]{1,0:T(8,128)(2,1)S(1)}) custom-call(s32[1]{0:T(128)} %bitcast.rank_ref, bf16[8,384,256]{2,1,0:T(8,128)(2,1)S(1)} %get-tuple-element.39.prob_ref, bf16[128,1024]{1,0:T(8,128)(2,1)S(1)} %get-tuple-element.33.qm, ...), custom_call_target="tpu_custom_call" | custom-call | bytes 1000 | tf_op jit(solution)/shard_map/key_grads/pallas_call | solution.py:324
  23.5 2.0 %collective-permute-start.8 = (bf16[128,512]{1,0:T(8,128)(2,1)S(1)}, bf16[128,512]{1,0:T(8,128)(2,1)S(1)}, u32[]{:S(2)}, u32[]{:S(2)}) collective-permute-start(bf16[128,512]{1,0:T(8,128)(2,1)S(1)} %get-tuple-element.53), channel_id=1, source_target_pairs={{2,0},{3,1},{4,2},{5,3},{6,4},{7,5},{8,6},{9,7},{10,8},{11,9},{12,... | collective-permute-start | bytes 393224 | tf_op jit(solution)/shard_map/ppermute | solution.py:349
  25.6 0.8 %collective-permute-start.9 = (bf16[128,512]{1,0:T(8,128)(2,1)S(1)}, bf16[128,512]{1,0:T(8,128)(2,1)S(1)}, u32[]{:S(2)}, u32[]{:S(2)}) collective-permute-start(bf16[128,512]{1,0:T(8,128)(2,1)S(1)} %get-tuple-element.54), channel_id=1, source_target_pairs={{3,0},{2,1},{5,2},{4,3},{7,4},{6,5},{9,6},{8,7},{11,8},{10,9},{13,... | collective-permute-start | bytes 393224 | tf_op jit(solution)/shard_map/ppermute | solution.py:349
  26.4 0.7 %collective-permute-start.5 = (bf16[128,3072]{1,0:T(8,128)(2,1)S(1)}, bf16[128,3072]{1,0:T(8,128)(2,1)S(1)}, u32[]{:S(2)}, u32[]{:S(2)}) collective-permute-start(bf16[128,3072]{1,0:T(8,128)(2,1)S(1)} %get-tuple-element.45), channel_id=1, source_target_pairs={{0,1},{1,0},{2,3},{3,2},{4,5},{5,4},{6,7},{7,6},{8,9},{9,8},{10,11... | collective-permute-start | bytes 2359304 | tf_op jit(solution)/shard_map/ppermute | solution.py:349
  27.1 0.3 own_values.1.dvm
  27.4 1.6 %collective-permute-done.5.got.near = bf16[128,3072]{1,0:T(8,128)(2,1)S(1)} collective-permute-done((bf16[128,3072]{1,0:T(8,128)(2,1)S(1)}, bf16[128,3072]{1,0:T(8,128)(2,1)S(1)}, u32[]{:S(2)}, u32[]{:S(2)}) %collective-permute-start.5) | collective-permute-done | bytes 786464 | tf_op jit(solution)/shard_map/ppermute | solution.py:349
  29.0 2.1 %other_grads.1 = (bf16[128,2048]{1,0:T(8,128)(2,1)}, f32[128,2048]{1,0:T(8,128)}, f32[128,512]{1,0:T(8,128)S(1)}, f32[128,1024]{1,0:T(8,128)}) custom-call(s32[1]{0:T(128)} %bitcast.rank_ref, bf16[8,384,256]{2,1,0:T(8,128)(2,1)S(1)} %get-tuple-element.39.prob_ref, bf16[8,384,256]{2,1,0:T(8,128)(2,1)S(1)} %get-tuple-element.44.dscore_ref, ...), custom_call_target="tpu_custom_call" | custom-call | bytes 1000 | tf_op jit(solution)/shard_map/other_grads/pallas_call | solution.py:324
  31.1 1.0 %collective-permute-done.9.backo = bf16[128,512]{1,0:T(8,128)(2,1)S(1)} collective-permute-done((bf16[128,512]{1,0:T(8,128)(2,1)S(1)}, bf16[128,512]{1,0:T(8,128)(2,1)S(1)}, u32[]{:S(2)}, u32[]{:S(2)}) %collective-permute-start.9) | collective-permute-done | bytes 131104 | tf_op jit(solution)/shard_map/ppermute | solution.py:349
  32.2 0.8 %join_keys.1 = f32[128,1024]{1,0:T(8,128)} custom-call(s32[1]{0:T(128)} %bitcast.rank_ref, f32[128,512]{1,0:T(8,128)S(1)} %get-tuple-element.52.mine, bf16[128,3072]{1,0:T(8,128)(2,1)S(1)} %collective-permute-done.5.got.near, bf16[128,512]{1,0:T(8,128)(2,1)S(1)} %collective-permute-done.8.backm, bf16[128,512]{1,0:T(8,128)(2,1)S(1)} %collective-permute-done.9.backo), custom_call_target="tpu_custom_call" | custom-call | bytes 1000 | tf_op jit(solution)/shard_map/join_keys/pallas_call | solution.py:324
  (16 shorter events, 0.1 us)
Async XLA Ops:
  0.6 1.0 %copy-start.2 = (bf16[128,1024]{1,0:T(8,128)(2,1)S(1)}, bf16[128,1024]{1,0:T(8,128)(2,1)}, u32[]{:S(2)}) copy-start(bf16[128,1024]{1,0:T(8,128)(2,1)} %k_ref.1) | copy-start | bytes 786436
  1.6 4.1 %copy-start = (bf16[128,2048]{1,0:T(8,128)(2,1)S(1)}, bf16[128,2048]{1,0:T(8,128)(2,1)}, u32[]{:S(2)}) copy-start(bf16[128,2048]{1,0:T(8,128)(2,1)} %q_ref) | copy-start | bytes 1572868
  1.6 4.1 %copy-start.1 = (bf16[128,2048]{1,0:T(8,128)(2,1)S(1)}, bf16[128,2048]{1,0:T(8,128)(2,1)}, u32[]{:S(2)}) copy-start(bf16[128,2048]{1,0:T(8,128)(2,1)} %g_ref.1) | copy-start | bytes 1572868
  1.6 4.1 %copy-start.3 = (bf16[128,1024]{1,0:T(8,128)(2,1)S(1)}, bf16[128,1024]{1,0:T(8,128)(2,1)}, u32[]{:S(2)}) copy-start(bf16[128,1024]{1,0:T(8,128)(2,1)} %k_ref.1) | copy-start | bytes 786436
  1.6 4.1 %copy-start.4 = (bf16[128,1024]{1,0:T(8,128)(2,1)S(1)}, bf16[128,1024]{1,0:T(8,128)(2,1)}, u32[]{:S(2)}) copy-start(bf16[128,1024]{1,0:T(8,128)(2,1)} %v_ref.1) | copy-start | bytes 786436
  1.6 4.1 %copy-start.5 = (s32[32]{0:T(128)S(1)}, s32[32]{0:T(128)}, u32[]{:S(2)}) copy-start(s32[32]{0:T(128)} %param.9) | copy-start | bytes 388
  1.7 9.6 %collective-permute-start.2 = (bf16[128,512]{1,0:T(8,128)(2,1)S(1)}, bf16[128,512]{1,0:T(8,128)(2,1)S(1)}, u32[]{:S(2)}, u32[]{:S(2)}) collective-permute-start(bf16[128,512]{1,0:T(8,128)(2,1)S(1)} %get-tuple-element.30), channel_id=1, source_target_pairs={{0,3},{1,2},{2,5},{3,4},{4,7},{5,6},{6,9},{7,8},{8,11},{9,10},{10,... | collective-permute-start | bytes 393224 | tf_op jit(solution)/shard_map/ppermute | solution.py:349
  4.1 11.7 %collective-permute-start.1 = (bf16[128,512]{1,0:T(8,128)(2,1)S(1)}, bf16[128,512]{1,0:T(8,128)(2,1)S(1)}, u32[]{:S(2)}, u32[]{:S(2)}) collective-permute-start(bf16[128,512]{1,0:T(8,128)(2,1)S(1)} %get-tuple-element.35.km), channel_id=1, source_target_pairs={{0,2},{1,3},{2,4},{3,5},{4,6},{5,7},{6,8},{7,9},{8,10},{9,11},{10,... | collective-permute-start | bytes 393224 | tf_op jit(solution)/shard_map/ppermute | solution.py:349
  6.1 11.5 %collective-permute-start.4 = (bf16[128,512]{1,0:T(8,128)(2,1)S(1)}, bf16[128,512]{1,0:T(8,128)(2,1)S(1)}, u32[]{:S(2)}, u32[]{:S(2)}) collective-permute-start(bf16[128,512]{1,0:T(8,128)(2,1)S(1)} %get-tuple-element.42), channel_id=1, source_target_pairs={{0,3},{1,2},{2,5},{3,4},{4,7},{5,6},{6,9},{7,8},{8,11},{9,10},{10,... | collective-permute-start | bytes 393224 | tf_op jit(solution)/shard_map/ppermute | solution.py:349
  7.7 13.2 %collective-permute-start.3 = (bf16[128,512]{1,0:T(8,128)(2,1)S(1)}, bf16[128,512]{1,0:T(8,128)(2,1)S(1)}, u32[]{:S(2)}, u32[]{:S(2)}) collective-permute-start(bf16[128,512]{1,0:T(8,128)(2,1)S(1)} %get-tuple-element.40.vm), channel_id=1, source_target_pairs={{0,2},{1,3},{2,4},{3,5},{4,6},{5,7},{6,8},{7,9},{8,10},{9,11},{10,... | collective-permute-start | bytes 393224 | tf_op jit(solution)/shard_map/ppermute | solution.py:349
  9.2 6.6 %collective-permute-start = (bf16[128,3072]{1,0:T(8,128)(2,1)S(1)}, bf16[128,3072]{1,0:T(8,128)(2,1)S(1)}, u32[]{:S(2)}, u32[]{:S(2)}) collective-permute-start(bf16[128,3072]{1,0:T(8,128)(2,1)S(1)} %get-tuple-element.36), channel_id=1, source_target_pairs={{0,1},{1,0},{2,3},{3,2},{4,5},{5,4},{6,7},{7,6},{8,9},{9,8},{10,11... | collective-permute-start | bytes 2359304 | tf_op jit(solution)/shard_map/ppermute | solution.py:349
  17.6 9.5 %collective-permute-start.6 = (bf16[128,512]{1,0:T(8,128)(2,1)S(1)}, bf16[128,512]{1,0:T(8,128)(2,1)S(1)}, u32[]{:S(2)}, u32[]{:S(2)}) collective-permute-start(bf16[128,512]{1,0:T(8,128)(2,1)S(1)} %get-tuple-element.46), channel_id=1, source_target_pairs={{2,0},{3,1},{4,2},{5,3},{6,4},{7,5},{8,6},{9,7},{10,8},{11,9},{12,... | collective-permute-start | bytes 393224 | tf_op jit(solution)/shard_map/ppermute | solution.py:349
  20.1 8.9 %collective-permute-start.7 = (bf16[128,512]{1,0:T(8,128)(2,1)S(1)}, bf16[128,512]{1,0:T(8,128)(2,1)S(1)}, u32[]{:S(2)}, u32[]{:S(2)}) collective-permute-start(bf16[128,512]{1,0:T(8,128)(2,1)S(1)} %get-tuple-element.49), channel_id=1, source_target_pairs={{3,0},{2,1},{5,2},{4,3},{7,4},{6,5},{9,6},{8,7},{11,8},{10,9},{13,... | collective-permute-start | bytes 393224 | tf_op jit(solution)/shard_map/ppermute | solution.py:349
  23.5 7.6 %collective-permute-start.8 = (bf16[128,512]{1,0:T(8,128)(2,1)S(1)}, bf16[128,512]{1,0:T(8,128)(2,1)S(1)}, u32[]{:S(2)}, u32[]{:S(2)}) collective-permute-start(bf16[128,512]{1,0:T(8,128)(2,1)S(1)} %get-tuple-element.53), channel_id=1, source_target_pairs={{2,0},{3,1},{4,2},{5,3},{6,4},{7,5},{8,6},{9,7},{10,8},{11,9},{12,... | collective-permute-start | bytes 393224 | tf_op jit(solution)/shard_map/ppermute | solution.py:349
  25.6 6.6 %collective-permute-start.9 = (bf16[128,512]{1,0:T(8,128)(2,1)S(1)}, bf16[128,512]{1,0:T(8,128)(2,1)S(1)}, u32[]{:S(2)}, u32[]{:S(2)}) collective-permute-start(bf16[128,512]{1,0:T(8,128)(2,1)S(1)} %get-tuple-element.54), channel_id=1, source_target_pairs={{3,0},{2,1},{5,2},{4,3},{7,4},{6,5},{9,6},{8,7},{11,8},{10,9},{13,... | collective-permute-start | bytes 393224 | tf_op jit(solution)/shard_map/ppermute | solution.py:349
  26.4 2.6 %collective-permute-start.5 = (bf16[128,3072]{1,0:T(8,128)(2,1)S(1)}, bf16[128,3072]{1,0:T(8,128)(2,1)S(1)}, u32[]{:S(2)}, u32[]{:S(2)}) collective-permute-start(bf16[128,3072]{1,0:T(8,128)(2,1)S(1)} %get-tuple-element.45), channel_id=1, source_target_pairs={{0,1},{1,0},{2,3},{3,2},{4,5},{5,4},{6,7},{7,6},{8,9},{9,8},{10,11... | collective-permute-start | bytes 2359304 | tf_op jit(solution)/shard_map/ppermute | solution.py:349

commit v5 on v4

--- a/solution.py
+++ b/solution.py
@@ -29,7 +29,7 @@
 CONTRACT_FIRST = (((0,), (0,)), ((), ()))
 
 
-COST = {"split_keys": 20000, "far_keys": 20000, "own_values": 20000}
+COST = {"own_grads": 20000, "split_keys": 20000, "far_keys": 20000}
 
 
 def dot(a, b):
@@ -208,8 +208,8 @@
 
 
 def key_kernel(
-    rank_ref, prob_ref, qm, gm, km, vm, near, ka, kb, v2m, v2o,
-    dscore_ref, dkm, dko, sent,
+    rank_ref, prob_ref, qm, gm, vm, near, v2m, v2o,
+    dscore_ref, dkm, dko,
 ):
     rows = qm.shape[0]
     odd = rank_ref[0] % 2 == 1
@@ -235,13 +235,21 @@
         grads[block] = dot(dscore, stacked(odd, qm, near, head, 0)[block])
         if block == 1:
             put(odd, dkm, dko, head, grads[0][:rows], grads[0][rows:] + grads[1])
-            send(head)
         return ()
 
-    def send(head):
+    staged(UNITS, product, lambda head, block, dprob: (dprob,), scale, far_grads)
+
+
+def sent_kernel(
+    rank_ref, prob_ref, dscore_ref, qm, gm, km, vm, near, ka, kb, v2m, v2o,
+    sent,
+):
+    rows = qm.shape[0]
+    odd = rank_ref[0] % 2 == 1
+    for head in range(CORE_HEADS):
         keys = (ka[:, span(head)], kb[:, span(head)]) + both(odd, km, near, head, AT_KEYS)
         at = head * CORES + jnp.where(odd, 0, 1)
-        out = dot_first(prob_ref[at], chosen(odd, value_blocks(head)))
+        out = dot_first(prob_ref[at], chosen(odd, (both(odd, v2m, v2o, head) + both(odd, vm, near, head, AT_VALUES))))
         dq = dot_first(dscore_ref[at], chosen(odd, keys))
         for j in range(GROUP):
             piece = slice(j * rows, (j + 1) * rows)
@@ -252,51 +260,49 @@
         sent[:, span(AT_KEYS + head)] = dk.astype(jnp.bfloat16)
         sent[:, span(AT_VALUES + head)] = dv.astype(jnp.bfloat16)
 
-    staged(UNITS, product, lambda head, block, dprob: (dprob,), scale, far_grads)
-
-
-def own_values_kernel(rank_ref, prob_ref, gm, near, backm, dvm):
-    rows = gm.shape[0]
+
+def own_kernel(
+    rank_ref, prob_ref, dscore_ref, qm, gm, km, vm, near, ka, kb, v2m, v2o, backm,
+    outm, dqm, dkm, dvm,
+):
+    rows = qm.shape[0]
     odd = rank_ref[0] % 2 == 1
     for core in range(CORES):
 
         @pl.when(rank_ref[0] % 2 == core)
         def _():
             for head in range(CORE_HEADS):
+                keys = (ka[:, span(head)], kb[:, span(head)]) + both(odd, km, near, head, AT_KEYS)
+                values = both(odd, v2m, v2o, head) + both(odd, vm, near, head, AT_VALUES)
+                queries = stacked(odd, qm, near, head, 0)
                 gradients = stacked(odd, gm, near, head, AT_GRADIENTS)
+                out, dq, dk = local_grads(core, prob_ref, dscore_ref, keys, values, queries, head, rows)
+                for j in range(GROUP):
+                    at = slice(j * rows, (j + 1) * rows)
+                    outm[:, span(head * GROUP + j)] = out[at].astype(jnp.bfloat16)
+                    dqm[:, span(head * GROUP + j)] = dq[at]
+                dkm[:, span(head)] = dk
                 dv = local_sum(core, prob_ref, gradients, head, rows)
                 dvm[:, span(head)] = dv + backm[:, span(head)].astype(jnp.float32)
 
 
-def rows_grads_kernel(
-    rank_ref, prob_ref, dscore_ref, qm, gm, km, vm, near, ka, kb, v2m, v2o, got, dvm, backo,
-    out_ref, dq_ref, dkm, dv_ref,
-):
-    rows = qm.shape[0]
-    odd = rank_ref[0] % 2 == 1
-    wide, narrow = qm.shape[1], km.shape[1]
+def join_kernel(rank_ref, got, outm, dqm, dvm, backo, out_ref, dq_ref, dv_ref):
+    odd = rank_ref[0] % CORES
+    wide, narrow = outm.shape[1], dvm.shape[1]
     for core in range(CORES):
-
-        @pl.when(rank_ref[0] % 2 == core)
+        here = slice(core * wide, (core + 1) * wide)
+        there = slice((1 - core) * wide, (2 - core) * wide)
+
+        @pl.when(odd == core)
         def _():
-            there = slice((1 - core) * wide, (2 - core) * wide)
+            out_ref[:, here] = outm[...]
             out_ref[:, there] = got[:, :wide]
+            dq_ref[:, here] = dqm[...]
             dq_ref[:, there] = got[:, wide : 2 * wide].astype(jnp.float32)
             dv_ref[:, core * narrow : (core + 1) * narrow] = dvm[...]
             dv_ref[:, (1 - core) * narrow : (2 - core) * narrow] = backo[...].astype(jnp.float32) + got[
                 :, AT_VALUES * HEAD_SIZE :
             ].astype(jnp.float32)
-            for head in range(CORE_HEADS):
-                keys = (ka[:, span(head)], kb[:, span(head)]) + both(odd, km, near, head, AT_KEYS)
-                values = both(odd, v2m, v2o, head) + both(odd, vm, near, head, AT_VALUES)
-                queries = stacked(odd, qm, near, head, 0)
-                out, dq, dk = local_grads(core, prob_ref, dscore_ref, keys, values, queries, head, rows)
-                for j in range(GROUP):
-                    at = slice(j * rows, (j + 1) * rows)
-                    here = span(core * CORE_QUERIES + head * GROUP + j)
-                    out_ref[:, here] = out[at].astype(jnp.bfloat16)
-                    dq_ref[:, here] = dq[at]
-                dkm[:, span(head)] = dk
 
 
 def add_kernel(offset, rank_ref, mine, near, backm, backo, target):
@@ -377,20 +383,27 @@
     )
     dvm, v2o = lax.optimization_barrier((dvm, v2o))
     dv_back = moved(dvm, behind), moved(dvo, recross)
-    dscore, dkm, dko, sent = run(
-        key_kernel, "key_grads", [pairs, narrow, narrow, all_sent],
-        index, prob, qm, gm, km, vm, near, ka, kb, v2m, v2o,
+    dscore, dkm, dko = run(
+        key_kernel, "key_grads", [pairs, narrow, narrow],
+        index, prob, qm, gm, vm, near, v2m, v2o,
     )
     dk_back = moved(dkm, behind), moved(dko, recross)
+    prob, dv_back1 = lax.optimization_barrier((prob, dv_back[1]))
+    dv_back = (dv_back[0], dv_back1)
+    (sent,) = run(
+        sent_kernel, "sent_grads", [all_sent],
+        index, prob, dscore, qm, gm, km, vm, near, ka, kb, v2m, v2o,
+    )
     got = moved(sent, swap)
-    (dvm,) = run(
-        own_values_kernel, "own_values", [narrow_sum], index, prob, gm, near, dv_back[0]
+    outm, dqm, dkm, dvm = run(
+        own_kernel, "own_grads", [wide, wide_sum, narrow_sum, narrow_sum],
+        index, prob, dscore, qm, gm, km, vm, near, ka, kb, v2m, v2o, dv_back[0],
     )
     got, dvm = lax.optimization_barrier((got, dvm))
-    attended, dq, dkm, dv = run(
-        rows_grads_kernel, "other_grads",
-        [shape(queries.shape, jnp.bfloat16), shape(queries.shape, jnp.float32), narrow_sum, full],
-        index, prob, dscore, qm, gm, km, vm, near, ka, kb, v2m, v2o, got, dvm, dv_back[1],
+    attended, dq, dv = run(
+        join_kernel, "join_rows",
+        [shape(queries.shape, jnp.bfloat16), shape(queries.shape, jnp.float32), full],
+        index, got, outm, dqm, dvm, dv_back[1],
     )
     (dk,) = run(functools.partial(add_kernel, AT_KEYS), "join_keys", [full], index, dkm, got, *dk_back)
     return attended, dq, dk, dv

time: 33.2 us -> 32.5 us (0.979)
  waiting for transfers between devices: 9.22 us -> 7.48 us
  starting transfers between devices: 14 us -> 15.3 us
    ppermute x10, waiting for transfers between devices: 9.22 us -> 7.48 us  [moved(): return lax.ppermute(value, AXES, pairs)]
    ppermute x10, starting transfers between devices: 14 us -> 15.3 us  [moved(): return lax.ppermute(value, AXES, pairs)]
    pallas_call x8 -> x9, Pallas kernels: 8.05 us -> 7.92 us  [run(): pl.pallas_call(kernel, in_specs=[small] + [there if i in far else whole f...]
  transfers between devices with their start and end apart: 10 -> 10, of which waited for: 4 -> 5; matrix products, arithmetic and copies ran while one was open for 0% -> 0% of each run, Pallas kernels for 22% -> 22%
where the time goes in v5:
time: 32.5 us; the launch traced here: 32.4 us
  starting transfers between devices  15.3 us (47%)
  Pallas kernels  7.92 us (24%)
  waiting for transfers between devices  7.48 us (23%)
  local copies, waits for them, and re-layouts  0.96 us (3%)
  between operations  0.74 us (2%)
    ppermute x10, starting transfers between devices, moved(): return lax.ppermute(value, AXES, pairs)  15.3 us
    pallas_call x9, Pallas kernels, run(): pl.pallas_call(kernel, in_specs=[small] + [there if i in far else whole f...  7.92 us
    ppermute x10, waiting for transfers between devices, moved(): return lax.ppermute(value, AXES, pairs)  7.48 us
    unnamed x12, local copies, waits for them, and re-layouts  0.96 us
  transfers between devices with their start and end apart: 10, of which 5 were waited for; matrix products, arithmetic and copies ran while one was open for 0% of the time, Pallas kernels for 22%

profile of v5, /device:TPU:0, one launch (start us, length us, event | category | flops | bytes accessed | tf_op | source)
XLA Modules:
  0.0 32.4 jit_solution(9556386823682844120)
XLA Ops:
  0.6 0.9 %copy-done.2 = bf16[128,1024]{1,0:T(8,128)(2,1)S(1)} copy-done((bf16[128,1024]{1,0:T(8,128)(2,1)S(1)}, bf16[128,1024]{1,0:T(8,128)(2,1)}, u32[]{:S(2)}) %copy-start.2) | copy-done | bytes 262168
  1.6 0.1 split_keys.1
  1.7 3.0 %collective-permute-start.1 = (bf16[128,512]{1,0:T(8,128)(2,1)S(1)}, bf16[128,512]{1,0:T(8,128)(2,1)S(1)}, u32[]{:S(2)}, u32[]{:S(2)}) collective-permute-start(bf16[128,512]{1,0:T(8,128)(2,1)S(1)} %get-tuple-element.39.km), channel_id=1, source_target_pairs={{0,2},{1,3},{2,4},{3,5},{4,6},{5,7},{6,8},{7,9},{8,10},{9,11},{10,... | collective-permute-start | bytes 393224 | tf_op jit(solution)/shard_map/ppermute | solution.py:355
  4.7 0.7 %collective-permute-start.2 = (bf16[128,512]{1,0:T(8,128)(2,1)S(1)}, bf16[128,512]{1,0:T(8,128)(2,1)S(1)}, u32[]{:S(2)}, u32[]{:S(2)}) collective-permute-start(bf16[128,512]{1,0:T(8,128)(2,1)S(1)} %get-tuple-element.34), channel_id=1, source_target_pairs={{0,3},{1,2},{2,5},{3,4},{4,7},{5,6},{6,9},{7,8},{8,11},{9,10},{10,... | collective-permute-start | bytes 393224 | tf_op jit(solution)/shard_map/ppermute | solution.py:355
  5.4 0.4 %split_rows.1 = (bf16[128,1024]{1,0:T(8,128)(2,1)S(1)}, bf16[128,1024]{1,0:T(8,128)(2,1)S(1)}, bf16[128,512]{1,0:T(8,128)(2,1)S(1)}, bf16[128,512]{1,0:T(8,128)(...) custom-call(s32[1]{0:T(128)} %bitcast.rank_ref, s32[1,32]{1,0:T(1,128)S(1)} %bitcast.2, ...), custom_call_target="tpu_custom_call" | custom-call | bytes 1000 | tf_op jit(solution)/shard_map/split_rows/pallas_call | solution.py:330
  5.8 1.0 %collective-permute-start = (bf16[128,3072]{1,0:T(8,128)(2,1)S(1)}, bf16[128,3072]{1,0:T(8,128)(2,1)S(1)}, u32[]{:S(2)}, u32[]{:S(2)}) collective-permute-start(bf16[128,3072]{1,0:T(8,128)(2,1)S(1)} %get-tuple-element.40), channel_id=1, source_target_pairs={{0,1},{1,0},{2,3},{3,2},{4,5},{5,4},{6,7},{7,6},{8,9},{9,8},{10,11... | collective-permute-start | bytes 2359304 | tf_op jit(solution)/shard_map/ppermute | solution.py:355
  6.8 1.2 %collective-permute-start.5 = (bf16[128,512]{1,0:T(8,128)(2,1)S(1)}, bf16[128,512]{1,0:T(8,128)(2,1)S(1)}, u32[]{:S(2)}, u32[]{:S(2)}) collective-permute-start(bf16[128,512]{1,0:T(8,128)(2,1)S(1)} %get-tuple-element.48), channel_id=1, source_target_pairs={{0,3},{1,2},{2,5},{3,4},{4,7},{5,6},{6,9},{7,8},{8,11},{9,10},{10,... | collective-permute-start | bytes 393224 | tf_op jit(solution)/shard_map/ppermute | solution.py:355
  8.0 1.5 %collective-permute-start.4 = (bf16[128,512]{1,0:T(8,128)(2,1)S(1)}, bf16[128,512]{1,0:T(8,128)(2,1)S(1)}, u32[]{:S(2)}, u32[]{:S(2)}) collective-permute-start(bf16[128,512]{1,0:T(8,128)(2,1)S(1)} %get-tuple-element.46.vm), channel_id=1, source_target_pairs={{0,2},{1,3},{2,4},{3,5},{4,6},{5,7},{6,8},{7,9},{8,10},{9,11},{10,... | collective-permute-start | bytes 393224 | tf_op jit(solution)/shard_map/ppermute | solution.py:355
  9.5 3.5 %collective-permute-done.1.mine = bf16[128,512]{1,0:T(8,128)(2,1)S(1)} collective-permute-done((bf16[128,512]{1,0:T(8,128)(2,1)S(1)}, bf16[128,512]{1,0:T(8,128)(2,1)S(1)}, u32[]{:S(2)}, u32[]{:S(2)}) %collective-permute-start.1) | collective-permute-done | bytes 131104 | tf_op jit(solution)/shard_map/ppermute | solution.py:355
  13.0 1.1 %collective-permute-done.2.other = bf16[128,512]{1,0:T(8,128)(2,1)S(1)} collective-permute-done((bf16[128,512]{1,0:T(8,128)(2,1)S(1)}, bf16[128,512]{1,0:T(8,128)(2,1)S(1)}, u32[]{:S(2)}, u32[]{:S(2)}) %collective-permute-start.2) | collective-permute-done | bytes 131104 | tf_op jit(solution)/shard_map/ppermute | solution.py:355
  14.2 1.7 %value_grads.1 = (bf16[8,384,256]{2,1,0:T(8,128)(2,1)S(1)}, bf16[128,512]{1,0:T(8,128)(2,1)S(1)}, bf16[128,512]{1,0:T(8,128)(2,1)S(1)}) custom-call(s32[1]{0:T(128)} %bitcast.rank_ref, f32[2,384,128]{2,1,0:T(8,128)S(1)} %get-tuple-element.36.bias_ref, bf16[128,1024]{1,0:T(8,128)(2,1)S(1)} %get-tuple-element.37.qm, ...), custom_call_target="tpu_custom_call" | custom-call | bytes 1000 | tf_op jit(solution)/shard_map/value_grads/pallas_call | solution.py:330
  15.9 3.5 %collective-permute-start.3 = (bf16[128,512]{1,0:T(8,128)(2,1)S(1)}, bf16[128,512]{1,0:T(8,128)(2,1)S(1)}, u32[]{:S(2)}, u32[]{:S(2)}) collective-permute-start(bf16[128,512]{1,0:T(8,128)(2,1)S(1)} %get-tuple-element.44), channel_id=1, source_target_pairs={{3,0},{2,1},{5,2},{4,3},{7,4},{6,5},{9,6},{8,7},{11,8},{10,9},{13,... | collective-permute-start | bytes 393224 | tf_op jit(solution)/shard_map/ppermute | solution.py:355
  19.4 1.0 %collective-permute-start.7 = (bf16[128,512]{1,0:T(8,128)(2,1)S(1)}, bf16[128,512]{1,0:T(8,128)(2,1)S(1)}, u32[]{:S(2)}, u32[]{:S(2)}) collective-permute-start(bf16[128,512]{1,0:T(8,128)(2,1)S(1)} %get-tuple-element.51), channel_id=1, source_target_pairs={{2,0},{3,1},{4,2},{5,3},{6,4},{7,5},{8,6},{9,7},{10,8},{11,9},{12,... | collective-permute-start | bytes 393224 | tf_op jit(solution)/shard_map/ppermute | solution.py:355
  20.4 0.3 %collective-permute-done.4.v2m = bf16[128,512]{1,0:T(8,128)(2,1)S(1)} collective-permute-done((bf16[128,512]{1,0:T(8,128)(2,1)S(1)}, bf16[128,512]{1,0:T(8,128)(2,1)S(1)}, u32[]{:S(2)}, u32[]{:S(2)}) %collective-permute-start.4) | collective-permute-done | bytes 131104 | tf_op jit(solution)/shard_map/ppermute | solution.py:355
  20.7 1.6 %key_grads.1 = (bf16[8,384,256]{2,1,0:T(8,128)(2,1)S(1)}, bf16[128,512]{1,0:T(8,128)(2,1)S(1)}, bf16[128,512]{1,0:T(8,128)(2,1)S(1)}) custom-call(s32[1]{0:T(128)} %bitcast.rank_ref, bf16[8,384,256]{2,1,0:T(8,128)(2,1)S(1)} %get-tuple-element.45.prob_ref, bf16[128,1024]{1,0:T(8,128)(2,1)S(1)} %get-tuple-element.37.qm, ...), custom_call_target="tpu_custom_call" | custom-call | bytes 1000 | tf_op jit(solution)/shard_map/key_grads/pallas_call | solution.py:330
  22.3 1.7 %collective-permute-start.8 = (bf16[128,512]{1,0:T(8,128)(2,1)S(1)}, bf16[128,512]{1,0:T(8,128)(2,1)S(1)}, u32[]{:S(2)}, u32[]{:S(2)}) collective-permute-start(bf16[128,512]{1,0:T(8,128)(2,1)S(1)} %get-tuple-element.61), channel_id=1, source_target_pairs={{2,0},{3,1},{4,2},{5,3},{6,4},{7,5},{8,6},{9,7},{10,8},{11,9},{12,... | collective-permute-start | bytes 393224 | tf_op jit(solution)/shard_map/ppermute | solution.py:355
  24.0 0.1 collective-permute-start.9
  24.1 0.9 %sent_grads.1 = bf16[128,3072]{1,0:T(8,128)(2,1)S(1)} custom-call(s32[1]{0:T(128)} %bitcast.rank_ref, bf16[8,384,256]{2,1,0:T(8,128)(2,1)S(1)} %get-tuple-element.45.prob_ref, bf16[8,384,256]{2,1,0:T(8,128)(2,1)S(1)} %get-tuple-element.50.dscore_ref, bf16[128,1024]{1,0:T(8,128)(2,1)S(1)} %get-tuple-element.37.qm, ...), custom_call_target="tpu_custom_call" | custom-call | bytes 1000 | tf_op jit(solution)/shard_map/sent_grads/pallas_call | solution.py:330
  25.0 1.6 %collective-permute-start.6 = (bf16[128,3072]{1,0:T(8,128)(2,1)S(1)}, bf16[128,3072]{1,0:T(8,128)(2,1)S(1)}, u32[]{:S(2)}, u32[]{:S(2)}) collective-permute-start(bf16[128,3072]{1,0:T(8,128)(2,1)S(1)} %sent_grads.1), channel_id=1, source_target_pairs={{0,1},{1,0},{2,3},{3,2},{4,5},{5,4},{6,7},{7,6},{8,9},{9,8},{10,11... | collective-permute-start | bytes 2359304 | tf_op jit(solution)/shard_map/ppermute | solution.py:355
  26.6 0.9 %own_grads.1 = (bf16[128,1024]{1,0:T(8,128)(2,1)S(1)}, f32[128,1024]{1,0:T(8,128)S(1)}, f32[128,512]{1,0:T(8,128)S(1)}, f32[128,512]{1,0:T(8,128)S(1)}) custom-call(s32[1]{0:T(128)} %bitcast.rank_ref, bf16[8,384,256]{2,1,0:T(8,128)(2,1)S(1)} %get-tuple-element.45.prob_ref, bf16[8,384,256]{2,1,0:T(8,128)(2,1)S(1)} %get-tuple-element.50.dscore_ref, ...), custom_call_target="tpu_custom_call" | custom-call | flops 20000000000 | bytes 1000 | tf_op jit(solution)/shard_map/own_grads/pallas_call | solution.py:330
  27.6 1.0 %collective-permute-done.6.got.near = bf16[128,3072]{1,0:T(8,128)(2,1)S(1)} collective-permute-done((bf16[128,3072]{1,0:T(8,128)(2,1)S(1)}, bf16[128,3072]{1,0:T(8,128)(2,1)S(1)}, u32[]{:S(2)}, u32[]{:S(2)}) %collective-permute-start.6) | collective-permute-done | bytes 786464 | tf_op jit(solution)/shard_map/ppermute | solution.py:355
  28.5 1.4 %join_rows.1 = (bf16[128,2048]{1,0:T(8,128)(2,1)}, f32[128,2048]{1,0:T(8,128)}, f32[128,1024]{1,0:T(8,128)}) custom-call(s32[1]{0:T(128)} %bitcast.rank_ref, bf16[128,3072]{1,0:T(8,128)(2,1)S(1)} %collective-permute-done.6.got.near, bf16[128,1024]{1,0:T(8,128)(2,1)S(1)} %get-tuple-element.54.outm, f32[128,1024]{1,0:T(8,128)S(1)} %get-tuple-element.55.dqm, ...), custom_call_target="tpu_custom_call" | custom-call | bytes 1000 | tf_op jit(solution)/shard_map/join_rows/pallas_call | solution.py:330
  30.0 1.5 %collective-permute-done.9.backo = bf16[128,512]{1,0:T(8,128)(2,1)S(1)} collective-permute-done((bf16[128,512]{1,0:T(8,128)(2,1)S(1)}, bf16[128,512]{1,0:T(8,128)(2,1)S(1)}, u32[]{:S(2)}, u32[]{:S(2)}) %collective-permute-start.9) | collective-permute-done | bytes 131104 | tf_op jit(solution)/shard_map/ppermute | solution.py:355
  31.5 0.8 %join_keys.1 = f32[128,1024]{1,0:T(8,128)} custom-call(s32[1]{0:T(128)} %bitcast.rank_ref, f32[128,512]{1,0:T(8,128)S(1)} %get-tuple-element.60.mine, bf16[128,3072]{1,0:T(8,128)(2,1)S(1)} %collective-permute-done.6.got.near, bf16[128,512]{1,0:T(8,128)(2,1)S(1)} %collective-permute-done.8.backm, bf16[128,512]{1,0:T(8,128)(2,1)S(1)} %collective-permute-done.9.backo), custom_call_target="tpu_custom_call" | custom-call | bytes 1000 | tf_op jit(solution)/shard_map/join_keys/pallas_call | solution.py:330
  (17 shorter events, 0.1 us)
Async XLA Ops:
  0.6 1.0 %copy-start.2 = (bf16[128,1024]{1,0:T(8,128)(2,1)S(1)}, bf16[128,1024]{1,0:T(8,128)(2,1)}, u32[]{:S(2)}) copy-start(bf16[128,1024]{1,0:T(8,128)(2,1)} %k_ref.1) | copy-start | bytes 786436
  1.6 3.8 %copy-start = (bf16[128,2048]{1,0:T(8,128)(2,1)S(1)}, bf16[128,2048]{1,0:T(8,128)(2,1)}, u32[]{:S(2)}) copy-start(bf16[128,2048]{1,0:T(8,128)(2,1)} %q_ref) | copy-start | bytes 1572868
  1.6 3.8 %copy-start.1 = (bf16[128,2048]{1,0:T(8,128)(2,1)S(1)}, bf16[128,2048]{1,0:T(8,128)(2,1)}, u32[]{:S(2)}) copy-start(bf16[128,2048]{1,0:T(8,128)(2,1)} %g_ref.1) | copy-start | bytes 1572868
  1.6 3.8 %copy-start.3 = (bf16[128,1024]{1,0:T(8,128)(2,1)S(1)}, bf16[128,1024]{1,0:T(8,128)(2,1)}, u32[]{:S(2)}) copy-start(bf16[128,1024]{1,0:T(8,128)(2,1)} %k_ref.1) | copy-start | bytes 786436
  1.6 3.8 %copy-start.4 = (bf16[128,1024]{1,0:T(8,128)(2,1)S(1)}, bf16[128,1024]{1,0:T(8,128)(2,1)}, u32[]{:S(2)}) copy-start(bf16[128,1024]{1,0:T(8,128)(2,1)} %v_ref.1) | copy-start | bytes 786436
  1.6 3.8 %copy-start.5 = (s32[32]{0:T(128)S(1)}, s32[32]{0:T(128)}, u32[]{:S(2)}) copy-start(s32[32]{0:T(128)} %param.9) | copy-start | bytes 388
  1.7 11.3 %collective-permute-start.1 = (bf16[128,512]{1,0:T(8,128)(2,1)S(1)}, bf16[128,512]{1,0:T(8,128)(2,1)S(1)}, u32[]{:S(2)}, u32[]{:S(2)}) collective-permute-start(bf16[128,512]{1,0:T(8,128)(2,1)S(1)} %get-tuple-element.39.km), channel_id=1, source_target_pairs={{0,2},{1,3},{2,4},{3,5},{4,6},{5,7},{6,8},{7,9},{8,10},{9,11},{10,... | collective-permute-start | bytes 393224 | tf_op jit(solution)/shard_map/ppermute | solution.py:355
  4.7 9.4 %collective-permute-start.2 = (bf16[128,512]{1,0:T(8,128)(2,1)S(1)}, bf16[128,512]{1,0:T(8,128)(2,1)S(1)}, u32[]{:S(2)}, u32[]{:S(2)}) collective-permute-start(bf16[128,512]{1,0:T(8,128)(2,1)S(1)} %get-tuple-element.34), channel_id=1, source_target_pairs={{0,3},{1,2},{2,5},{3,4},{4,7},{5,6},{6,9},{7,8},{8,11},{9,10},{10,... | collective-permute-start | bytes 393224 | tf_op jit(solution)/shard_map/ppermute | solution.py:355
  5.8 8.4 %collective-permute-start = (bf16[128,3072]{1,0:T(8,128)(2,1)S(1)}, bf16[128,3072]{1,0:T(8,128)(2,1)S(1)}, u32[]{:S(2)}, u32[]{:S(2)}) collective-permute-start(bf16[128,3072]{1,0:T(8,128)(2,1)S(1)} %get-tuple-element.40), channel_id=1, source_target_pairs={{0,1},{1,0},{2,3},{3,2},{4,5},{5,4},{6,7},{7,6},{8,9},{9,8},{10,11... | collective-permute-start | bytes 2359304 | tf_op jit(solution)/shard_map/ppermute | solution.py:355
  6.8 12.5 %collective-permute-start.5 = (bf16[128,512]{1,0:T(8,128)(2,1)S(1)}, bf16[128,512]{1,0:T(8,128)(2,1)S(1)}, u32[]{:S(2)}, u32[]{:S(2)}) collective-permute-start(bf16[128,512]{1,0:T(8,128)(2,1)S(1)} %get-tuple-element.48), channel_id=1, source_target_pairs={{0,3},{1,2},{2,5},{3,4},{4,7},{5,6},{6,9},{7,8},{8,11},{9,10},{10,... | collective-permute-start | bytes 393224 | tf_op jit(solution)/shard_map/ppermute | solution.py:355
  8.0 12.7 %collective-permute-start.4 = (bf16[128,512]{1,0:T(8,128)(2,1)S(1)}, bf16[128,512]{1,0:T(8,128)(2,1)S(1)}, u32[]{:S(2)}, u32[]{:S(2)}) collective-permute-start(bf16[128,512]{1,0:T(8,128)(2,1)S(1)} %get-tuple-element.46.vm), channel_id=1, source_target_pairs={{0,2},{1,3},{2,4},{3,5},{4,6},{5,7},{6,8},{7,9},{8,10},{9,11},{10,... | collective-permute-start | bytes 393224 | tf_op jit(solution)/shard_map/ppermute | solution.py:355
  15.9 8.3 %collective-permute-start.3 = (bf16[128,512]{1,0:T(8,128)(2,1)S(1)}, bf16[128,512]{1,0:T(8,128)(2,1)S(1)}, u32[]{:S(2)}, u32[]{:S(2)}) collective-permute-start(bf16[128,512]{1,0:T(8,128)(2,1)S(1)} %get-tuple-element.44), channel_id=1, source_target_pairs={{3,0},{2,1},{5,2},{4,3},{7,4},{6,5},{9,6},{8,7},{11,8},{10,9},{13,... | collective-permute-start | bytes 393224 | tf_op jit(solution)/shard_map/ppermute | solution.py:355
  19.4 7.3 %collective-permute-start.7 = (bf16[128,512]{1,0:T(8,128)(2,1)S(1)}, bf16[128,512]{1,0:T(8,128)(2,1)S(1)}, u32[]{:S(2)}, u32[]{:S(2)}) collective-permute-start(bf16[128,512]{1,0:T(8,128)(2,1)S(1)} %get-tuple-element.51), channel_id=1, source_target_pairs={{2,0},{3,1},{4,2},{5,3},{6,4},{7,5},{8,6},{9,7},{10,8},{11,9},{12,... | collective-permute-start | bytes 393224 | tf_op jit(solution)/shard_map/ppermute | solution.py:355
  22.3 7.7 %collective-permute-start.8 = (bf16[128,512]{1,0:T(8,128)(2,1)S(1)}, bf16[128,512]{1,0:T(8,128)(2,1)S(1)}, u32[]{:S(2)}, u32[]{:S(2)}) collective-permute-start(bf16[128,512]{1,0:T(8,128)(2,1)S(1)} %get-tuple-element.61), channel_id=1, source_target_pairs={{2,0},{3,1},{4,2},{5,3},{6,4},{7,5},{8,6},{9,7},{10,8},{11,9},{12,... | collective-permute-start | bytes 393224 | tf_op jit(solution)/shard_map/ppermute | solution.py:355
  24.0 7.5 %collective-permute-start.9 = (bf16[128,512]{1,0:T(8,128)(2,1)S(1)}, bf16[128,512]{1,0:T(8,128)(2,1)S(1)}, u32[]{:S(2)}, u32[]{:S(2)}) collective-permute-start(bf16[128,512]{1,0:T(8,128)(2,1)S(1)} %get-tuple-element.62), channel_id=1, source_target_pairs={{3,0},{2,1},{5,2},{4,3},{7,4},{6,5},{9,6},{8,7},{11,8},{10,9},{13,... | collective-permute-start | bytes 393224 | tf_op jit(solution)/shard_map/ppermute | solution.py:355
  25.0 3.5 %collective-permute-start.6 = (bf16[128,3072]{1,0:T(8,128)(2,1)S(1)}, bf16[128,3072]{1,0:T(8,128)(2,1)S(1)}, u32[]{:S(2)}, u32[]{:S(2)}) collective-permute-start(bf16[128,3072]{1,0:T(8,128)(2,1)S(1)} %sent_grads.1), channel_id=1, source_target_pairs={{0,1},{1,0},{2,3},{3,2},{4,5},{5,4},{6,7},{7,6},{8,9},{9,8},{10,11... | collective-permute-start | bytes 2359304 | tf_op jit(solution)/shard_map/ppermute | solution.py:355

commit v6 on v5

--- a/solution.py
+++ b/solution.py
@@ -381,7 +381,7 @@
         value_kernel, "value_grads", [pairs, narrow, narrow],
         index, bias, qm, gm, km, near, ka, kb,
     )
-    dvm, v2o = lax.optimization_barrier((dvm, v2o))
+    dvo, v2o = lax.optimization_barrier((dvo, v2o))
     dv_back = moved(dvm, behind), moved(dvo, recross)
     dscore, dkm, dko = run(
         key_kernel, "key_grads", [pairs, narrow, narrow],

time: 32.5 us -> 32.2 us (level); the launches traced: 32.4 us -> 31.6 us
  starting transfers between devices: 15.3 us -> 14.5 us
    ppermute x10, starting transfers between devices: 15.3 us -> 14.5 us  [moved(): return lax.ppermute(value, AXES, pairs)]
  transfers between devices with their start and end apart: 10 -> 10, of which waited for: 5 -> 7; matrix products, arithmetic and copies ran while one was open for 0% -> 0% of each run, Pallas kernels for 22% -> 22%
where the time goes in v6:
time: 32.2 us; the launch traced here: 31.6 us
  starting transfers between devices  14.5 us (45%)
  Pallas kernels  7.92 us (25%)
  waiting for transfers between devices  7.49 us (23%)
  local copies, waits for them, and re-layouts  0.96 us (3%)
  between operations  0.74 us (2%)
    ppermute x10, starting transfers between devices, moved(): return lax.ppermute(value, AXES, pairs)  14.5 us
    pallas_call x9, Pallas kernels, run(): pl.pallas_call(kernel, in_specs=[small] + [there if i in far else whole f...  7.92 us
    ppermute x10, waiting for transfers between devices, moved(): return lax.ppermute(value, AXES, pairs)  7.49 us
    unnamed x12, local copies, waits for them, and re-layouts  0.96 us
  transfers between devices with their start and end apart: 10, of which 7 were waited for; matrix products, arithmetic and copies ran while one was open for 0% of the time, Pallas kernels for 22%

profile of v6, /device:TPU:0, one launch (start us, length us, event | category | flops | bytes accessed | tf_op | source)
XLA Modules:
  0.0 31.6 jit_solution(18207371644420448128)
XLA Ops:
  0.6 0.9 %copy-done.2 = bf16[128,1024]{1,0:T(8,128)(2,1)S(1)} copy-done((bf16[128,1024]{1,0:T(8,128)(2,1)S(1)}, bf16[128,1024]{1,0:T(8,128)(2,1)}, u32[]{:S(2)}) %copy-start.2) | copy-done | bytes 262168
  1.7 3.0 %collective-permute-start.1 = (bf16[128,512]{1,0:T(8,128)(2,1)S(1)}, bf16[128,512]{1,0:T(8,128)(2,1)S(1)}, u32[]{:S(2)}, u32[]{:S(2)}) collective-permute-start(bf16[128,512]{1,0:T(8,128)(2,1)S(1)} %get-tuple-element.39.km), channel_id=1, source_target_pairs={{0,2},{1,3},{2,4},{3,5},{4,6},{5,7},{6,8},{7,9},{8,10},{9,11},{10,... | collective-permute-start | bytes 393224 | tf_op jit(solution)/shard_map/ppermute | solution.py:355
  4.7 0.7 %collective-permute-start.2 = (bf16[128,512]{1,0:T(8,128)(2,1)S(1)}, bf16[128,512]{1,0:T(8,128)(2,1)S(1)}, u32[]{:S(2)}, u32[]{:S(2)}) collective-permute-start(bf16[128,512]{1,0:T(8,128)(2,1)S(1)} %get-tuple-element.34), channel_id=1, source_target_pairs={{0,3},{1,2},{2,5},{3,4},{4,7},{5,6},{6,9},{7,8},{8,11},{9,10},{10,... | collective-permute-start | bytes 393224 | tf_op jit(solution)/shard_map/ppermute | solution.py:355
  5.4 0.4 %split_rows.1 = (bf16[128,1024]{1,0:T(8,128)(2,1)S(1)}, bf16[128,1024]{1,0:T(8,128)(2,1)S(1)}, bf16[128,512]{1,0:T(8,128)(2,1)S(1)}, bf16[128,512]{1,0:T(8,128)(...) custom-call(s32[1]{0:T(128)} %bitcast.rank_ref, s32[1,32]{1,0:T(1,128)S(1)} %bitcast.2, ...), custom_call_target="tpu_custom_call" | custom-call | bytes 1000 | tf_op jit(solution)/shard_map/split_rows/pallas_call | solution.py:330
  5.8 1.0 %collective-permute-start = (bf16[128,3072]{1,0:T(8,128)(2,1)S(1)}, bf16[128,3072]{1,0:T(8,128)(2,1)S(1)}, u32[]{:S(2)}, u32[]{:S(2)}) collective-permute-start(bf16[128,3072]{1,0:T(8,128)(2,1)S(1)} %get-tuple-element.40), channel_id=1, source_target_pairs={{0,1},{1,0},{2,3},{3,2},{4,5},{5,4},{6,7},{7,6},{8,9},{9,8},{10,11... | collective-permute-start | bytes 2359304 | tf_op jit(solution)/shard_map/ppermute | solution.py:355
  6.8 1.2 %collective-permute-start.3 = (bf16[128,512]{1,0:T(8,128)(2,1)S(1)}, bf16[128,512]{1,0:T(8,128)(2,1)S(1)}, u32[]{:S(2)}, u32[]{:S(2)}) collective-permute-start(bf16[128,512]{1,0:T(8,128)(2,1)S(1)} %get-tuple-element.45), channel_id=1, source_target_pairs={{0,3},{1,2},{2,5},{3,4},{4,7},{5,6},{6,9},{7,8},{8,11},{9,10},{10,... | collective-permute-start | bytes 393224 | tf_op jit(solution)/shard_map/ppermute | solution.py:355
  8.0 1.5 %collective-permute-start.5 = (bf16[128,512]{1,0:T(8,128)(2,1)S(1)}, bf16[128,512]{1,0:T(8,128)(2,1)S(1)}, u32[]{:S(2)}, u32[]{:S(2)}) collective-permute-start(bf16[128,512]{1,0:T(8,128)(2,1)S(1)} %get-tuple-element.48.vm), channel_id=1, source_target_pairs={{0,2},{1,3},{2,4},{3,5},{4,6},{5,7},{6,8},{7,9},{8,10},{9,11},{10,... | collective-permute-start | bytes 393224 | tf_op jit(solution)/shard_map/ppermute | solution.py:355
  9.5 3.5 %collective-permute-done.1.mine = bf16[128,512]{1,0:T(8,128)(2,1)S(1)} collective-permute-done((bf16[128,512]{1,0:T(8,128)(2,1)S(1)}, bf16[128,512]{1,0:T(8,128)(2,1)S(1)}, u32[]{:S(2)}, u32[]{:S(2)}) %collective-permute-start.1) | collective-permute-done | bytes 131104 | tf_op jit(solution)/shard_map/ppermute | solution.py:355
  13.0 1.1 %collective-permute-done.2.other = bf16[128,512]{1,0:T(8,128)(2,1)S(1)} collective-permute-done((bf16[128,512]{1,0:T(8,128)(2,1)S(1)}, bf16[128,512]{1,0:T(8,128)(2,1)S(1)}, u32[]{:S(2)}, u32[]{:S(2)}) %collective-permute-start.2) | collective-permute-done | bytes 131104 | tf_op jit(solution)/shard_map/ppermute | solution.py:355
  14.2 1.7 %value_grads.1 = (bf16[8,384,256]{2,1,0:T(8,128)(2,1)S(1)}, bf16[128,512]{1,0:T(8,128)(2,1)S(1)}, bf16[128,512]{1,0:T(8,128)(2,1)S(1)}) custom-call(s32[1]{0:T(128)} %bitcast.rank_ref, f32[2,384,128]{2,1,0:T(8,128)S(1)} %get-tuple-element.36.bias_ref, bf16[128,1024]{1,0:T(8,128)(2,1)S(1)} %get-tuple-element.37.qm, ...), custom_call_target="tpu_custom_call" | custom-call | bytes 1000 | tf_op jit(solution)/shard_map/value_grads/pallas_call | solution.py:330
  15.9 1.1 %collective-permute-done.3.v2o = bf16[128,512]{1,0:T(8,128)(2,1)S(1)} collective-permute-done((bf16[128,512]{1,0:T(8,128)(2,1)S(1)}, bf16[128,512]{1,0:T(8,128)(2,1)S(1)}, u32[]{:S(2)}, u32[]{:S(2)}) %collective-permute-start.3) | collective-permute-done | bytes 131104 | tf_op jit(solution)/shard_map/ppermute | solution.py:355
  17.0 3.1 %collective-permute-start.4 = (bf16[128,512]{1,0:T(8,128)(2,1)S(1)}, bf16[128,512]{1,0:T(8,128)(2,1)S(1)}, u32[]{:S(2)}, u32[]{:S(2)}) collective-permute-start(bf16[128,512]{1,0:T(8,128)(2,1)S(1)} %get-tuple-element.46), channel_id=1, source_target_pairs={{3,0},{2,1},{5,2},{4,3},{7,4},{6,5},{9,6},{8,7},{11,8},{10,9},{13,... | collective-permute-start | bytes 393224 | tf_op jit(solution)/shard_map/ppermute | solution.py:355
  20.1 1.0 %collective-permute-start.7 = (bf16[128,512]{1,0:T(8,128)(2,1)S(1)}, bf16[128,512]{1,0:T(8,128)(2,1)S(1)}, u32[]{:S(2)}, u32[]{:S(2)}) collective-permute-start(bf16[128,512]{1,0:T(8,128)(2,1)S(1)} %get-tuple-element.51), channel_id=1, source_target_pairs={{2,0},{3,1},{4,2},{5,3},{6,4},{7,5},{8,6},{9,7},{10,8},{11,9},{12,... | collective-permute-start | bytes 393224 | tf_op jit(solution)/shard_map/ppermute | solution.py:355
  21.1 1.6 %key_grads.1 = (bf16[8,384,256]{2,1,0:T(8,128)(2,1)S(1)}, bf16[128,512]{1,0:T(8,128)(2,1)S(1)}, bf16[128,512]{1,0:T(8,128)(2,1)S(1)}) custom-call(s32[1]{0:T(128)} %bitcast.rank_ref, bf16[8,384,256]{2,1,0:T(8,128)(2,1)S(1)} %get-tuple-element.47.prob_ref, bf16[128,1024]{1,0:T(8,128)(2,1)S(1)} %get-tuple-element.37.qm, ...), custom_call_target="tpu_custom_call" | custom-call | bytes 1000 | tf_op jit(solution)/shard_map/key_grads/pallas_call | solution.py:330
  22.7 1.3 %collective-permute-start.8 = (bf16[128,512]{1,0:T(8,128)(2,1)S(1)}, bf16[128,512]{1,0:T(8,128)(2,1)S(1)}, u32[]{:S(2)}, u32[]{:S(2)}) collective-permute-start(bf16[128,512]{1,0:T(8,128)(2,1)S(1)} %get-tuple-element.61), channel_id=1, source_target_pairs={{2,0},{3,1},{4,2},{5,3},{6,4},{7,5},{8,6},{9,7},{10,8},{11,9},{12,... | collective-permute-start | bytes 393224 | tf_op jit(solution)/shard_map/ppermute | solution.py:355
  24.1 0.9 %sent_grads.1 = bf16[128,3072]{1,0:T(8,128)(2,1)S(1)} custom-call(s32[1]{0:T(128)} %bitcast.rank_ref, bf16[8,384,256]{2,1,0:T(8,128)(2,1)S(1)} %get-tuple-element.47.prob_ref, bf16[8,384,256]{2,1,0:T(8,128)(2,1)S(1)} %get-tuple-element.50.dscore_ref, bf16[128,1024]{1,0:T(8,128)(2,1)S(1)} %get-tuple-element.37.qm, ...), custom_call_target="tpu_custom_call" | custom-call | bytes 1000 | tf_op jit(solution)/shard_map/sent_grads/pallas_call | solution.py:330
  25.0 1.5 %collective-permute-start.6 = (bf16[128,3072]{1,0:T(8,128)(2,1)S(1)}, bf16[128,3072]{1,0:T(8,128)(2,1)S(1)}, u32[]{:S(2)}, u32[]{:S(2)}) collective-permute-start(bf16[128,3072]{1,0:T(8,128)(2,1)S(1)} %sent_grads.1), channel_id=1, source_target_pairs={{0,1},{1,0},{2,3},{3,2},{4,5},{5,4},{6,7},{7,6},{8,9},{9,8},{10,11... | collective-permute-start | bytes 2359304 | tf_op jit(solution)/shard_map/ppermute | solution.py:355
  26.6 0.7 %collective-permute-done.7.backm = bf16[128,512]{1,0:T(8,128)(2,1)S(1)} collective-permute-done((bf16[128,512]{1,0:T(8,128)(2,1)S(1)}, bf16[128,512]{1,0:T(8,128)(2,1)S(1)}, u32[]{:S(2)}, u32[]{:S(2)}) %collective-permute-start.7) | collective-permute-done | bytes 131104 | tf_op jit(solution)/shard_map/ppermute | solution.py:355
  27.3 0.9 %own_grads.1 = (bf16[128,1024]{1,0:T(8,128)(2,1)S(1)}, f32[128,1024]{1,0:T(8,128)S(1)}, f32[128,512]{1,0:T(8,128)S(1)}, f32[128,512]{1,0:T(8,128)S(1)}) custom-call(s32[1]{0:T(128)} %bitcast.rank_ref, bf16[8,384,256]{2,1,0:T(8,128)(2,1)S(1)} %get-tuple-element.47.prob_ref, bf16[8,384,256]{2,1,0:T(8,128)(2,1)S(1)} %get-tuple-element.50.dscore_ref, ...), custom_call_target="tpu_custom_call" | custom-call | flops 20000000000 | bytes 1000 | tf_op jit(solution)/shard_map/own_grads/pallas_call | solution.py:330
  28.2 0.3 collective-permute-done.6.got.near
  28.5 1.4 %join_rows.1 = (bf16[128,2048]{1,0:T(8,128)(2,1)}, f32[128,2048]{1,0:T(8,128)}, f32[128,1024]{1,0:T(8,128)}) custom-call(s32[1]{0:T(128)} %bitcast.rank_ref, bf16[128,3072]{1,0:T(8,128)(2,1)S(1)} %collective-permute-done.6.got.near, bf16[128,1024]{1,0:T(8,128)(2,1)S(1)} %get-tuple-element.54.outm, f32[128,1024]{1,0:T(8,128)S(1)} %get-tuple-element.55.dqm, ...), custom_call_target="tpu_custom_call" | custom-call | bytes 1000 | tf_op jit(solution)/shard_map/join_rows/pallas_call | solution.py:330
  29.9 0.2 collective-permute-done.8.backm
  30.1 0.7 %collective-permute-done.9.backo = bf16[128,512]{1,0:T(8,128)(2,1)S(1)} collective-permute-done((bf16[128,512]{1,0:T(8,128)(2,1)S(1)}, bf16[128,512]{1,0:T(8,128)(2,1)S(1)}, u32[]{:S(2)}, u32[]{:S(2)}) %collective-permute-start.9) | collective-permute-done | bytes 131104 | tf_op jit(solution)/shard_map/ppermute | solution.py:355
  30.8 0.8 %join_keys.1 = f32[128,1024]{1,0:T(8,128)} custom-call(s32[1]{0:T(128)} %bitcast.rank_ref, f32[128,512]{1,0:T(8,128)S(1)} %get-tuple-element.60.mine, bf16[128,3072]{1,0:T(8,128)(2,1)S(1)} %collective-permute-done.6.got.near, bf16[128,512]{1,0:T(8,128)(2,1)S(1)} %collective-permute-done.8.backm, bf16[128,512]{1,0:T(8,128)(2,1)S(1)} %collective-permute-done.9.backo), custom_call_target="tpu_custom_call" | custom-call | bytes 1000 | tf_op jit(solution)/shard_map/join_keys/pallas_call | solution.py:330
  (17 shorter events, 0.2 us)
Async XLA Ops:
  0.6 1.0 %copy-start.2 = (bf16[128,1024]{1,0:T(8,128)(2,1)S(1)}, bf16[128,1024]{1,0:T(8,128)(2,1)}, u32[]{:S(2)}) copy-start(bf16[128,1024]{1,0:T(8,128)(2,1)} %k_ref.1) | copy-start | bytes 786436
  1.6 3.8 %copy-start = (bf16[128,2048]{1,0:T(8,128)(2,1)S(1)}, bf16[128,2048]{1,0:T(8,128)(2,1)}, u32[]{:S(2)}) copy-start(bf16[128,2048]{1,0:T(8,128)(2,1)} %q_ref) | copy-start | bytes 1572868
  1.6 3.8 %copy-start.1 = (bf16[128,2048]{1,0:T(8,128)(2,1)S(1)}, bf16[128,2048]{1,0:T(8,128)(2,1)}, u32[]{:S(2)}) copy-start(bf16[128,2048]{1,0:T(8,128)(2,1)} %g_ref.1) | copy-start | bytes 1572868
  1.6 3.8 %copy-start.3 = (bf16[128,1024]{1,0:T(8,128)(2,1)S(1)}, bf16[128,1024]{1,0:T(8,128)(2,1)}, u32[]{:S(2)}) copy-start(bf16[128,1024]{1,0:T(8,128)(2,1)} %k_ref.1) | copy-start | bytes 786436
  1.6 3.8 %copy-start.4 = (bf16[128,1024]{1,0:T(8,128)(2,1)S(1)}, bf16[128,1024]{1,0:T(8,128)(2,1)}, u32[]{:S(2)}) copy-start(bf16[128,1024]{1,0:T(8,128)(2,1)} %v_ref.1) | copy-start | bytes 786436
  1.6 3.8 %copy-start.5 = (s32[32]{0:T(128)S(1)}, s32[32]{0:T(128)}, u32[]{:S(2)}) copy-start(s32[32]{0:T(128)} %param.9) | copy-start | bytes 388
  1.7 11.3 %collective-permute-start.1 = (bf16[128,512]{1,0:T(8,128)(2,1)S(1)}, bf16[128,512]{1,0:T(8,128)(2,1)S(1)}, u32[]{:S(2)}, u32[]{:S(2)}) collective-permute-start(bf16[128,512]{1,0:T(8,128)(2,1)S(1)} %get-tuple-element.39.km), channel_id=1, source_target_pairs={{0,2},{1,3},{2,4},{3,5},{4,6},{5,7},{6,8},{7,9},{8,10},{9,11},{10,... | collective-permute-start | bytes 393224 | tf_op jit(solution)/shard_map/ppermute | solution.py:355
  4.7 9.4 %collective-permute-start.2 = (bf16[128,512]{1,0:T(8,128)(2,1)S(1)}, bf16[128,512]{1,0:T(8,128)(2,1)S(1)}, u32[]{:S(2)}, u32[]{:S(2)}) collective-permute-start(bf16[128,512]{1,0:T(8,128)(2,1)S(1)} %get-tuple-element.34), channel_id=1, source_target_pairs={{0,3},{1,2},{2,5},{3,4},{4,7},{5,6},{6,9},{7,8},{8,11},{9,10},{10,... | collective-permute-start | bytes 393224 | tf_op jit(solution)/shard_map/ppermute | solution.py:355
  5.8 8.4 %collective-permute-start = (bf16[128,3072]{1,0:T(8,128)(2,1)S(1)}, bf16[128,3072]{1,0:T(8,128)(2,1)S(1)}, u32[]{:S(2)}, u32[]{:S(2)}) collective-permute-start(bf16[128,3072]{1,0:T(8,128)(2,1)S(1)} %get-tuple-element.40), channel_id=1, source_target_pairs={{0,1},{1,0},{2,3},{3,2},{4,5},{5,4},{6,7},{7,6},{8,9},{9,8},{10,11... | collective-permute-start | bytes 2359304 | tf_op jit(solution)/shard_map/ppermute | solution.py:355
  6.8 10.1 %collective-permute-start.3 = (bf16[128,512]{1,0:T(8,128)(2,1)S(1)}, bf16[128,512]{1,0:T(8,128)(2,1)S(1)}, u32[]{:S(2)}, u32[]{:S(2)}) collective-permute-start(bf16[128,512]{1,0:T(8,128)(2,1)S(1)} %get-tuple-element.45), channel_id=1, source_target_pairs={{0,3},{1,2},{2,5},{3,4},{4,7},{5,6},{6,9},{7,8},{8,11},{9,10},{10,... | collective-permute-start | bytes 393224 | tf_op jit(solution)/shard_map/ppermute | solution.py:355
  8.0 13.1 %collective-permute-start.5 = (bf16[128,512]{1,0:T(8,128)(2,1)S(1)}, bf16[128,512]{1,0:T(8,128)(2,1)S(1)}, u32[]{:S(2)}, u32[]{:S(2)}) collective-permute-start(bf16[128,512]{1,0:T(8,128)(2,1)S(1)} %get-tuple-element.48.vm), channel_id=1, source_target_pairs={{0,2},{1,3},{2,4},{3,5},{4,6},{5,7},{6,8},{7,9},{8,10},{9,11},{10,... | collective-permute-start | bytes 393224 | tf_op jit(solution)/shard_map/ppermute | solution.py:355
  17.0 7.2 %collective-permute-start.4 = (bf16[128,512]{1,0:T(8,128)(2,1)S(1)}, bf16[128,512]{1,0:T(8,128)(2,1)S(1)}, u32[]{:S(2)}, u32[]{:S(2)}) collective-permute-start(bf16[128,512]{1,0:T(8,128)(2,1)S(1)} %get-tuple-element.46), channel_id=1, source_target_pairs={{3,0},{2,1},{5,2},{4,3},{7,4},{6,5},{9,6},{8,7},{11,8},{10,9},{13,... | collective-permute-start | bytes 393224 | tf_op jit(solution)/shard_map/ppermute | solution.py:355
  20.1 7.2 %collective-permute-start.7 = (bf16[128,512]{1,0:T(8,128)(2,1)S(1)}, bf16[128,512]{1,0:T(8,128)(2,1)S(1)}, u32[]{:S(2)}, u32[]{:S(2)}) collective-permute-start(bf16[128,512]{1,0:T(8,128)(2,1)S(1)} %get-tuple-element.51), channel_id=1, source_target_pairs={{2,0},{3,1},{4,2},{5,3},{6,4},{7,5},{8,6},{9,7},{10,8},{11,9},{12,... | collective-permute-start | bytes 393224 | tf_op jit(solution)/shard_map/ppermute | solution.py:355
  22.7 7.4 %collective-permute-start.8 = (bf16[128,512]{1,0:T(8,128)(2,1)S(1)}, bf16[128,512]{1,0:T(8,128)(2,1)S(1)}, u32[]{:S(2)}, u32[]{:S(2)}) collective-permute-start(bf16[128,512]{1,0:T(8,128)(2,1)S(1)} %get-tuple-element.61), channel_id=1, source_target_pairs={{2,0},{3,1},{4,2},{5,3},{6,4},{7,5},{8,6},{9,7},{10,8},{11,9},{12,... | collective-permute-start | bytes 393224 | tf_op jit(solution)/shard_map/ppermute | solution.py:355
  24.0 6.7 %collective-permute-start.9 = (bf16[128,512]{1,0:T(8,128)(2,1)S(1)}, bf16[128,512]{1,0:T(8,128)(2,1)S(1)}, u32[]{:S(2)}, u32[]{:S(2)}) collective-permute-start(bf16[128,512]{1,0:T(8,128)(2,1)S(1)} %get-tuple-element.62), channel_id=1, source_target_pairs={{3,0},{2,1},{5,2},{4,3},{7,4},{6,5},{9,6},{8,7},{11,8},{10,9},{13,... | collective-permute-start | bytes 393224 | tf_op jit(solution)/shard_map/ppermute | solution.py:355
  25.0 3.4 %collective-permute-start.6 = (bf16[128,3072]{1,0:T(8,128)(2,1)S(1)}, bf16[128,3072]{1,0:T(8,128)(2,1)S(1)}, u32[]{:S(2)}, u32[]{:S(2)}) collective-permute-start(bf16[128,3072]{1,0:T(8,128)(2,1)S(1)} %sent_grads.1), channel_id=1, source_target_pairs={{0,1},{1,0},{2,3},{3,2},{4,5},{5,4},{6,7},{7,6},{8,9},{9,8},{10,11... | collective-permute-start | bytes 2359304 | tf_op jit(solution)/shard_map/ppermute | solution.py:355

commit v7 on v6

--- a/solution.py
+++ b/solution.py
@@ -126,7 +126,11 @@
         copy.wait()
 
 
-def order_kernel(rank_ref, mine, other, first, second):
+def mark_kernel(rank_ref, source, target):
+    target[...] = source[: target.shape[0], : target.shape[1]]
+
+
+def order_kernel(rank_ref, mine, other, mark, first, second):
     odd = rank_ref[0] % 2
     for core in range(CORES):
 
@@ -207,8 +211,17 @@
     return total + jnp.where(odd, dot(pairs_ref[here + 1, rows : 2 * rows], sources[1]), 0.0)
 
 
+def near_kernel(rank_ref, gm, vm, near, dprob_ref):
+    rows = gm.shape[0]
+    odd = rank_ref[0] % 2 == 1
+    for head, block in UNITS:
+        values = jnp.concatenate(both(odd, vm, near, head, AT_VALUES)[: block + 1], axis=0)
+        gradients = stacked(odd, gm, near, head, AT_GRADIENTS)[block]
+        dprob_ref[head * CORES + block, : (block + 1) * rows] = dot_last(values, gradients)
+
+
 def key_kernel(
-    rank_ref, prob_ref, qm, gm, vm, near, v2m, v2o,
+    rank_ref, near_dprob, prob_ref, qm, gm, vm, near, v2m, v2o,
     dscore_ref, dkm, dko,
 ):
     rows = qm.shape[0]
@@ -220,8 +233,9 @@
 
     def product(head, block):
         gradients = stacked(odd, gm, near, head, AT_GRADIENTS)[block]
-        values = jnp.concatenate(value_blocks(head)[block : block + 3], axis=0)
-        return (dot_last(values, gradients),)
+        values = jnp.concatenate(both(odd, v2m, v2o, head)[block:], axis=0)
+        far = dot_last(values, gradients)
+        return (jnp.concatenate([far, near_dprob[head * CORES + block, : (block + 1) * rows]], axis=0),)
 
     def scale(head, block, dprob):
         at = head * CORES + block
@@ -376,16 +390,22 @@
     )
     v2m, v2o = moved(vm, ahead), moved(vx, across)
     near = moved(sent, swap)
-    ka, kb = run(order_kernel, "far_keys", [narrow] * 2, index, k2m, k2o)
+    (mark,) = run(mark_kernel, "mark", [shape((16, HEAD_SIZE), jnp.bfloat16)], index, k2m)
+    ka, kb = run(order_kernel, "far_keys", [narrow] * 2, index, k2m, k2o, mark)
     prob, dvm, dvo = run(
         value_kernel, "value_grads", [pairs, narrow, narrow],
         index, bias, qm, gm, km, near, ka, kb,
     )
-    dvo, v2o = lax.optimization_barrier((dvo, v2o))
+    later_rows, dvm, dvo = lax.optimization_barrier((gm, dvm, dvo))
+    (near_dprob,) = run(
+        near_kernel, "near_values", [shape((KEY_VALUE_HEADS, 2 * rows, GROUP * rows), jnp.float32)],
+        index, later_rows, vm, near,
+    )
+    dvo, v2o, near_dprob = lax.optimization_barrier((dvo, v2o, near_dprob))
     dv_back = moved(dvm, behind), moved(dvo, recross)
     dscore, dkm, dko = run(
         key_kernel, "key_grads", [pairs, narrow, narrow],
-        index, prob, qm, gm, vm, near, v2m, v2o,
+        index, near_dprob, prob, qm, gm, vm, near, v2m, v2o,
     )
     dk_back = moved(dkm, behind), moved(dko, recross)
     prob, dv_back1 = lax.optimization_barrier((prob, dv_back[1]))

time: 32.2 us -> 32.2 us (level)
  Pallas kernels: 7.92 us -> 8.26 us
    pallas_call x9 -> x11, Pallas kernels: 7.92 us -> 8.26 us  [run(): pl.pallas_call(kernel, in_specs=[small] + [there if i in far else whole f...]
  transfers between devices with their start and end apart: 10 -> 10, of which waited for: 7 -> 7; matrix products, arithmetic and copies ran while one was open for 0% -> 0% of each run, Pallas kernels for 22% -> 23%
where the time goes in v7:
time: 32.2 us; the launch traced here: 31.6 us
  starting transfers between devices  14.4 us (45%)
  Pallas kernels  8.26 us (26%)
  waiting for transfers between devices  7.23 us (22%)
  local copies, waits for them, and re-layouts  0.96 us (3%)
  between operations  0.75 us (2%)
    ppermute x10, starting transfers between devices, moved(): return lax.ppermute(value, AXES, pairs)  14.4 us
    pallas_call x11, Pallas kernels, run(): pl.pallas_call(kernel, in_specs=[small] + [there if i in far else whole f...  8.26 us
    ppermute x10, waiting for transfers between devices, moved(): return lax.ppermute(value, AXES, pairs)  7.23 us
    unnamed x12, local copies, waits for them, and re-layouts  0.96 us
  transfers between devices with their start and end apart: 10, of which 7 were waited for; matrix products, arithmetic and copies ran while one was open for 0% of the time, Pallas kernels for 23%

profile of v7, /device:TPU:0, one launch (start us, length us, event | category | flops | bytes accessed | tf_op | source)
XLA Modules:
  0.0 31.6 jit_solution(10285586164149555184)
XLA Ops:
  0.6 0.9 %copy-done.2 = bf16[128,1024]{1,0:T(8,128)(2,1)S(1)} copy-done((bf16[128,1024]{1,0:T(8,128)(2,1)S(1)}, bf16[128,1024]{1,0:T(8,128)(2,1)}, u32[]{:S(2)}) %copy-start.2) | copy-done | bytes 262168
  1.7 3.0 %collective-permute-start.1 = (bf16[128,512]{1,0:T(8,128)(2,1)S(1)}, bf16[128,512]{1,0:T(8,128)(2,1)S(1)}, u32[]{:S(2)}, u32[]{:S(2)}) collective-permute-start(bf16[128,512]{1,0:T(8,128)(2,1)S(1)} %get-tuple-element.43.km), channel_id=1, source_target_pairs={{0,2},{1,3},{2,4},{3,5},{4,6},{5,7},{6,8},{7,9},{8,10},{9,11},{10,... | collective-permute-start | bytes 393224 | tf_op jit(solution)/shard_map/ppermute | solution.py:369
  4.7 0.7 %collective-permute-start.2 = (bf16[128,512]{1,0:T(8,128)(2,1)S(1)}, bf16[128,512]{1,0:T(8,128)(2,1)S(1)}, u32[]{:S(2)}, u32[]{:S(2)}) collective-permute-start(bf16[128,512]{1,0:T(8,128)(2,1)S(1)} %get-tuple-element.38), channel_id=1, source_target_pairs={{0,3},{1,2},{2,5},{3,4},{4,7},{5,6},{6,9},{7,8},{8,11},{9,10},{10,... | collective-permute-start | bytes 393224 | tf_op jit(solution)/shard_map/ppermute | solution.py:369
  5.4 0.4 %split_rows.1 = (bf16[128,1024]{1,0:T(8,128)(2,1)S(1)}, bf16[128,1024]{1,0:T(8,128)(2,1)S(1)}, bf16[128,512]{1,0:T(8,128)(2,1)S(1)}, bf16[128,512]{1,0:T(8,128)(...) custom-call(s32[1]{0:T(128)} %bitcast.rank_ref, s32[1,32]{1,0:T(1,128)S(1)} %bitcast.2, ...), custom_call_target="tpu_custom_call" | custom-call | bytes 1000 | tf_op jit(solution)/shard_map/split_rows/pallas_call | solution.py:344
  5.8 2.1 %collective-permute-start.3 = (bf16[128,512]{1,0:T(8,128)(2,1)S(1)}, bf16[128,512]{1,0:T(8,128)(2,1)S(1)}, u32[]{:S(2)}, u32[]{:S(2)}) collective-permute-start(bf16[128,512]{1,0:T(8,128)(2,1)S(1)} %get-tuple-element.51), channel_id=1, source_target_pairs={{0,3},{1,2},{2,5},{3,4},{4,7},{5,6},{6,9},{7,8},{8,11},{9,10},{10,... | collective-permute-start | bytes 393224 | tf_op jit(solution)/shard_map/ppermute | solution.py:369
  7.9 1.5 %collective-permute-start.5 = (bf16[128,512]{1,0:T(8,128)(2,1)S(1)}, bf16[128,512]{1,0:T(8,128)(2,1)S(1)}, u32[]{:S(2)}, u32[]{:S(2)}) collective-permute-start(bf16[128,512]{1,0:T(8,128)(2,1)S(1)} %get-tuple-element.53.vm), channel_id=1, source_target_pairs={{0,2},{1,3},{2,4},{3,5},{4,6},{5,7},{6,8},{7,9},{8,10},{9,11},{10,... | collective-permute-start | bytes 393224 | tf_op jit(solution)/shard_map/ppermute | solution.py:369
  9.5 3.5 %collective-permute-done.1.source.mine = bf16[128,512]{1,0:T(8,128)(2,1)S(1)} collective-permute-done((bf16[128,512]{1,0:T(8,128)(2,1)S(1)}, bf16[128,512]{1,0:T(8,128)(2,1)S(1)}, u32[]{:S(2)}, u32[]{:S(2)}) %collective-permute-start.1) | collective-permute-done | bytes 131104 | tf_op jit(solution)/shard_map/ppermute | solution.py:369
  13.0 1.1 %collective-permute-done.2.other = bf16[128,512]{1,0:T(8,128)(2,1)S(1)} collective-permute-done((bf16[128,512]{1,0:T(8,128)(2,1)S(1)}, bf16[128,512]{1,0:T(8,128)(2,1)S(1)}, u32[]{:S(2)}, u32[]{:S(2)}) %collective-permute-start.2) | collective-permute-done | bytes 131104 | tf_op jit(solution)/shard_map/ppermute | solution.py:369
  14.2 1.7 %value_grads.1 = (bf16[8,384,256]{2,1,0:T(8,128)(2,1)S(1)}, bf16[128,512]{1,0:T(8,128)(2,1)S(1)}, bf16[128,512]{1,0:T(8,128)(2,1)S(1)}) custom-call(s32[1]{0:T(128)} %bitcast.rank_ref, f32[2,384,128]{2,1,0:T(8,128)S(1)} %get-tuple-element.40.bias_ref, bf16[128,1024]{1,0:T(8,128)(2,1)S(1)} %get-tuple-element.41.qm, ...), custom_call_target="tpu_custom_call" | custom-call | bytes 1000 | tf_op jit(solution)/shard_map/value_grads/pallas_call | solution.py:344
  15.9 0.4 %near_values.1.near_dprob = f32[8,256,256]{2,1,0:T(8,128)S(1)} custom-call(s32[1]{0:T(128)} %bitcast.rank_ref, bf16[128,1024]{1,0:T(8,128)(2,1)S(1)} %get-tuple-element.52.gm, bf16[128,512]{1,0:T(8,128)(2,1)S(1)} %get-tuple-element.53.vm, bf16[128,3072]{1,0:T(8,128)(2,1)S(1)} %collective-permute-done.near), custom_call_target="tpu_custom_call" | custom-call | bytes 1000 | tf_op jit(solution)/shard_map/near_values/pallas_call | solution.py:344
  16.3 0.7 %collective-permute-done.3.v2o = bf16[128,512]{1,0:T(8,128)(2,1)S(1)} collective-permute-done((bf16[128,512]{1,0:T(8,128)(2,1)S(1)}, bf16[128,512]{1,0:T(8,128)(2,1)S(1)}, u32[]{:S(2)}, u32[]{:S(2)}) %collective-permute-start.3) | collective-permute-done | bytes 131104 | tf_op jit(solution)/shard_map/ppermute | solution.py:369
  17.0 3.1 %collective-permute-start.4 = (bf16[128,512]{1,0:T(8,128)(2,1)S(1)}, bf16[128,512]{1,0:T(8,128)(2,1)S(1)}, u32[]{:S(2)}, u32[]{:S(2)}) collective-permute-start(bf16[128,512]{1,0:T(8,128)(2,1)S(1)} %get-tuple-element.54), channel_id=1, source_target_pairs={{3,0},{2,1},{5,2},{4,3},{7,4},{6,5},{9,6},{8,7},{11,8},{10,9},{13,... | collective-permute-start | bytes 393224 | tf_op jit(solution)/shard_map/ppermute | solution.py:369
  20.1 1.0 %collective-permute-start.7 = (bf16[128,512]{1,0:T(8,128)(2,1)S(1)}, bf16[128,512]{1,0:T(8,128)(2,1)S(1)}, u32[]{:S(2)}, u32[]{:S(2)}) collective-permute-start(bf16[128,512]{1,0:T(8,128)(2,1)S(1)} %get-tuple-element.59), channel_id=1, source_target_pairs={{2,0},{3,1},{4,2},{5,3},{6,4},{7,5},{8,6},{9,7},{10,8},{11,9},{12,... | collective-permute-start | bytes 393224 | tf_op jit(solution)/shard_map/ppermute | solution.py:369
  21.1 1.6 %key_grads.1 = (bf16[8,384,256]{2,1,0:T(8,128)(2,1)S(1)}, bf16[128,512]{1,0:T(8,128)(2,1)S(1)}, bf16[128,512]{1,0:T(8,128)(2,1)S(1)}) custom-call(s32[1]{0:T(128)} %bitcast.rank_ref, f32[8,256,256]{2,1,0:T(8,128)S(1)} %near_values.1.near_dprob, bf16[8,384,256]{2,1,0:T(8,128)(2,1)S(1)} %get-tuple-element.55.prob_ref, ...), custom_call_target="tpu_custom_call" | custom-call | bytes 1000 | tf_op jit(solution)/shard_map/key_grads/pallas_call | solution.py:344
  22.7 1.3 %collective-permute-start.8 = (bf16[128,512]{1,0:T(8,128)(2,1)S(1)}, bf16[128,512]{1,0:T(8,128)(2,1)S(1)}, u32[]{:S(2)}, u32[]{:S(2)}) collective-permute-start(bf16[128,512]{1,0:T(8,128)(2,1)S(1)} %get-tuple-element.69), channel_id=1, source_target_pairs={{2,0},{3,1},{4,2},{5,3},{6,4},{7,5},{8,6},{9,7},{10,8},{11,9},{12,... | collective-permute-start | bytes 393224 | tf_op jit(solution)/shard_map/ppermute | solution.py:369
  24.1 0.9 %sent_grads.1 = bf16[128,3072]{1,0:T(8,128)(2,1)S(1)} custom-call(s32[1]{0:T(128)} %bitcast.rank_ref, bf16[8,384,256]{2,1,0:T(8,128)(2,1)S(1)} %get-tuple-element.55.prob_ref, bf16[8,384,256]{2,1,0:T(8,128)(2,1)S(1)} %get-tuple-element.58.dscore_ref, bf16[128,1024]{1,0:T(8,128)(2,1)S(1)} %get-tuple-element.41.qm, ...), custom_call_target="tpu_custom_call" | custom-call | bytes 1000 | tf_op jit(solution)/shard_map/sent_grads/pallas_call | solution.py:344
  25.0 1.5 %collective-permute-start.6 = (bf16[128,3072]{1,0:T(8,128)(2,1)S(1)}, bf16[128,3072]{1,0:T(8,128)(2,1)S(1)}, u32[]{:S(2)}, u32[]{:S(2)}) collective-permute-start(bf16[128,3072]{1,0:T(8,128)(2,1)S(1)} %sent_grads.1), channel_id=1, source_target_pairs={{0,1},{1,0},{2,3},{3,2},{4,5},{5,4},{6,7},{7,6},{8,9},{9,8},{10,11... | collective-permute-start | bytes 2359304 | tf_op jit(solution)/shard_map/ppermute | solution.py:369
  26.5 0.8 %collective-permute-done.7.backm = bf16[128,512]{1,0:T(8,128)(2,1)S(1)} collective-permute-done((bf16[128,512]{1,0:T(8,128)(2,1)S(1)}, bf16[128,512]{1,0:T(8,128)(2,1)S(1)}, u32[]{:S(2)}, u32[]{:S(2)}) %collective-permute-start.7) | collective-permute-done | bytes 131104 | tf_op jit(solution)/shard_map/ppermute | solution.py:369
  27.3 0.9 %own_grads.1 = (bf16[128,1024]{1,0:T(8,128)(2,1)S(1)}, f32[128,1024]{1,0:T(8,128)S(1)}, f32[128,512]{1,0:T(8,128)S(1)}, f32[128,512]{1,0:T(8,128)S(1)}) custom-call(s32[1]{0:T(128)} %bitcast.rank_ref, bf16[8,384,256]{2,1,0:T(8,128)(2,1)S(1)} %get-tuple-element.55.prob_ref, bf16[8,384,256]{2,1,0:T(8,128)(2,1)S(1)} %get-tuple-element.58.dscore_ref, ...), custom_call_target="tpu_custom_call" | custom-call | flops 20000000000 | bytes 1000 | tf_op jit(solution)/shard_map/own_grads/pallas_call | solution.py:344
  28.2 0.2 collective-permute-done.6.got.near
  28.4 1.5 %join_rows.1 = (bf16[128,2048]{1,0:T(8,128)(2,1)}, f32[128,2048]{1,0:T(8,128)}, f32[128,1024]{1,0:T(8,128)}) custom-call(s32[1]{0:T(128)} %bitcast.rank_ref, bf16[128,3072]{1,0:T(8,128)(2,1)S(1)} %collective-permute-done.6.got.near, bf16[128,1024]{1,0:T(8,128)(2,1)S(1)} %get-tuple-element.62.outm, f32[128,1024]{1,0:T(8,128)S(1)} %get-tuple-element.63.dqm, ...), custom_call_target="tpu_custom_call" | custom-call | bytes 1000 | tf_op jit(solution)/shard_map/join_rows/pallas_call | solution.py:344
  29.9 0.2 collective-permute-done.8.backm
  30.1 0.7 %collective-permute-done.9.backo = bf16[128,512]{1,0:T(8,128)(2,1)S(1)} collective-permute-done((bf16[128,512]{1,0:T(8,128)(2,1)S(1)}, bf16[128,512]{1,0:T(8,128)(2,1)S(1)}, u32[]{:S(2)}, u32[]{:S(2)}) %collective-permute-start.9) | collective-permute-done | bytes 131104 | tf_op jit(solution)/shard_map/ppermute | solution.py:369
  30.8 0.8 %join_keys.1 = f32[128,1024]{1,0:T(8,128)} custom-call(s32[1]{0:T(128)} %bitcast.rank_ref, f32[128,512]{1,0:T(8,128)S(1)} %get-tuple-element.68.mine, bf16[128,3072]{1,0:T(8,128)(2,1)S(1)} %collective-permute-done.6.got.near, bf16[128,512]{1,0:T(8,128)(2,1)S(1)} %collective-permute-done.8.backm, bf16[128,512]{1,0:T(8,128)(2,1)S(1)} %collective-permute-done.9.backo), custom_call_target="tpu_custom_call" | custom-call | bytes 1000 | tf_op jit(solution)/shard_map/join_keys/pallas_call | solution.py:344
  (19 shorter events, 0.2 us)
Async XLA Ops:
  0.6 1.0 %copy-start.2 = (bf16[128,1024]{1,0:T(8,128)(2,1)S(1)}, bf16[128,1024]{1,0:T(8,128)(2,1)}, u32[]{:S(2)}) copy-start(bf16[128,1024]{1,0:T(8,128)(2,1)} %k_ref.1) | copy-start | bytes 786436
  1.6 3.8 %copy-start = (bf16[128,2048]{1,0:T(8,128)(2,1)S(1)}, bf16[128,2048]{1,0:T(8,128)(2,1)}, u32[]{:S(2)}) copy-start(bf16[128,2048]{1,0:T(8,128)(2,1)} %q_ref) | copy-start | bytes 1572868
  1.6 3.8 %copy-start.1 = (bf16[128,2048]{1,0:T(8,128)(2,1)S(1)}, bf16[128,2048]{1,0:T(8,128)(2,1)}, u32[]{:S(2)}) copy-start(bf16[128,2048]{1,0:T(8,128)(2,1)} %g_ref.1) | copy-start | bytes 1572868
  1.6 3.8 %copy-start.3 = (bf16[128,1024]{1,0:T(8,128)(2,1)S(1)}, bf16[128,1024]{1,0:T(8,128)(2,1)}, u32[]{:S(2)}) copy-start(bf16[128,1024]{1,0:T(8,128)(2,1)} %k_ref.1) | copy-start | bytes 786436
  1.6 3.8 %copy-start.4 = (bf16[128,1024]{1,0:T(8,128)(2,1)S(1)}, bf16[128,1024]{1,0:T(8,128)(2,1)}, u32[]{:S(2)}) copy-start(bf16[128,1024]{1,0:T(8,128)(2,1)} %v_ref.1) | copy-start | bytes 786436
  1.6 3.8 %copy-start.5 = (s32[32]{0:T(128)S(1)}, s32[32]{0:T(128)}, u32[]{:S(2)}) copy-start(s32[32]{0:T(128)} %param.9) | copy-start | bytes 388
  1.7 11.3 %collective-permute-start.1 = (bf16[128,512]{1,0:T(8,128)(2,1)S(1)}, bf16[128,512]{1,0:T(8,128)(2,1)S(1)}, u32[]{:S(2)}, u32[]{:S(2)}) collective-permute-start(bf16[128,512]{1,0:T(8,128)(2,1)S(1)} %get-tuple-element.43.km), channel_id=1, source_target_pairs={{0,2},{1,3},{2,4},{3,5},{4,6},{5,7},{6,8},{7,9},{8,10},{9,11},{10,... | collective-permute-start | bytes 393224 | tf_op jit(solution)/shard_map/ppermute | solution.py:369
  4.7 9.4 %collective-permute-start.2 = (bf16[128,512]{1,0:T(8,128)(2,1)S(1)}, bf16[128,512]{1,0:T(8,128)(2,1)S(1)}, u32[]{:S(2)}, u32[]{:S(2)}) collective-permute-start(bf16[128,512]{1,0:T(8,128)(2,1)S(1)} %get-tuple-element.38), channel_id=1, source_target_pairs={{0,3},{1,2},{2,5},{3,4},{4,7},{5,6},{6,9},{7,8},{8,11},{9,10},{10,... | collective-permute-start | bytes 393224 | tf_op jit(solution)/shard_map/ppermute | solution.py:369
  5.8 11.1 %collective-permute-start.3 = (bf16[128,512]{1,0:T(8,128)(2,1)S(1)}, bf16[128,512]{1,0:T(8,128)(2,1)S(1)}, u32[]{:S(2)}, u32[]{:S(2)}) collective-permute-start(bf16[128,512]{1,0:T(8,128)(2,1)S(1)} %get-tuple-element.51), channel_id=1, source_target_pairs={{0,3},{1,2},{2,5},{3,4},{4,7},{5,6},{6,9},{7,8},{8,11},{9,10},{10,... | collective-permute-start | bytes 393224 | tf_op jit(solution)/shard_map/ppermute | solution.py:369
  7.9 13.2 %collective-permute-start.5 = (bf16[128,512]{1,0:T(8,128)(2,1)S(1)}, bf16[128,512]{1,0:T(8,128)(2,1)S(1)}, u32[]{:S(2)}, u32[]{:S(2)}) collective-permute-start(bf16[128,512]{1,0:T(8,128)(2,1)S(1)} %get-tuple-element.53.vm), channel_id=1, source_target_pairs={{0,2},{1,3},{2,4},{3,5},{4,6},{5,7},{6,8},{7,9},{8,10},{9,11},{10,... | collective-permute-start | bytes 393224 | tf_op jit(solution)/shard_map/ppermute | solution.py:369
  9.5 4.7 %collective-permute-start = (bf16[128,3072]{1,0:T(8,128)(2,1)S(1)}, bf16[128,3072]{1,0:T(8,128)(2,1)S(1)}, u32[]{:S(2)}, u32[]{:S(2)}) collective-permute-start(bf16[128,3072]{1,0:T(8,128)(2,1)S(1)} %get-tuple-element.44), channel_id=1, source_target_pairs={{0,1},{1,0},{2,3},{3,2},{4,5},{5,4},{6,7},{7,6},{8,9},{9,8},{10,11... | collective-permute-start | bytes 2359304 | tf_op jit(solution)/shard_map/ppermute | solution.py:369
  17.0 7.1 %collective-permute-start.4 = (bf16[128,512]{1,0:T(8,128)(2,1)S(1)}, bf16[128,512]{1,0:T(8,128)(2,1)S(1)}, u32[]{:S(2)}, u32[]{:S(2)}) collective-permute-start(bf16[128,512]{1,0:T(8,128)(2,1)S(1)} %get-tuple-element.54), channel_id=1, source_target_pairs={{3,0},{2,1},{5,2},{4,3},{7,4},{6,5},{9,6},{8,7},{11,8},{10,9},{13,... | collective-permute-start | bytes 393224 | tf_op jit(solution)/shard_map/ppermute | solution.py:369
  20.1 7.2 %collective-permute-start.7 = (bf16[128,512]{1,0:T(8,128)(2,1)S(1)}, bf16[128,512]{1,0:T(8,128)(2,1)S(1)}, u32[]{:S(2)}, u32[]{:S(2)}) collective-permute-start(bf16[128,512]{1,0:T(8,128)(2,1)S(1)} %get-tuple-element.59), channel_id=1, source_target_pairs={{2,0},{3,1},{4,2},{5,3},{6,4},{7,5},{8,6},{9,7},{10,8},{11,9},{12,... | collective-permute-start | bytes 393224 | tf_op jit(solution)/shard_map/ppermute | solution.py:369
  22.7 7.4 %collective-permute-start.8 = (bf16[128,512]{1,0:T(8,128)(2,1)S(1)}, bf16[128,512]{1,0:T(8,128)(2,1)S(1)}, u32[]{:S(2)}, u32[]{:S(2)}) collective-permute-start(bf16[128,512]{1,0:T(8,128)(2,1)S(1)} %get-tuple-element.69), channel_id=1, source_target_pairs={{2,0},{3,1},{4,2},{5,3},{6,4},{7,5},{8,6},{9,7},{10,8},{11,9},{12,... | collective-permute-start | bytes 393224 | tf_op jit(solution)/shard_map/ppermute | solution.py:369
  24.0 6.8 %collective-permute-start.9 = (bf16[128,512]{1,0:T(8,128)(2,1)S(1)}, bf16[128,512]{1,0:T(8,128)(2,1)S(1)}, u32[]{:S(2)}, u32[]{:S(2)}) collective-permute-start(bf16[128,512]{1,0:T(8,128)(2,1)S(1)} %get-tuple-element.70), channel_id=1, source_target_pairs={{3,0},{2,1},{5,2},{4,3},{7,4},{6,5},{9,6},{8,7},{11,8},{10,9},{13,... | collective-permute-start | bytes 393224 | tf_op jit(solution)/shard_map/ppermute | solution.py:369
  25.0 3.4 %collective-permute-start.6 = (bf16[128,3072]{1,0:T(8,128)(2,1)S(1)}, bf16[128,3072]{1,0:T(8,128)(2,1)S(1)}, u32[]{:S(2)}, u32[]{:S(2)}) collective-permute-start(bf16[128,3072]{1,0:T(8,128)(2,1)S(1)} %sent_grads.1), channel_id=1, source_target_pairs={{0,1},{1,0},{2,3},{3,2},{4,5},{5,4},{6,7},{7,6},{8,9},{9,8},{10,11... | collective-permute-start | bytes 2359304 | tf_op jit(solution)/shard_map/ppermute | solution.py:369

commit v8 on v7

--- a/solution.py
+++ b/solution.py
@@ -401,7 +401,7 @@
         near_kernel, "near_values", [shape((KEY_VALUE_HEADS, 2 * rows, GROUP * rows), jnp.float32)],
         index, later_rows, vm, near,
     )
-    dvo, v2o, near_dprob = lax.optimization_barrier((dvo, v2o, near_dprob))
+    dvm, dvo, v2o, near_dprob = lax.optimization_barrier((dvm, dvo, v2o, near_dprob))
     dv_back = moved(dvm, behind), moved(dvo, recross)
     dscore, dkm, dko = run(
         key_kernel, "key_grads", [pairs, narrow, narrow],

time: 32.2 us -> 32.2 us (level)
  no operation moved by 1% of the time
where the time goes in v8:
time: 32.2 us; the launch traced here: 31.6 us
  starting transfers between devices  14.4 us (45%)
  Pallas kernels  8.26 us (26%)
  waiting for transfers between devices  7.23 us (22%)
  local copies, waits for them, and re-layouts  0.96 us (3%)
  between operations  0.75 us (2%)
    ppermute x10, starting transfers between devices, moved(): return lax.ppermute(value, AXES, pairs)  14.4 us
    pallas_call x11, Pallas kernels, run(): pl.pallas_call(kernel, in_specs=[small] + [there if i in far else whole f...  8.26 us
    ppermute x10, waiting for transfers between devices, moved(): return lax.ppermute(value, AXES, pairs)  7.23 us
    unnamed x12, local copies, waits for them, and re-layouts  0.96 us
  transfers between devices with their start and end apart: 10, of which 7 were waited for; matrix products, arithmetic and copies ran while one was open for 0% of the time, Pallas kernels for 23%

profile of v8, /device:TPU:0, one launch (start us, length us, event | category | flops | bytes accessed | tf_op | source)
XLA Modules:
  0.0 31.6 jit_solution(10285586164149555184)
XLA Ops:
  0.6 0.9 %copy-done.2 = bf16[128,1024]{1,0:T(8,128)(2,1)S(1)} copy-done((bf16[128,1024]{1,0:T(8,128)(2,1)S(1)}, bf16[128,1024]{1,0:T(8,128)(2,1)}, u32[]{:S(2)}) %copy-start.2) | copy-done | bytes 262168
  1.7 3.0 %collective-permute-start.1 = (bf16[128,512]{1,0:T(8,128)(2,1)S(1)}, bf16[128,512]{1,0:T(8,128)(2,1)S(1)}, u32[]{:S(2)}, u32[]{:S(2)}) collective-permute-start(bf16[128,512]{1,0:T(8,128)(2,1)S(1)} %get-tuple-element.44.km), channel_id=1, source_target_pairs={{0,2},{1,3},{2,4},{3,5},{4,6},{5,7},{6,8},{7,9},{8,10},{9,11},{10,... | collective-permute-start | bytes 393224 | tf_op jit(solution)/shard_map/ppermute | solution.py:369
  4.7 0.7 %collective-permute-start.2 = (bf16[128,512]{1,0:T(8,128)(2,1)S(1)}, bf16[128,512]{1,0:T(8,128)(2,1)S(1)}, u32[]{:S(2)}, u32[]{:S(2)}) collective-permute-start(bf16[128,512]{1,0:T(8,128)(2,1)S(1)} %get-tuple-element.39), channel_id=1, source_target_pairs={{0,3},{1,2},{2,5},{3,4},{4,7},{5,6},{6,9},{7,8},{8,11},{9,10},{10,... | collective-permute-start | bytes 393224 | tf_op jit(solution)/shard_map/ppermute | solution.py:369
  5.4 0.4 %split_rows.1 = (bf16[128,1024]{1,0:T(8,128)(2,1)S(1)}, bf16[128,1024]{1,0:T(8,128)(2,1)S(1)}, bf16[128,512]{1,0:T(8,128)(2,1)S(1)}, bf16[128,512]{1,0:T(8,128)(...) custom-call(s32[1]{0:T(128)} %bitcast.rank_ref, s32[1,32]{1,0:T(1,128)S(1)} %bitcast.2, ...), custom_call_target="tpu_custom_call" | custom-call | bytes 1000 | tf_op jit(solution)/shard_map/split_rows/pallas_call | solution.py:344
  5.8 2.1 %collective-permute-start.3 = (bf16[128,512]{1,0:T(8,128)(2,1)S(1)}, bf16[128,512]{1,0:T(8,128)(2,1)S(1)}, u32[]{:S(2)}, u32[]{:S(2)}) collective-permute-start(bf16[128,512]{1,0:T(8,128)(2,1)S(1)} %get-tuple-element.53), channel_id=1, source_target_pairs={{0,3},{1,2},{2,5},{3,4},{4,7},{5,6},{6,9},{7,8},{8,11},{9,10},{10,... | collective-permute-start | bytes 393224 | tf_op jit(solution)/shard_map/ppermute | solution.py:369
  7.9 1.5 %collective-permute-start.5 = (bf16[128,512]{1,0:T(8,128)(2,1)S(1)}, bf16[128,512]{1,0:T(8,128)(2,1)S(1)}, u32[]{:S(2)}, u32[]{:S(2)}) collective-permute-start(bf16[128,512]{1,0:T(8,128)(2,1)S(1)} %get-tuple-element.55.vm), channel_id=1, source_target_pairs={{0,2},{1,3},{2,4},{3,5},{4,6},{5,7},{6,8},{7,9},{8,10},{9,11},{10,... | collective-permute-start | bytes 393224 | tf_op jit(solution)/shard_map/ppermute | solution.py:369
  9.5 3.5 %collective-permute-done.1.source.mine = bf16[128,512]{1,0:T(8,128)(2,1)S(1)} collective-permute-done((bf16[128,512]{1,0:T(8,128)(2,1)S(1)}, bf16[128,512]{1,0:T(8,128)(2,1)S(1)}, u32[]{:S(2)}, u32[]{:S(2)}) %collective-permute-start.1) | collective-permute-done | bytes 131104 | tf_op jit(solution)/shard_map/ppermute | solution.py:369
  13.0 1.1 %collective-permute-done.2.other = bf16[128,512]{1,0:T(8,128)(2,1)S(1)} collective-permute-done((bf16[128,512]{1,0:T(8,128)(2,1)S(1)}, bf16[128,512]{1,0:T(8,128)(2,1)S(1)}, u32[]{:S(2)}, u32[]{:S(2)}) %collective-permute-start.2) | collective-permute-done | bytes 131104 | tf_op jit(solution)/shard_map/ppermute | solution.py:369
  14.2 1.7 %value_grads.1 = (bf16[8,384,256]{2,1,0:T(8,128)(2,1)S(1)}, bf16[128,512]{1,0:T(8,128)(2,1)S(1)}, bf16[128,512]{1,0:T(8,128)(2,1)S(1)}) custom-call(s32[1]{0:T(128)} %bitcast.rank_ref, f32[2,384,128]{2,1,0:T(8,128)S(1)} %get-tuple-element.41.bias_ref, bf16[128,1024]{1,0:T(8,128)(2,1)S(1)} %get-tuple-element.42.qm, ...), custom_call_target="tpu_custom_call" | custom-call | bytes 1000 | tf_op jit(solution)/shard_map/value_grads/pallas_call | solution.py:344
  15.9 0.4 %near_values.1.near_dprob = f32[8,256,256]{2,1,0:T(8,128)S(1)} custom-call(s32[1]{0:T(128)} %bitcast.rank_ref, bf16[128,1024]{1,0:T(8,128)(2,1)S(1)} %get-tuple-element.54.gm, bf16[128,512]{1,0:T(8,128)(2,1)S(1)} %get-tuple-element.55.vm, bf16[128,3072]{1,0:T(8,128)(2,1)S(1)} %collective-permute-done.near), custom_call_target="tpu_custom_call" | custom-call | bytes 1000 | tf_op jit(solution)/shard_map/near_values/pallas_call | solution.py:344
  16.3 0.7 %collective-permute-done.3.v2o = bf16[128,512]{1,0:T(8,128)(2,1)S(1)} collective-permute-done((bf16[128,512]{1,0:T(8,128)(2,1)S(1)}, bf16[128,512]{1,0:T(8,128)(2,1)S(1)}, u32[]{:S(2)}, u32[]{:S(2)}) %collective-permute-start.3) | collective-permute-done | bytes 131104 | tf_op jit(solution)/shard_map/ppermute | solution.py:369
  17.0 3.1 %collective-permute-start.4 = (bf16[128,512]{1,0:T(8,128)(2,1)S(1)}, bf16[128,512]{1,0:T(8,128)(2,1)S(1)}, u32[]{:S(2)}, u32[]{:S(2)}) collective-permute-start(bf16[128,512]{1,0:T(8,128)(2,1)S(1)} %get-tuple-element.56), channel_id=1, source_target_pairs={{3,0},{2,1},{5,2},{4,3},{7,4},{6,5},{9,6},{8,7},{11,8},{10,9},{13,... | collective-permute-start | bytes 393224 | tf_op jit(solution)/shard_map/ppermute | solution.py:369
  20.1 1.0 %collective-permute-start.7 = (bf16[128,512]{1,0:T(8,128)(2,1)S(1)}, bf16[128,512]{1,0:T(8,128)(2,1)S(1)}, u32[]{:S(2)}, u32[]{:S(2)}) collective-permute-start(bf16[128,512]{1,0:T(8,128)(2,1)S(1)} %get-tuple-element.61), channel_id=1, source_target_pairs={{2,0},{3,1},{4,2},{5,3},{6,4},{7,5},{8,6},{9,7},{10,8},{11,9},{12,... | collective-permute-start | bytes 393224 | tf_op jit(solution)/shard_map/ppermute | solution.py:369
  21.1 1.6 %key_grads.1 = (bf16[8,384,256]{2,1,0:T(8,128)(2,1)S(1)}, bf16[128,512]{1,0:T(8,128)(2,1)S(1)}, bf16[128,512]{1,0:T(8,128)(2,1)S(1)}) custom-call(s32[1]{0:T(128)} %bitcast.rank_ref, f32[8,256,256]{2,1,0:T(8,128)S(1)} %near_values.1.near_dprob, bf16[8,384,256]{2,1,0:T(8,128)(2,1)S(1)} %get-tuple-element.57.prob_ref, ...), custom_call_target="tpu_custom_call" | custom-call | bytes 1000 | tf_op jit(solution)/shard_map/key_grads/pallas_call | solution.py:344
  22.7 1.3 %collective-permute-start.8 = (bf16[128,512]{1,0:T(8,128)(2,1)S(1)}, bf16[128,512]{1,0:T(8,128)(2,1)S(1)}, u32[]{:S(2)}, u32[]{:S(2)}) collective-permute-start(bf16[128,512]{1,0:T(8,128)(2,1)S(1)} %get-tuple-element.71), channel_id=1, source_target_pairs={{2,0},{3,1},{4,2},{5,3},{6,4},{7,5},{8,6},{9,7},{10,8},{11,9},{12,... | collective-permute-start | bytes 393224 | tf_op jit(solution)/shard_map/ppermute | solution.py:369
  24.1 0.9 %sent_grads.1 = bf16[128,3072]{1,0:T(8,128)(2,1)S(1)} custom-call(s32[1]{0:T(128)} %bitcast.rank_ref, bf16[8,384,256]{2,1,0:T(8,128)(2,1)S(1)} %get-tuple-element.57.prob_ref, bf16[8,384,256]{2,1,0:T(8,128)(2,1)S(1)} %get-tuple-element.60.dscore_ref, bf16[128,1024]{1,0:T(8,128)(2,1)S(1)} %get-tuple-element.42.qm, ...), custom_call_target="tpu_custom_call" | custom-call | bytes 1000 | tf_op jit(solution)/shard_map/sent_grads/pallas_call | solution.py:344
  25.0 1.5 %collective-permute-start.6 = (bf16[128,3072]{1,0:T(8,128)(2,1)S(1)}, bf16[128,3072]{1,0:T(8,128)(2,1)S(1)}, u32[]{:S(2)}, u32[]{:S(2)}) collective-permute-start(bf16[128,3072]{1,0:T(8,128)(2,1)S(1)} %sent_grads.1), channel_id=1, source_target_pairs={{0,1},{1,0},{2,3},{3,2},{4,5},{5,4},{6,7},{7,6},{8,9},{9,8},{10,11... | collective-permute-start | bytes 2359304 | tf_op jit(solution)/shard_map/ppermute | solution.py:369
  26.5 0.8 %collective-permute-done.7.backm = bf16[128,512]{1,0:T(8,128)(2,1)S(1)} collective-permute-done((bf16[128,512]{1,0:T(8,128)(2,1)S(1)}, bf16[128,512]{1,0:T(8,128)(2,1)S(1)}, u32[]{:S(2)}, u32[]{:S(2)}) %collective-permute-start.7) | collective-permute-done | bytes 131104 | tf_op jit(solution)/shard_map/ppermute | solution.py:369
  27.3 0.9 %own_grads.1 = (bf16[128,1024]{1,0:T(8,128)(2,1)S(1)}, f32[128,1024]{1,0:T(8,128)S(1)}, f32[128,512]{1,0:T(8,128)S(1)}, f32[128,512]{1,0:T(8,128)S(1)}) custom-call(s32[1]{0:T(128)} %bitcast.rank_ref, bf16[8,384,256]{2,1,0:T(8,128)(2,1)S(1)} %get-tuple-element.57.prob_ref, bf16[8,384,256]{2,1,0:T(8,128)(2,1)S(1)} %get-tuple-element.60.dscore_ref, ...), custom_call_target="tpu_custom_call" | custom-call | flops 20000000000 | bytes 1000 | tf_op jit(solution)/shard_map/own_grads/pallas_call | solution.py:344
  28.2 0.2 collective-permute-done.6.got.near
  28.4 1.5 %join_rows.1 = (bf16[128,2048]{1,0:T(8,128)(2,1)}, f32[128,2048]{1,0:T(8,128)}, f32[128,1024]{1,0:T(8,128)}) custom-call(s32[1]{0:T(128)} %bitcast.rank_ref, bf16[128,3072]{1,0:T(8,128)(2,1)S(1)} %collective-permute-done.6.got.near, bf16[128,1024]{1,0:T(8,128)(2,1)S(1)} %get-tuple-element.64.outm, f32[128,1024]{1,0:T(8,128)S(1)} %get-tuple-element.65.dqm, ...), custom_call_target="tpu_custom_call" | custom-call | bytes 1000 | tf_op jit(solution)/shard_map/join_rows/pallas_call | solution.py:344
  29.9 0.2 collective-permute-done.8.backm
  30.1 0.7 %collective-permute-done.9.backo = bf16[128,512]{1,0:T(8,128)(2,1)S(1)} collective-permute-done((bf16[128,512]{1,0:T(8,128)(2,1)S(1)}, bf16[128,512]{1,0:T(8,128)(2,1)S(1)}, u32[]{:S(2)}, u32[]{:S(2)}) %collective-permute-start.9) | collective-permute-done | bytes 131104 | tf_op jit(solution)/shard_map/ppermute | solution.py:369
  30.8 0.8 %join_keys.1 = f32[128,1024]{1,0:T(8,128)} custom-call(s32[1]{0:T(128)} %bitcast.rank_ref, f32[128,512]{1,0:T(8,128)S(1)} %get-tuple-element.70.mine, bf16[128,3072]{1,0:T(8,128)(2,1)S(1)} %collective-permute-done.6.got.near, bf16[128,512]{1,0:T(8,128)(2,1)S(1)} %collective-permute-done.8.backm, bf16[128,512]{1,0:T(8,128)(2,1)S(1)} %collective-permute-done.9.backo), custom_call_target="tpu_custom_call" | custom-call | bytes 1000 | tf_op jit(solution)/shard_map/join_keys/pallas_call | solution.py:344
  (19 shorter events, 0.2 us)
Async XLA Ops:
  0.6 1.0 %copy-start.2 = (bf16[128,1024]{1,0:T(8,128)(2,1)S(1)}, bf16[128,1024]{1,0:T(8,128)(2,1)}, u32[]{:S(2)}) copy-start(bf16[128,1024]{1,0:T(8,128)(2,1)} %k_ref.1) | copy-start | bytes 786436
  1.6 3.8 %copy-start = (bf16[128,2048]{1,0:T(8,128)(2,1)S(1)}, bf16[128,2048]{1,0:T(8,128)(2,1)}, u32[]{:S(2)}) copy-start(bf16[128,2048]{1,0:T(8,128)(2,1)} %q_ref) | copy-start | bytes 1572868
  1.6 3.8 %copy-start.1 = (bf16[128,2048]{1,0:T(8,128)(2,1)S(1)}, bf16[128,2048]{1,0:T(8,128)(2,1)}, u32[]{:S(2)}) copy-start(bf16[128,2048]{1,0:T(8,128)(2,1)} %g_ref.1) | copy-start | bytes 1572868
  1.6 3.8 %copy-start.3 = (bf16[128,1024]{1,0:T(8,128)(2,1)S(1)}, bf16[128,1024]{1,0:T(8,128)(2,1)}, u32[]{:S(2)}) copy-start(bf16[128,1024]{1,0:T(8,128)(2,1)} %k_ref.1) | copy-start | bytes 786436
  1.6 3.8 %copy-start.4 = (bf16[128,1024]{1,0:T(8,128)(2,1)S(1)}, bf16[128,1024]{1,0:T(8,128)(2,1)}, u32[]{:S(2)}) copy-start(bf16[128,1024]{1,0:T(8,128)(2,1)} %v_ref.1) | copy-start | bytes 786436
  1.6 3.8 %copy-start.5 = (s32[32]{0:T(128)S(1)}, s32[32]{0:T(128)}, u32[]{:S(2)}) copy-start(s32[32]{0:T(128)} %param.9) | copy-start | bytes 388
  1.7 11.3 %collective-permute-start.1 = (bf16[128,512]{1,0:T(8,128)(2,1)S(1)}, bf16[128,512]{1,0:T(8,128)(2,1)S(1)}, u32[]{:S(2)}, u32[]{:S(2)}) collective-permute-start(bf16[128,512]{1,0:T(8,128)(2,1)S(1)} %get-tuple-element.44.km), channel_id=1, source_target_pairs={{0,2},{1,3},{2,4},{3,5},{4,6},{5,7},{6,8},{7,9},{8,10},{9,11},{10,... | collective-permute-start | bytes 393224 | tf_op jit(solution)/shard_map/ppermute | solution.py:369
  4.7 9.4 %collective-permute-start.2 = (bf16[128,512]{1,0:T(8,128)(2,1)S(1)}, bf16[128,512]{1,0:T(8,128)(2,1)S(1)}, u32[]{:S(2)}, u32[]{:S(2)}) collective-permute-start(bf16[128,512]{1,0:T(8,128)(2,1)S(1)} %get-tuple-element.39), channel_id=1, source_target_pairs={{0,3},{1,2},{2,5},{3,4},{4,7},{5,6},{6,9},{7,8},{8,11},{9,10},{10,... | collective-permute-start | bytes 393224 | tf_op jit(solution)/shard_map/ppermute | solution.py:369
  5.8 11.1 %collective-permute-start.3 = (bf16[128,512]{1,0:T(8,128)(2,1)S(1)}, bf16[128,512]{1,0:T(8,128)(2,1)S(1)}, u32[]{:S(2)}, u32[]{:S(2)}) collective-permute-start(bf16[128,512]{1,0:T(8,128)(2,1)S(1)} %get-tuple-element.53), channel_id=1, source_target_pairs={{0,3},{1,2},{2,5},{3,4},{4,7},{5,6},{6,9},{7,8},{8,11},{9,10},{10,... | collective-permute-start | bytes 393224 | tf_op jit(solution)/shard_map/ppermute | solution.py:369
  7.9 13.2 %collective-permute-start.5 = (bf16[128,512]{1,0:T(8,128)(2,1)S(1)}, bf16[128,512]{1,0:T(8,128)(2,1)S(1)}, u32[]{:S(2)}, u32[]{:S(2)}) collective-permute-start(bf16[128,512]{1,0:T(8,128)(2,1)S(1)} %get-tuple-element.55.vm), channel_id=1, source_target_pairs={{0,2},{1,3},{2,4},{3,5},{4,6},{5,7},{6,8},{7,9},{8,10},{9,11},{10,... | collective-permute-start | bytes 393224 | tf_op jit(solution)/shard_map/ppermute | solution.py:369
  9.5 4.7 %collective-permute-start = (bf16[128,3072]{1,0:T(8,128)(2,1)S(1)}, bf16[128,3072]{1,0:T(8,128)(2,1)S(1)}, u32[]{:S(2)}, u32[]{:S(2)}) collective-permute-start(bf16[128,3072]{1,0:T(8,128)(2,1)S(1)} %get-tuple-element.45), channel_id=1, source_target_pairs={{0,1},{1,0},{2,3},{3,2},{4,5},{5,4},{6,7},{7,6},{8,9},{9,8},{10,11... | collective-permute-start | bytes 2359304 | tf_op jit(solution)/shard_map/ppermute | solution.py:369
  17.0 7.1 %collective-permute-start.4 = (bf16[128,512]{1,0:T(8,128)(2,1)S(1)}, bf16[128,512]{1,0:T(8,128)(2,1)S(1)}, u32[]{:S(2)}, u32[]{:S(2)}) collective-permute-start(bf16[128,512]{1,0:T(8,128)(2,1)S(1)} %get-tuple-element.56), channel_id=1, source_target_pairs={{3,0},{2,1},{5,2},{4,3},{7,4},{6,5},{9,6},{8,7},{11,8},{10,9},{13,... | collective-permute-start | bytes 393224 | tf_op jit(solution)/shard_map/ppermute | solution.py:369
  20.1 7.2 %collective-permute-start.7 = (bf16[128,512]{1,0:T(8,128)(2,1)S(1)}, bf16[128,512]{1,0:T(8,128)(2,1)S(1)}, u32[]{:S(2)}, u32[]{:S(2)}) collective-permute-start(bf16[128,512]{1,0:T(8,128)(2,1)S(1)} %get-tuple-element.61), channel_id=1, source_target_pairs={{2,0},{3,1},{4,2},{5,3},{6,4},{7,5},{8,6},{9,7},{10,8},{11,9},{12,... | collective-permute-start | bytes 393224 | tf_op jit(solution)/shard_map/ppermute | solution.py:369
  22.7 7.4 %collective-permute-start.8 = (bf16[128,512]{1,0:T(8,128)(2,1)S(1)}, bf16[128,512]{1,0:T(8,128)(2,1)S(1)}, u32[]{:S(2)}, u32[]{:S(2)}) collective-permute-start(bf16[128,512]{1,0:T(8,128)(2,1)S(1)} %get-tuple-element.71), channel_id=1, source_target_pairs={{2,0},{3,1},{4,2},{5,3},{6,4},{7,5},{8,6},{9,7},{10,8},{11,9},{12,... | collective-permute-start | bytes 393224 | tf_op jit(solution)/shard_map/ppermute | solution.py:369
  24.0 6.8 %collective-permute-start.9 = (bf16[128,512]{1,0:T(8,128)(2,1)S(1)}, bf16[128,512]{1,0:T(8,128)(2,1)S(1)}, u32[]{:S(2)}, u32[]{:S(2)}) collective-permute-start(bf16[128,512]{1,0:T(8,128)(2,1)S(1)} %get-tuple-element.72), channel_id=1, source_target_pairs={{3,0},{2,1},{5,2},{4,3},{7,4},{6,5},{9,6},{8,7},{11,8},{10,9},{13,... | collective-permute-start | bytes 393224 | tf_op jit(solution)/shard_map/ppermute | solution.py:369
  25.0 3.4 %collective-permute-start.6 = (bf16[128,3072]{1,0:T(8,128)(2,1)S(1)}, bf16[128,3072]{1,0:T(8,128)(2,1)S(1)}, u32[]{:S(2)}, u32[]{:S(2)}) collective-permute-start(bf16[128,3072]{1,0:T(8,128)(2,1)S(1)} %sent_grads.1), channel_id=1, source_target_pairs={{0,1},{1,0},{2,3},{3,2},{4,5},{5,4},{6,7},{7,6},{8,9},{9,8},{10,11... | collective-permute-start | bytes 2359304 | tf_op jit(solution)/shard_map/ppermute | solution.py:369
